TPU v7x, 128 devices: a whole 4x4x4 slice. The times are simulated.
128 devices in a mesh: dp: 8 (over x, core), mp: 16 (over z, y).
Axes of the slice: x: 4, y: 4, z: 4, core: 2. Of those that a mesh axis runs over, the one named last changes fastest.
Arguments:
- tokens: bfloat16 [16384, 2048], P(('dp', 'mp')), may hold values from -6 to 6
- doc_start: int32 [16384], P('dp'), may hold values from 0 to 1, as said below
- gain_first: float32 [2048], replicated, may hold values from 0.5 to 1.5
- w_query: bfloat16 [2048, 256], P(None, 'mp'), may hold values from -0.125 to 0.125
- w_key: bfloat16 [2048, 256], P(None, 'mp'), may hold values from -0.125 to 0.125
- w_value: bfloat16 [2048, 2048], P(None, 'mp'), may hold values from -0.125 to 0.125
- w_out: bfloat16 [2048, 2048], P('mp'), may hold values from -0.5 to 0.5
- gain_second: float32 [2048], replicated, may hold values from 0.5 to 1.5
- w_gate: bfloat16 [2048, 5632], P(None, 'mp'), may hold values from -0.125 to 0.125
- w_up: bfloat16 [2048, 5632], P(None, 'mp'), may hold values from -0.125 to 0.125
- w_down: bfloat16 [5632, 2048], P('mp'), may hold values from -0.078125 to 0.078125
- out_grad: bfloat16 [16384, 2048], P(('dp', 'mp')), may hold values from -6 to 6
Outputs:
- block_out: float32 [16384, 2048], P(('dp', 'mp'))
- input_grad: float32 [16384, 2048], P(('dp', 'mp'))
- grad_gain_first: float32 [2048], replicated
- grad_query: float32 [2048, 256], P(None, 'mp')
- grad_key: float32 [2048, 256], P(None, 'mp')
- grad_value: float32 [2048, 2048], P(None, 'mp')
- grad_out: float32 [2048, 2048], P('mp')
- grad_gain_second: float32 [2048], replicated
- grad_gate: float32 [2048, 5632], P(None, 'mp')
- grad_up: float32 [2048, 5632], P(None, 'mp')
- grad_down: float32 [5632, 2048], P('mp')
Inputs may be any that keep to these rules, and one draw needn't show every extreme that they name: `doc_start`: 1 marks the first token of a document and 0 the others; the first token of every row of 2048 tokens is marked.
All inputs are finite; a program needn't handle non-finite values.
Results may differ from a plain program's by a relative error of at most 0.025.
Values may be sent and summed in bfloat16 or wider, within the bound.
No kernel may reach another device: no remote copies, remote signals or barrier semaphores. Data moves between devices by JAX's collectives and lax.ppermute only.
A program may use at most 192 MiB of HBM per device.

v0:
```python
import jax
import jax.numpy as jnp
from jax import lax
from jax.sharding import PartitionSpec as P

FEAT = 16
HEAD_V = 128


EPS = 1e-05
F32 = jnp.float32
BF16 = jnp.bfloat16


def rows_product(left, right):
    return jnp.dot(left, right, preferred_element_type=F32)


def over_rows(left, right):
    return jnp.einsum("ta,tb->ab", left, right, preferred_element_type=F32)


def against(left, right):
    return jnp.einsum("ta,ba->tb", left, right, preferred_element_type=F32)


def rows_of(array, start, count):
    return lax.dynamic_slice_in_dim(array, start, count, 0)


def norm_back(grad_normed, unit, inverse, gains):
    scaled = grad_normed * gains
    return inverse * (scaled - unit * jnp.mean(scaled * unit, axis=1, keepdims=True))


def body(
    tokens,
    doc_start,
    gain_first,
    w_query,
    w_key,
    w_value,
    w_out,
    gain_second,
    w_gate,
    w_up,
    w_down,
    out_grad,
):
    rows = tokens.shape[0]
    length = doc_start.shape[0]
    heads_dev = w_query.shape[1] // FEAT
    scaling = FEAT ** (-0.5)
    block = min(512, length)
    starts = jnp.arange(length // block, dtype=jnp.int32) * block
    doc_ids = jnp.cumsum(doc_start, dtype=jnp.int32)
    positions = jnp.arange(length, dtype=jnp.int32)
    x_rows = tokens.astype(F32)
    first_inv = lax.rsqrt(jnp.mean(x_rows * x_rows, axis=1, keepdims=True) + EPS)
    first_unit = x_rows * first_inv
    first_normed = (first_unit * gain_first).astype(BF16)
    seq_first = lax.all_gather(first_normed, "mp", axis=0, tiled=True)
    queries = rows_product(seq_first, w_query).astype(BF16).reshape(length, heads_dev, FEAT)
    key_rows = rows_product(seq_first, w_key).astype(BF16).reshape(length, heads_dev, FEAT)
    value_rows = rows_product(seq_first, w_value).astype(BF16).reshape(length, heads_dev, HEAD_V)

    def block_scores(start, query_block):
        doc_block = lax.dynamic_slice_in_dim(doc_ids, start, block, 0)
        row_index = start + jnp.arange(block, dtype=jnp.int32)
        allowed = (positions[None, :] <= row_index[:, None]) & (
            doc_ids[None, :] == doc_block[:, None]
        )
        scores = (
            jnp.einsum("thf,shf->hts", query_block, key_rows, preferred_element_type=F32) * scaling
        )
        weight = jnp.where(allowed[None], 1.0 + scores + 0.5 * scores * scores, 0.0)
        return (allowed, scores, weight)

    def forward_block(start):
        query_block = rows_of(queries, start, block)
        allowed, scores, weight = block_scores(start, query_block)
        numerator = jnp.einsum(
            "hts,shc->thc", weight.astype(BF16), value_rows, preferred_element_type=F32
        )
        return (numerator, jnp.transpose(jnp.sum(weight, axis=2)))

    numerator, denominator = lax.map(forward_block, starts)
    numerator = numerator.reshape(length, heads_dev, HEAD_V)
    denominator = denominator.reshape(length, heads_dev)
    mixed_out = (
        (numerator / denominator[:, :, None]).astype(BF16).reshape(length, heads_dev * HEAD_V)
    )
    first_branch = lax.psum_scatter(
        rows_product(rows_of(mixed_out, jnp.int32(0), rows * lax.axis_size("mp")), w_out).astype(
            jnp.bfloat16
        ),
        "mp",
        scatter_dimension=0,
        tiled=True,
    ).astype(jnp.float32)
    mid_rows = x_rows + first_branch
    second_inv = lax.rsqrt(jnp.mean(mid_rows * mid_rows, axis=1, keepdims=True) + EPS)
    second_unit = mid_rows * second_inv
    second_normed = (second_unit * gain_second).astype(BF16)
    seq_second = lax.all_gather(second_normed, "mp", axis=0, tiled=True)
    gate_rows = rows_product(seq_second, w_gate)
    up_rows = rows_product(seq_second, w_up)
    sigmoid_gate = jax.nn.sigmoid(gate_rows)
    silu_gate = gate_rows * sigmoid_gate
    hidden = (silu_gate * up_rows).astype(BF16)
    block_out = mid_rows + lax.psum_scatter(
        rows_product(rows_of(hidden, jnp.int32(0), rows * lax.axis_size("mp")), w_down).astype(
            jnp.bfloat16
        ),
        "mp",
        scatter_dimension=0,
        tiled=True,
    ).astype(jnp.float32)
    cot_rows = lax.all_gather(out_grad, "mp", axis=0, tiled=True)
    grad_down = over_rows(hidden, cot_rows)
    grad_hidden = against(cot_rows, w_down)
    up_delta = (grad_hidden * silu_gate).astype(BF16)
    gate_delta = (
        grad_hidden * up_rows * sigmoid_gate * (1.0 + gate_rows * (1.0 - sigmoid_gate))
    ).astype(BF16)
    grad_gate = over_rows(seq_second, gate_delta)
    grad_up = over_rows(seq_second, up_delta)
    start = jnp.int32(0)
    grad_second = lax.psum_scatter(
        (
            against(rows_of(gate_delta, start, rows * lax.axis_size("mp")), w_gate)
            + against(rows_of(up_delta, start, rows * lax.axis_size("mp")), w_up)
        ).astype(jnp.bfloat16),
        "mp",
        scatter_dimension=0,
        tiled=True,
    ).astype(jnp.float32)
    gain_second_part = jnp.sum(grad_second * second_unit, axis=0)
    grad_mid = out_grad.astype(F32) + norm_back(grad_second, second_unit, second_inv, gain_second)
    grad_branch = grad_mid.astype(BF16)
    grad_rows = lax.all_gather(grad_branch, "mp", axis=0, tiled=True)
    grad_out = over_rows(mixed_out, grad_rows)
    grad_mixed = against(grad_rows, w_out)
    grad_mixed = grad_mixed.reshape(length, heads_dev, HEAD_V)
    grad_numer = (grad_mixed / denominator[:, :, None]).astype(BF16)
    grad_denom = -jnp.sum(grad_mixed * numerator, axis=2) / (denominator * denominator)

    def backward_block(carried, start):
        key_sum, value_sum = carried
        query_block = rows_of(queries, start, block)
        allowed, scores, weight = block_scores(start, query_block)
        numer_block = rows_of(grad_numer, start, block)
        denom_block = rows_of(grad_denom, start, block)
        grad_weight = (
            jnp.einsum("thc,shc->hts", numer_block, value_rows, preferred_element_type=F32)
            + jnp.transpose(denom_block)[:, :, None]
        )
        grad_scores = jnp.where(allowed[None], grad_weight * (1.0 + scores), 0.0).astype(BF16)
        query_grad = (
            jnp.einsum("hts,shf->thf", grad_scores, key_rows, preferred_element_type=F32) * scaling
        ).astype(BF16)
        key_sum = (
            key_sum
            + jnp.einsum("hts,thf->shf", grad_scores, query_block, preferred_element_type=F32)
            * scaling
        )
        value_sum = value_sum + jnp.einsum(
            "hts,thc->shc", weight.astype(BF16), numer_block, preferred_element_type=F32
        )
        return ((key_sum, value_sum), query_grad)

    zero_keys = jnp.zeros((length, heads_dev, FEAT), F32)
    zero_values = jnp.zeros((length, heads_dev, HEAD_V), F32)
    (key_sum, value_sum), query_grads = lax.scan(backward_block, (zero_keys, zero_values), starts)
    grad_queries = query_grads.reshape(length, heads_dev * FEAT)
    grad_keys = key_sum.astype(BF16).reshape(length, heads_dev * FEAT)
    grad_values = value_sum.astype(BF16).reshape(length, heads_dev * HEAD_V)
    grad_query = over_rows(seq_first, grad_queries)
    grad_key = over_rows(seq_first, grad_keys)
    grad_value = over_rows(seq_first, grad_values)
    start = jnp.int32(0)
    total = against(rows_of(grad_queries, start, rows * lax.axis_size("mp")), w_query)
    total = total + against(rows_of(grad_keys, start, rows * lax.axis_size("mp")), w_key)
    grad_first = lax.psum_scatter(
        (total + against(rows_of(grad_values, start, rows * lax.axis_size("mp")), w_value)).astype(
            jnp.bfloat16
        ),
        "mp",
        scatter_dimension=0,
        tiled=True,
    ).astype(jnp.float32)
    gain_first_part = jnp.sum(grad_first * first_unit, axis=0)
    input_grad = grad_mid + norm_back(grad_first, first_unit, first_inv, gain_first)
    summed = (
        lax.psum(grad_query.astype(jnp.bfloat16), "dp").astype(jnp.float32),
        lax.psum(grad_key.astype(jnp.bfloat16), "dp").astype(jnp.float32),
        lax.psum(grad_value.astype(jnp.bfloat16), "dp").astype(jnp.float32),
        lax.psum(grad_out.astype(jnp.bfloat16), "dp").astype(jnp.float32),
        lax.psum(grad_gate.astype(jnp.bfloat16), "dp").astype(jnp.float32),
        lax.psum(grad_up.astype(jnp.bfloat16), "dp").astype(jnp.float32),
        lax.psum(grad_down.astype(jnp.bfloat16), "dp").astype(jnp.float32),
    )
    gain_totals = lax.psum((gain_first_part, gain_second_part), ("dp", "mp"))
    return (
        block_out,
        input_grad,
        gain_totals[0],
        summed[0],
        summed[1],
        summed[2],
        summed[3],
        gain_totals[1],
        summed[4],
        summed[5],
        summed[6],
    )


def solution(mesh):
    return jax.shard_map(
        body,
        mesh=mesh,
        in_specs=(
            P(("dp", "mp"), None),
            P("dp"),
            P(),
            P(None, "mp"),
            P(None, "mp"),
            P(None, "mp"),
            P("mp", None),
            P(),
            P(None, "mp"),
            P(None, "mp"),
            P("mp", None),
            P(("dp", "mp"), None),
        ),
        out_specs=(
            P(("dp", "mp"), None),
            P(("dp", "mp"), None),
            P(),
            P(None, "mp"),
            P(None, "mp"),
            P(None, "mp"),
            P("mp", None),
            P(),
            P(None, "mp"),
            P(None, "mp"),
            P("mp", None),
        ),
        check_vma=False,
    )
```

profile of v0, /device:TPU:0, one launch (start us, length us, event | category | flops | bytes accessed | tf_op | source)
XLA Modules:
  0.0 882.1 jit_solution(2938881371729584707)
XLA Ops:
  12.5 72.1 %all-gather.5.cloned.1.call-done = bf16[2048,2048]{1,0:T(8,128)(2,1)} async-done(((bf16[128,2048]{1,0:T(8,128)(2,1)}), bf16[2048,2048]{1,0:T(8,128)(2,1)}) %all-gather.5.cloned.1.call-update) | async-done | bytes 8388624 | tf_op jit(solution)/shard_map/all_gather | solution.py:62
  84.7 5.8 fusion.48
  95.2 25.1 %while.32 = (s32[]{:T(128)}, f32[4,512,1,128]{3,1,2,0:T(8,128)S(1)}, f32[4,512,1]{1,2,0:T(1,128)S(1)}, s32[4]{0:T(128)S(1)}, s32[2048]{0:T(1024)S(1)}, /*index=5...) while((s32[]{:T(128)}, ...), condition=%wide.region_5.6_spmd.clone, body=%wide.region_3.5_spmd.clone.sunk | while | flops 313524224 | bytes 5087415 | solution.py:87
  122.8 7.1 convolution_convert_fusion.1
  130.0 84.9 %reduce-scatter.5.cloned.1.call-done = bf16[128,2048]{1,0:T(8,128)(2,1)} async-done(((bf16[2048,2048]{1,0:T(8,128)(2,1)}), bf16[128,2048]{1,0:T(8,128)(2,1)}) %reduce-scatter.5.cloned.1.call-update) | async-done | bytes 524304 | tf_op jit(solution)/shard_map/reduce_scatter | solution.py:93
  219.4 69.2 %all-gather.7.cloned.1.call-done = bf16[2048,2048]{1,0:T(8,128)(2,1)} async-done(((bf16[128,2048]{1,0:T(8,128)(2,1)}), bf16[2048,2048]{1,0:T(8,128)(2,1)}) %all-gather.7.cloned.1.call-update) | async-done | bytes 8388624 | tf_op jit(solution)/shard_map/all_gather | solution.py:105
  288.5 8.6 fusion.80
  297.2 4.8 fusion.79
  302.0 59.0 %all-gather.9.cloned.1.call-done = bf16[2048,2048]{1,0:T(8,128)(2,1)} async-done(((bf16[128,2048]{1,0:T(8,128)(2,1)}), bf16[2048,2048]{1,0:T(8,128)(2,1)}) %all-gather.9.cloned.1.call-update) | async-done | bytes 8388624 | tf_op jit(solution)/shard_map/all_gather | solution.py:119
  361.0 11.7 %multiply_convert_fusion = (bf16[2048,352]{0,1:T(8,128)(2,1)S(1)}, bf16[2048,352]{0,1:T(8,128)(2,1)S(1)}, bf16[2048,352]{0,1:T(8,128)(2,1)}) fusion(f32[2048,352]{0,1:T(8,128)} %fusion.79, f32[2048,352]{0,1:T(8,128)} %fusion.80, bf16[2048,2048]{1,0:T(8,128)(2,1)} %all-gather.9.cloned.1.call-done, bf16[352,2048]{1,0:T(8,128)(2,1)S(1)} %copy-done), kind=kOutput, calls=%fused_computation.55 | convolution fusion | flops 2963603456 | bytes 19922944 | tf_op jit(solution)/shard_map/ta,ba->tb/dot_general | solution.py:24
  372.8 8.3 fusion.81
  381.1 10.2 %add_convert_fusion.1 = bf16[2048,2048]{1,0:T(8,128)(2,1)} fusion(f32[2048,2048]{1,0:T(8,128)} %fusion.81, bf16[2048,352]{0,1:T(8,128)(2,1)S(1)} %get-tuple-element.420, bf16[2048,352]{0,1:T(8,128)(2,1)S(1)} %copy-done.13), kind=kOutput, calls=%fused_computation.52 | convolution fusion | flops 2961178624 | bytes 28049408 | tf_op jit(solution)/shard_map/ta,ba->tb/dot_general | solution.py:24
  391.4 84.5 %reduce-scatter.9.cloned.1.call-done = bf16[128,2048]{1,0:T(8,128)(2,1)} async-done(((bf16[2048,2048]{1,0:T(8,128)(2,1)}), bf16[128,2048]{1,0:T(8,128)(2,1)}) %reduce-scatter.9.cloned.1.call-update) | async-done | bytes 524304 | tf_op jit(solution)/shard_map/reduce_scatter | solution.py:129
  480.6 8.2 convolution_convert_fusion.2
  488.9 8.3 convolution_convert_fusion.3
  497.2 4.2 convolution_convert_fusion.4
  501.4 49.6 %all-gather.11.cloned.1.call-done = bf16[2048,2048]{1,0:T(8,128)(2,1)} async-done(((bf16[128,2048]{1,0:T(8,128)(2,1)}), bf16[2048,2048]{1,0:T(8,128)(2,1)}) %all-gather.11.cloned.1.call-update) | async-done | bytes 8388624 | tf_op jit(solution)/shard_map/all_gather | solution.py:141
  550.9 7.5 multiply_reduce_fusion
  558.4 37.5 %while.33 = (s32[]{:T(128)}, f32[2048,1,16]{0,2,1:T(8,128)S(1)}, f32[2048,1,128]{0,2,1:T(8,128)}, bf16[4,512,1,16]{1,3,2,0:T(8,128)(2,1)S(1)}, s32[4]{0:T(128)S(...) while((s32[]{:T(128)}, f32[2048,1,16]{0,2,1:T(8,128)S(1)}, ...), condition=%wide.region_13.14_spmd.clone, body=%wide.region_12.13_spmd.clone.sunk | while | flops 658096640 | bytes 32723256 | solution.py:174
  596.0 5.8 convolution_convert_fusion.5
  601.8 5.4 convolution_convert_fusion.9
  607.1 5.4 convolution_convert_fusion.8
  612.5 3.3 convolution_convert_fusion.6
  616.6 8.4 fusion.82
  625.1 8.2 fusion.73
  633.3 16.3 %add_convert_fusion = bf16[2048,2048]{1,0:T(8,128)(2,1)} fusion(f32[2048,2048]{1,0:T(8,128)} %fusion.82, f32[2048,2048]{1,0:T(8,128)} %fusion.73, bf16[2048,128]{1,0:T(8,128)(2,1)S(1)} %copy-done.21, f32[2048,1,128]{0,2,1:T(8,128)} %get-tuple-element.280), kind=kOutput, calls=%fused_computation.51 | convolution fusion | flops 1086586880 | bytes 43515904 | tf_op jit(solution)/shard_map/ta,ba->tb/dot_general | solution.py:24
  649.7 8.5 convolution_convert_fusion
  658.2 36.9 %all-reduce.4.cloned.1.call-done = (bf16[2048,16]{0,1:T(8,128)(2,1)}, bf16[2048,16]{0,1:T(8,128)(2,1)}, bf16[2048,128]{1,0:T(8,128)(2,1)}, bf16[128,2048]{1,0:T(...) async-done(((bf16[2048,16]{0,1:T(8,128)(2,1)}, bf16[2048,16]{0,1:T(8,128)(2,1)}, bf16[2048,128]{1,0:T(8,128)(2,1)}, ...) | async-done | bytes 5505040 | tf_op jit(solution)/shard_map/psum | solution.py:195
  708.3 75.5 %reduce-scatter.11.cloned.1.call-done = bf16[128,2048]{1,0:T(8,128)(2,1)} async-done(((bf16[2048,2048]{1,0:T(8,128)(2,1)}), bf16[128,2048]{1,0:T(8,128)(2,1)}) %reduce-scatter.11.cloned.1.call-update) | async-done | bytes 524304 | tf_op jit(solution)/shard_map/reduce_scatter | solution.py:184
  785.8 65.8 %all-reduce = (f32[2048]{0:T(1024)}, f32[2048]{0:T(1024)}) all-reduce(f32[2048]{0:T(1024)} %get-tuple-element.369, f32[2048]{0:T(1024)} %get-tuple-element.367), channel_id=1, replica_groups=mesh['dp'=8,'mp'=16] {'dp','mp'}, use_global_device_ids=true, to_apply=%region_17.18 | all-reduce | flops 4096 | bytes 32768 | tf_op jit(solution)/shard_map/psum | solution.py:203
  852.8 18.9 %reduce-scatter.7.cloned.1.call-done = bf16[128,2048]{1,0:T(8,128)(2,1)} async-done(((bf16[2048,2048]{1,0:T(8,128)(2,1)}), bf16[128,2048]{1,0:T(8,128)(2,1)}) %reduce-scatter.7.cloned.1.call-update) | async-done | bytes 524304 | tf_op jit(solution)/shard_map/reduce_scatter | solution.py:111
  871.8 3.4 fusion.57
  (209 shorter events, 85.5 us)
Async XLA Ops:
  7.2 353.8 %copy-start = (bf16[352,2048]{1,0:T(8,128)(2,1)S(1)}, bf16[352,2048]{1,0:T(8,128)(2,1)}, u32[]{:S(2)}) copy-start(bf16[352,2048]{1,0:T(8,128)(2,1)} %param.26) | copy-start | bytes 4325380
  7.2 77.5 %all-gather.5.cloned.1.call-start = ((), (), s32[]{:S(2)}) async-start(), calls=%async_computation.4 | async-start | bytes 8912896 | tf_op jit(solution)/shard_map/all_gather | solution.py:62
  11.2 203.7 %reduce-scatter.5.cloned.1.call-start = ((), (), s32[]{:S(2)}) async-start(), calls=%async_computation.5 | async-start | bytes 8912896 | tf_op jit(solution)/shard_map/reduce_scatter | solution.py:93
  12.5 77.9 %copy-start.22 = (bf16[2048,16]{0,1:T(8,128)(2,1)S(1)}, bf16[2048,16]{0,1:T(8,128)(2,1)}, u32[]{:S(2)}) copy-start(bf16[2048,16]{0,1:T(8,128)(2,1)} %param.19) | copy-start | bytes 196612
  129.9 85.0 %copy-start.2 = (bf16[128,2048]{1,0:T(8,128)(2,1)S(1)}, bf16[128,2048]{1,0:T(8,128)(2,1)}, u32[]{:S(2)}) copy-start(bf16[128,2048]{1,0:T(8,128)(2,1)} %param.16) | copy-start | bytes 1572868
  129.9 86.3 %copy-start.25 = (f32[2048]{0:T(1024)S(1)}, f32[2048]{0:T(1024)}, u32[]{:S(2)}) copy-start(f32[2048]{0:T(1024)} %param.23) | copy-start | bytes 24580
  129.9 158.6 %all-gather.7.cloned.1.call-start = ((), (), s32[]{:S(2)}) async-start(), calls=%async_computation.6 | async-start | bytes 8912896 | tf_op jit(solution)/shard_map/all_gather | solution.py:105
  216.2 261.8 %copy-start.27 = (f32[128]{0:T(128)}, f32[128]{0:T(128)S(1)}, u32[]{:S(2)}) copy-start(f32[128]{0:T(128)S(1)} %add_rsqrt_fusion) | copy-start | bytes 1540
  218.3 142.7 %all-gather.9.cloned.1.call-start = ((), (), s32[]{:S(2)}) async-start(), calls=%async_computation.8 | async-start | bytes 8912896 | tf_op jit(solution)/shard_map/all_gather | solution.py:119
  218.9 257.0 %reduce-scatter.9.cloned.1.call-start = ((), (), s32[]{:S(2)}) async-start(), calls=%async_computation.9 | async-start | bytes 8912896 | tf_op jit(solution)/shard_map/reduce_scatter | solution.py:129
  288.5 8.7 copy-start.17
  288.5 8.7 copy-start.30
  361.0 11.8 %copy-start.18 = (bf16[2048,352]{0,1:T(8,128)(2,1)S(1)}, bf16[2048,352]{0,1:T(8,128)(2,1)}, u32[]{:S(2)}) copy-start(bf16[2048,352]{0,1:T(8,128)(2,1)} %param.24) | copy-start | bytes 4325380
  372.8 8.3 copy-start.11
  372.8 8.3 copy-start.5
  372.8 8.3 copy-start.13
  391.3 84.6 %copy-start.3 = (bf16[128,2048]{1,0:T(8,128)(2,1)S(1)}, bf16[128,2048]{1,0:T(8,128)(2,1)}, u32[]{:S(2)}) copy-start(bf16[128,2048]{1,0:T(8,128)(2,1)} %reduce-scatter.5.cloned.1.call-done) | copy-start | bytes 1572868
  391.3 159.6 %all-gather.11.cloned.1.call-start = ((), (), s32[]{:S(2)}) async-start(), calls=%async_computation.10 | async-start | bytes 8912896 | tf_op jit(solution)/shard_map/all_gather | solution.py:141
  480.5 214.6 %all-reduce.4.cloned.1.call-start = ((), (), s32[]{:S(2)}) async-start(), calls=%async_computation.12 | async-start | bytes 11010048 | tf_op jit(solution)/shard_map/psum | solution.py:195
  480.6 8.2 copy-start.12
  480.6 16.5 %slice-start.2 = ((s8[8388608]{0:T(1024)(128)(4,1)}), s8[4194304]{0:T(1024)(128)(4,1)S(1)}, s32[]{:S(2)}) async-start(s8[8388608]{0:T(1024)(128)(4,1)} %bitcast.194), calls=%async_computation.15 | async-start | bytes 8388608
  488.9 8.3 slice-start.3
  488.9 8.3 copy-start.32
  601.8 10.7 %slice-start = ((s8[8388608]{0:T(1024)(128)(4,1)}), s8[4194304]{0:T(1024)(128)(4,1)S(1)}, s32[]{:S(2)}) async-start(s8[8388608]{0:T(1024)(128)(4,1)} %bitcast.180), calls=%async_computation.13 | async-start | bytes 8388608
  615.8 9.2 %copy-start.24 = (bf16[2048,16]{0,1:T(8,128)(2,1)S(1)}, bf16[2048,16]{0,1:T(8,128)(2,1)}, u32[]{:S(2)}) copy-start(bf16[2048,16]{0,1:T(8,128)(2,1)} %param.20) | copy-start | bytes 196612
  615.8 167.9 %reduce-scatter.11.cloned.1.call-start = ((), (), s32[]{:S(2)}) async-start(), calls=%async_computation.11 | async-start | bytes 8912896 | tf_op jit(solution)/shard_map/reduce_scatter | solution.py:184
  625.0 8.3 copy-start.21
  649.6 222.2 %reduce-scatter.7.cloned.1.call-start = ((), (), s32[]{:S(2)}) async-start(), calls=%async_computation.7 | async-start | bytes 8912896 | tf_op jit(solution)/shard_map/reduce_scatter | solution.py:111
  695.1 9.3 %copy-start.15 = (bf16[2048,352]{0,1:T(8,128)(2,1)S(1)}, bf16[2048,352]{0,1:T(8,128)(2,1)}, u32[]{:S(2)}) copy-start(bf16[2048,352]{0,1:T(8,128)(2,1)} %get-tuple-element.416) | copy-start | bytes 4325380
  704.4 79.3 %copy-start.26 = (f32[2048]{0:T(1024)S(1)}, f32[2048]{0:T(1024)}, u32[]{:S(2)}) copy-start(f32[2048]{0:T(1024)} %param.18) | copy-start | bytes 24580
  704.4 167.4 %copy-start.6 = (bf16[128,2048]{1,0:T(8,128)(2,1)S(1)}, bf16[128,2048]{1,0:T(8,128)(2,1)}, u32[]{:S(2)}) copy-start(bf16[128,2048]{1,0:T(8,128)(2,1)} %param.27) | copy-start | bytes 1572868
  704.4 167.4 %copy-start.7 = (bf16[128,2048]{1,0:T(8,128)(2,1)S(1)}, bf16[128,2048]{1,0:T(8,128)(2,1)}, u32[]{:S(2)}) copy-start(bf16[128,2048]{1,0:T(8,128)(2,1)} %reduce-scatter.9.cloned.1.call-done) | copy-start | bytes 1572868
  (23 other events, 64.8 us)
Sparse Core Ops, SparseCore 0:
  11.3 73.3 all-gather.4
  130.1 84.7 reduce-scatter.4
  218.4 70.0 all-gather.6
  290.5 70.4 all-gather.8
  391.5 84.3 reduce-scatter.8
  480.6 70.2 all-gather.10
  615.9 79.1 all-reduce.3
  698.5 85.1 reduce-scatter.10
  787.2 84.5 reduce-scatter.6
where the time goes:
time: 891 us; the launch traced here: 882 us
  waiting for transfers between devices  551 us (62%)
  matrix products  186 us (21%)
  blocking collectives  65.8 us (7%)
  other arithmetic  37.8 us (4%)
  loops' own time  16.2 us (2%)
  between operations  14.6 us (2%)
  local copies, waits for them, and re-layouts  10 us (1%)
    reduce_scatter x1, waiting for transfers between devices, body(): lax.psum_scatter(rows_product(rows_of(mixed_out, jnp.int32(0), rows * lax...  84.9 us
    reduce_scatter x1, waiting for transfers between devices, body(): lax.psum_scatter((against(rows_of(gate_delta, start, rows * lax.axis_size...  84.5 us
    reduce_scatter x1, waiting for transfers between devices, body(): lax.psum_scatter((total + against(rows_of(grad_values, start, rows * lax....  75.5 us
    all_gather x1, waiting for transfers between devices, body(): seq_first = lax.all_gather(first_normed, 'mp', axis=0, tiled=True)  72.1 us
    dot_general x7, matrix products, against(): return jnp.einsum('ta,ba->tb', left, right, preferred_element_type=F32)  70.7 us
    all_gather x1, waiting for transfers between devices, body(): seq_second = lax.all_gather(second_normed, 'mp', axis=0, tiled=True)  69.2 us
    psum x1, blocking collectives, body(): gain_totals = lax.psum((gain_first_part, gain_second_part), ('dp', 'mp'))  65.8 us
    all_gather x1, waiting for transfers between devices, body(): cot_rows = lax.all_gather(out_grad, 'mp', axis=0, tiled=True)  59 us
  transfers between devices with their start and end apart: 9, of which 9 were waited for; matrix products, arithmetic and copies ran while one was open for 11% of the time, Pallas kernels for 0%

commit v1 on v0

v1 whole, which is shorter than its diff:
```python
import jax
import jax.numpy as jnp
from jax import lax
from jax.experimental import pallas as pl
from jax.experimental.pallas import tpu as pltpu
from jax.sharding import Mesh, PartitionSpec as P

FEAT = 16
HEAD_V = 128
EPS = 1e-05
F32 = jnp.float32
BF16 = jnp.bfloat16
TOK = 128
GROUP = 512
SEQ = 2048
HEAD_ROWS = 2 * FEAT + HEAD_V
AXES = ("x", "core", "z", "y")
D = 2048
HID = 352
PIECE = 256


def shifted(array, axis, by):
    return lax.ppermute(array, axis, [(i, (i + by) % 4) for i in range(4)])


def swapped(array):
    return lax.ppermute(array, "core", [(0, 1), (1, 0)])


def gathered(array, axis):
    return [
        array,
        shifted(array, axis, 3),
        shifted(array, axis, 2),
        shifted(array, axis, 1),
    ]


def ring_gathered(array, axis):
    half = array.shape[0] // 2
    ahead, back = shifted(array, axis, 3), shifted(array, axis, 1)
    return [array, ahead, shifted(back[:half], axis, 1), shifted(ahead[half:], axis, 3), back]


def ring_start(opposite, axis):
    return shifted(opposite[0], axis, 1), shifted(opposite[1], axis, 3)


def ring_end(arrived, ahead, back, axis):
    half = ahead.shape[0] // 2
    first, second = arrived
    ahead = jnp.concatenate([ahead[:half] + first, ahead[half:]], axis=0)
    back = jnp.concatenate([back[:half], back[half:] + second], axis=0)
    return shifted(ahead, axis, 1), shifted(back, axis, 3)


def exchanged(blocks, axis):
    return [
        blocks[0],
        shifted(blocks[1], axis, 1),
        shifted(blocks[2], axis, 2),
        shifted(blocks[3], axis, 3),
    ]


def in_order(blocks, at):
    stacked = jnp.stack(blocks)
    return jnp.concatenate(
        [lax.dynamic_index_in_dim(stacked, (j - at) % 4, 0, keepdims=False) for j in range(4)], axis=0
    )


def nn(left, right):
    return jnp.dot(left, right, preferred_element_type=F32)


def nt(left, right):
    return lax.dot_general(left, right, (((1,), (1,)), ((), ())), preferred_element_type=F32)


def tn(left, right):
    return lax.dot_general(left, right, (((0,), (0,)), ((), ())), preferred_element_type=F32)


def pair_mask(start_row, si, ti, first, rows):
    row = lax.broadcasted_iota(jnp.int32, (rows, GROUP), 0) + (si * GROUP + first)
    mask = row >= start_row
    if si == ti:
        column = lax.broadcasted_iota(jnp.int32, (rows, GROUP), 1) + ti * GROUP
        mask = mask & (row <= column)
    return mask


def forward_kernel(
    at_ref, q0, q1, q2, q3, start_ref, mixed_ref, numer_ref, denom_ref, qkv_ref, keys
):
    for d, ref in enumerate((q0, q1, q2, q3)):
        qkv_ref[(at_ref[2] + 4 - d) % 4] = ref[...]
    for si in range(4):
        keys[si] = jnp.transpose(qkv_ref[si, FEAT : 2 * FEAT, :].astype(F32)).astype(BF16)
    for ti in range(4):
        query = (qkv_ref[ti, 0:FEAT, :].astype(F32) * (FEAT**-0.5)).astype(BF16)
        start_row = start_ref[:, ti * GROUP : (ti + 1) * GROUP]
        numer = jnp.zeros((HEAD_V, GROUP), F32)
        denom = jnp.zeros((1, GROUP), F32)
        for si in range(ti + 1):
            one = nn(keys[si], query) + 1.0
            weight = jnp.where(
                pair_mask(start_row, si, ti, 0, GROUP), 0.5 * (one * one) + 0.5, 0.0
            )
            denom = denom + jnp.sum(weight, axis=0, keepdims=True)
            numer = numer + nn(qkv_ref[si, 2 * FEAT :, :], weight.astype(BF16))
        numer_ref[ti] = numer
        denom_ref[ti] = denom
        mixed = (numer / denom).astype(BF16)
        for j in range(4):
            mixed_ref[ti * 4 + j] = mixed[:, j * TOK : (j + 1) * TOK]


def attention_forward(order, at, qkv, start_row, wait):
    return order.call(
        forward_kernel,
        "attention_forward",
        (
            jax.ShapeDtypeStruct((16, HEAD_V, TOK), BF16),
            jax.ShapeDtypeStruct((4, HEAD_V, GROUP), F32),
            jax.ShapeDtypeStruct((4, 1, GROUP), F32),
            like(4, HEAD_ROWS, GROUP),
        ),
        (at, *qkv, start_row),
        [pltpu.VMEM((4, GROUP, FEAT), BF16)],
        wait,
        in_specs=[SMEM] + [WHOLE] * 5,
        out_specs=(WHOLE,) * 4,
    )


def backward_kernel(
    at_ref,
    qkv_ref,
    cot_ref,
    numer_ref,
    denom_ref,
    start_ref,
    g0,
    g1,
    g2,
    g3,
    out_ref,
    keys,
    values,
    key_sum,
    value_sum,
):
    for si in range(4):
        keys[si] = jnp.transpose(qkv_ref[si, FEAT : 2 * FEAT, :].astype(F32)).astype(BF16)
        values[si] = jnp.transpose(qkv_ref[si, 2 * FEAT :, :].astype(F32)).astype(BF16)
    key_sum[...] = jnp.zeros_like(key_sum)
    value_sum[...] = jnp.zeros_like(value_sum)
    for ti in range(4):
        query_f32 = qkv_ref[ti, 0:FEAT, :].astype(F32) * (FEAT**-0.5)
        query = query_f32.astype(BF16)
        query_rows = jnp.transpose(query_f32).astype(BF16)
        start_row = start_ref[:, ti * GROUP : (ti + 1) * GROUP]
        inverse = 1.0 / denom_ref[ti]
        cot = jnp.concatenate([cot_ref[ti * 4 + j] for j in range(4)], axis=1).astype(F32)
        cot_denom = -jnp.sum(cot * numer_ref[ti], axis=0, keepdims=True) * (inverse * inverse)
        cot_f32 = cot * inverse
        cot_numer = cot_f32.astype(BF16)
        cot_rows = jnp.transpose(cot_f32).astype(BF16)
        query_sum = jnp.zeros((FEAT, GROUP), F32)
        for si in range(ti + 1):
            one = nn(keys[si], query) + 1.0
            mask = pair_mask(start_row, si, ti, 0, GROUP)
            weight = jnp.where(mask, 0.5 * (one * one) + 0.5, 0.0).astype(BF16)
            value_sum[si] += nn(weight, cot_rows)
            cot_weight = nn(values[si], cot_numer) + cot_denom
            cot_score = jnp.where(mask, cot_weight * one, 0.0).astype(BF16)
            key_sum[si] += nn(cot_score, query_rows)
            query_sum = query_sum + nn(qkv_ref[si, FEAT : 2 * FEAT, :], cot_score)
        out_ref[ti, 0:FEAT, :] = (query_sum * (FEAT**-0.5)).astype(BF16)
    for si in range(4):
        out_ref[si, FEAT : 2 * FEAT, :] = jnp.transpose(key_sum[si]).astype(BF16)
        out_ref[si, 2 * FEAT :, :] = jnp.transpose(value_sum[si]).astype(BF16)
    for d, ref in enumerate((g0, g1, g2, g3)):
        ref[...] = out_ref[(at_ref[2] + d) % 4]


def attention_backward(order, at, qkv, cot, numer, denom, start_row):
    return order.call(
        backward_kernel,
        "attention_backward",
        (like(HEAD_ROWS, GROUP),) * 4,
        (at, qkv, cot, numer, denom, start_row),
        [
            pltpu.VMEM((4, HEAD_ROWS, GROUP), BF16),
            pltpu.VMEM((4, GROUP, FEAT), BF16),
            pltpu.VMEM((4, GROUP, HEAD_V), BF16),
            pltpu.VMEM((4, GROUP, FEAT), F32),
            pltpu.VMEM((4, GROUP, HEAD_V), F32),
        ],
        in_specs=[SMEM] + [WHOLE] * 5,
        out_specs=(WHOLE,) * 4,
    )


VMEM_LIMIT = 52 * 2**20


class Order:
    def __init__(self):
        self.last = ()

    def call(self, kernel, name, out_shape, args, scratch=(), wait=(), **specs):
        at, first, *rest = args
        first = lax.optimization_barrier((first, *self.last, *wait))[0]
        out = pl.pallas_call(
            kernel,
            out_shape=out_shape,
            scratch_shapes=list(scratch),
            compiler_params=pltpu.CompilerParams(vmem_limit_bytes=VMEM_LIMIT),
            cost_estimate=pl.CostEstimate(flops=1, bytes_accessed=1, transcendentals=0),
            name=name,
            **specs,
        )(at, first, *rest)
        self.last = (out[0] if isinstance(out, (tuple, list)) else out,)
        return out


SMEM = pl.BlockSpec(memory_space=pltpu.SMEM)
WHOLE = pl.BlockSpec(memory_space=pltpu.VMEM)


def spec(*shape, at=None):
    def index(i):
        return tuple(i if k == at else 0 for k in range(len(shape)))

    return pl.BlockSpec(shape, index)


def like(*shape, dtype=BF16):
    return jax.ShapeDtypeStruct(shape, dtype)


def piece_at(at_ref, place, own_core):
    core = at_ref[1] if own_core else 1 - at_ref[1]
    return pl.multiple_of(((at_ref[0] + place) % 4 * 2 + core) * PIECE, PIECE)


def inverse_rms(rows):
    return lax.rsqrt(jnp.mean(rows * rows, axis=1, keepdims=True) + EPS)


def norm_back(grad_normed, unit, inverse, gains):
    scaled = grad_normed * gains
    return inverse * (scaled - unit * jnp.mean(scaled * unit, axis=1, keepdims=True))


RING_ROWS = ((0, 0, TOK), (1, 0, TOK), (2, 0, TOK // 2), (2, TOK // 2, TOK // 2), (3, 0, TOK))


def project_kernel(at_ref, *refs):
    tokens, weights, gain_ref = refs[:5], refs[5:10], refs[10]
    outs, normed_ref = refs[11:15], refs[15]
    for token_ref, (d, first, count) in zip(tokens, RING_ROWS):
        rows = token_ref[...].astype(F32)
        normed = (rows * inverse_rms(rows) * gain_ref[...]).astype(BF16)
        at = pl.multiple_of((at_ref[3] + d) % 4 * TOK, TOK) + first
        normed_ref[pl.ds(pl.multiple_of(at, count), count), :] = normed
    normed = normed_ref[...]
    half = HEAD_ROWS // 2
    for d, w_ref in ((0, weights[0]), (1, weights[1]), (3, weights[4])):
        outs[d][...] = nt(w_ref[...], normed).astype(BF16)
    outs[2][:half, :] = nt(weights[2][...], normed).astype(BF16)
    outs[2][half:, :] = nt(weights[3][...], normed).astype(BF16)


def project(order, at, token_blocks, head_blocks, gain, wait):
    return order.call(
        project_kernel,
        "project",
        (like(HEAD_ROWS, GROUP),) * 4 + (like(GROUP, D),),
        (at, *token_blocks, *head_blocks, gain[None, :]),
        wait=wait,
        in_specs=[SMEM] + [WHOLE] * 11,
        out_specs=(WHOLE,) * 5,
    )


def half_at(at_ref, own):
    core = at_ref[1] if own else 1 - at_ref[1]
    return pl.ds(pl.multiple_of(core * 1024, 1024), 1024)


def middle_kernel(at_ref, mixed_ref, token_ref, gain_ref, own_ref, other_ref, mid_ref, normed_ref):
    mixed = jnp.transpose(mixed_ref[...].astype(F32)).astype(BF16)
    for own, w_ref in ((True, own_ref), (False, other_ref)):
        columns = half_at(at_ref, own)
        mid_ref[:, columns] = token_ref[:, columns].astype(F32) + nn(mixed, w_ref[...])
    mid = mid_ref[...]
    normed_ref[...] = (mid * inverse_rms(mid) * gain_ref[...]).astype(BF16)


def middle(order, at, mixed, tokens, gain, weights):
    return order.call(
        middle_kernel,
        "middle",
        (like(TOK, D, dtype=F32), like(TOK, D)),
        (at, mixed, tokens, gain[None, :], *weights),
        in_specs=[SMEM] + [WHOLE] * 5,
        out_specs=(WHOLE, WHOLE),
    )


RING = ((0, TOK), (TOK, TOK), (2 * TOK, TOK // 2), (2 * TOK + TOK // 2, TOK // 2), (3 * TOK, TOK))
RING_SPECS = [spec(count, D) for _, count in RING]
RING_LIKE = tuple(like(count, D) for _, count in RING)


def feed_kernel(at_ref, *refs):
    blocks, cot_refs, gu_mine, gu_other = refs[:5], refs[5:10], refs[10], refs[11]
    down_refs, (hidden_ref, gate_ref, up_ref) = refs[12:20], refs[20:23]
    outs, (rows, cots, downs, total) = refs[23:28], refs[28:]
    step = pl.program_id(0)

    @pl.when(step == 0)
    def _():
        for (first, count), block, cot_ref in zip(RING, blocks, cot_refs):
            at = slice(first, first + count)
            for own in (0, 1):
                rows[own, at, :] = block[:, half_at(at_ref, own == 0)]
                for d in range(4):
                    columns = pl.ds(piece_at(at_ref, d, own == 0), PIECE)
                    piece = own * 4 + d
                    cots[at, piece * PIECE : (piece + 1) * PIECE] = cot_ref[:, columns]

    weights = (gu_mine, gu_other)
    for d, w_ref in enumerate(down_refs):
        downs[:, d * PIECE : (d + 1) * PIECE] = w_ref[0]
    both_rows = nt(gu_mine[0], rows[0]) + nt(gu_other[0], rows[1])
    gate_rows, up_rows = both_rows[:HID], both_rows[HID:]
    grad_hidden = nt(downs[...], cots[...])
    sigmoid_gate = 1.0 / (1.0 + jnp.exp(-gate_rows))
    silu_gate = gate_rows * sigmoid_gate
    hidden_ref[0] = (silu_gate * up_rows).astype(BF16)
    up_delta = (grad_hidden * silu_gate).astype(BF16)
    gate_delta = (
        grad_hidden * up_rows * (sigmoid_gate + silu_gate * (1.0 - sigmoid_gate))
    ).astype(BF16)
    gate_ref[0] = gate_delta
    up_ref[0] = up_delta
    both_delta = jnp.concatenate([gate_delta, up_delta], axis=0)
    for own in (0, 1):
        part = tn(both_delta, weights[own][0])

        @pl.when(step == 0)
        def _():
            total[own] = part

        @pl.when(step > 0)
        def _():
            total[own] += part

    @pl.when(step == 3)
    def _():
        for (first, count), out_ref in zip(RING, outs):
            for own in (0, 1):
                out_ref[:, half_at(at_ref, own == 0)] = total[
                    own, first : first + count, :
                ].astype(BF16)


def feed(order, at, second_blocks, cot_blocks, gu_mine, gu_other, down_pieces, wait):
    deltas = like(4, HID, GROUP)
    return order.call(
        feed_kernel,
        "feed",
        (deltas, deltas, deltas) + RING_LIKE,
        (at, *second_blocks, *cot_blocks, gu_mine, gu_other, *down_pieces),
        [
            pltpu.VMEM((2, GROUP, 1024), BF16),
            pltpu.VMEM((GROUP, D), BF16),
            pltpu.VMEM((HID, D), BF16),
            pltpu.VMEM((2, GROUP, 1024), F32),
        ],
        wait,
        grid=(4,),
        in_specs=[SMEM]
        + RING_SPECS * 2
        + [spec(1, 2 * HID, 1024, at=0)] * 2
        + [spec(1, HID, PIECE, at=0)] * 8,
        out_specs=(spec(1, HID, GROUP, at=0),) * 3 + tuple(RING_SPECS),
    )


def down_kernel(at_ref, hidden_ref, *refs):
    weights, outs, rows = refs[:8], refs[8:13], refs[13]
    for z in range(4):
        rows[z] = jnp.transpose(hidden_ref[z].astype(F32)).astype(BF16)
    for d in range(8):
        part = nn(rows[0], weights[d][0])
        for z in range(1, 4):
            part = part + nn(rows[z], weights[d][z])
        columns = pl.ds(piece_at(at_ref, d % 4, d < 4), PIECE)
        for (first, count), out_ref in zip(RING, outs):
            out_ref[:, columns] = part[first : first + count].astype(BF16)


def down(order, at, hidden, down_pieces):
    return order.call(
        down_kernel,
        "down",
        RING_LIKE,
        (at, hidden, *down_pieces),
        [pltpu.VMEM((4, GROUP, HID), BF16)],
        in_specs=[SMEM] + [WHOLE] * 9,
        out_specs=(WHOLE,) * 5,
    )


def feed_grads_kernel(own, count, at_ref, *refs):
    lefts, blocks, others = refs[:count], refs[count : count + 5], refs[count + 5 : -2]
    out_ref, rows = refs[-2:]
    step = pl.program_id(0)

    @pl.when(step == 0)
    def _():
        core = at_ref[1] if own else 1 - at_ref[1]
        for (first, size), block in zip(RING, blocks):
            for k in range(4):
                columns = pl.ds(pl.multiple_of((k * 2 + core) * PIECE, PIECE), PIECE)
                rows[first : first + size, k * PIECE : (k + 1) * PIECE] = block[:, columns]

    for i, left_ref in enumerate(lefts):
        part = nn(left_ref[0], rows[...])
        for k in range(4):
            block = part[:, k * PIECE : (k + 1) * PIECE]
            if own:
                block = block + others[0][k, 0, i * HID : (i + 1) * HID, :].astype(F32)
            out_ref[k, 0, i * HID : (i + 1) * HID, :] = block.astype(BF16)


def feed_grads(order, at, lefts, blocks, other=None, wait=()):
    own, count = other is not None, len(lefts)
    grads = spec(4, 1, count * HID, PIECE, at=1)
    return order.call(
        lambda *refs: feed_grads_kernel(own, count, *refs),
        "feed_grads_own" if own else "feed_grads",
        like(4, 4, count * HID, PIECE),
        (at, *lefts, *blocks) + ((other,) if own else ()),
        [pltpu.VMEM((GROUP, 1024), BF16)],
        wait,
        grid=(4,),
        in_specs=[SMEM]
        + [spec(1, HID, GROUP, at=0)] * count
        + RING_SPECS
        + ([grads] if own else []),
        out_specs=grads,
    )


def turn_kernel(
    at_ref,
    s0,
    s1,
    s3,
    mid_ref,
    cot_ref,
    gain_ref,
    own_ref,
    other_ref,
    grad_mid_ref,
    branch_ref,
    mixed_ref,
    gain_part_ref,
):
    grad_second = s0[...].astype(F32) + s1[...].astype(F32) + s3[...].astype(F32)
    mid = mid_ref[...]
    inverse = inverse_rms(mid)
    unit = mid * inverse
    gain_part_ref[...] = jnp.sum(grad_second * unit, axis=0, keepdims=True)
    grad_mid = cot_ref[...].astype(F32) + norm_back(grad_second, unit, inverse, gain_ref[...])
    grad_mid_ref[...] = grad_mid
    branch_ref[...] = grad_mid.astype(BF16)
    total = nt(own_ref[...], branch_ref[:, half_at(at_ref, True)])
    total = total + nt(other_ref[...], branch_ref[:, half_at(at_ref, False)])
    mixed_ref[...] = total.astype(BF16)


def turn(order, at, second_sums, mid_rows, out_grad, gain, weights):
    return order.call(
        turn_kernel,
        "turn",
        (
            like(TOK, D, dtype=F32),
            like(TOK, D),
            like(D, TOK),
            like(1, D, dtype=F32),
        ),
        (at, *second_sums, mid_rows, out_grad, gain[None, :], *weights),
        in_specs=[SMEM] + [WHOLE] * 8,
        out_specs=(WHOLE,) * 4,
    )


def split_pieces(at_ref, rows, d, mine_ref, other_ref):
    for k in range(4):
        low = rows[:, 2 * k * PIECE : (2 * k + 1) * PIECE]
        high = rows[:, (2 * k + 1) * PIECE : (2 * k + 2) * PIECE]
        first = at_ref[1] == 0
        count = rows.shape[0]
        mine_ref[d, k, :count] = jnp.where(first, low, high).astype(BF16)
        other_ref[d, k, :count] = jnp.where(first, high, low).astype(BF16)


def out_grads_kernel(at_ref, m0, m1, m2, m3, b0, b1, b2a, b2b, b3, mine_ref, other_ref, rows):
    for (first, count), block_ref in zip(RING, (b0, b1, b2a, b2b, b3)):
        rows[first : first + count, :] = block_ref[...]
    for back, mixed_ref in enumerate((m0, m1, m2, m3)):
        mixed = jnp.concatenate([mixed_ref[(at_ref[3] + d) % 4] for d in range(4)], axis=1)
        split_pieces(at_ref, nn(mixed, rows[...]), (4 - back) % 4, mine_ref, other_ref)


def out_grads(order, at, mixed_heads, branch_blocks):
    return order.call(
        out_grads_kernel,
        "out_grads",
        (like(4, 4, HEAD_V, PIECE), like(4, 4, HEAD_V, PIECE)),
        (at, *mixed_heads, *branch_blocks),
        [pltpu.VMEM((GROUP, D), BF16)],
        in_specs=[SMEM] + [WHOLE] * 9,
        out_specs=(WHOLE, WHOLE),
    )


BOTH_ROWS = HEAD_ROWS + HEAD_V


def head_grads_kernel(
    at_ref, g0, g1, g2, g3, normed_ref, out_mine, out_other, mine_ref, other_ref
):
    for back, grads_ref in enumerate((g0, g1, g2, g3)):
        part = nn(grads_ref[...], normed_ref[...])
        split_pieces(at_ref, part, (4 - back) % 4, mine_ref, other_ref)
    mine_ref[:, :, HEAD_ROWS:, :] = out_mine[...]
    other_ref[:, :, HEAD_ROWS:, :] = out_other[...]


def head_grads(order, at, grads, normed, outs):
    both = like(4, 4, BOTH_ROWS, PIECE)
    return order.call(
        head_grads_kernel,
        "head_grads",
        (both, both),
        (at, *grads, normed, *outs),
        in_specs=[SMEM] + [WHOLE] * 7,
        out_specs=(WHOLE, WHOLE),
    )


def first_kernel(at_ref, *refs):
    grads, (w0, w1, w2a, w2b, w3), tokens = refs[:4], refs[4:9], refs[9:14]
    outs, gain_ref = refs[14:19], refs[19]
    half = HEAD_ROWS // 2
    gain_part = jnp.zeros((1, D), F32)
    for token_ref, out_ref, (d, first, count) in zip(tokens, outs, RING_ROWS):
        columns = pl.ds(pl.multiple_of((at_ref[3] + d) % 4 * TOK, TOK), TOK)
        part = tn(grads[0][:, columns], w0[...]) + tn(grads[3][:, columns], w1[...])
        part = part + tn(grads[1][:, columns], w3[...])
        part = part + tn(grads[2][:half, columns], w2a[...])
        part = part + tn(grads[2][half:, columns], w2b[...])
        part = part[first : first + count]
        rows = token_ref[...].astype(F32)
        gain_part = gain_part + jnp.sum(part * (rows * inverse_rms(rows)), axis=0, keepdims=True)
        out_ref[...] = part.astype(BF16)
    gain_ref[...] = gain_part


def first_part(order, at, grads, head_blocks, token_blocks):
    return order.call(
        first_kernel,
        "first_part",
        RING_LIKE + (like(1, D, dtype=F32),),
        (at, *grads, *head_blocks, *token_blocks),
        in_specs=[SMEM] + [WHOLE] * 14,
        out_specs=(WHOLE,) * 6,
    )


def collect_kernel(at_ref, *refs):
    outs = refs[8:]
    for own in (True, False):
        for d in range(4):
            columns = pl.ds(piece_at(at_ref, d, own), PIECE)
            first = 0
            for out_ref in outs:
                rows = out_ref.shape[0]
                block = refs[d if own else 4 + d][first : first + rows, :]
                out_ref[:, columns] = block.astype(F32)
                first += -rows // 16 * -16


def collect(order, at, mine, name, *rows):
    other = [swapped(block) for block in mine]
    return order.call(
        collect_kernel,
        name,
        tuple(like(r, D, dtype=F32) for r in rows),
        (at, *mine, *other),
        in_specs=[SMEM] + [WHOLE] * 8,
        out_specs=(WHOLE,) * len(rows),
    )


def after(array, *needed):
    return lax.optimization_barrier((array, *needed))[0]


def body(
    tokens,
    doc_start,
    gain_first,
    w_query,
    w_key,
    w_value,
    w_out,
    gain_second,
    w_gate,
    w_up,
    w_down,
    out_grad,
):
    order = Order()
    at = jnp.stack([lax.axis_index(a) for a in AXES]).astype(jnp.int32)
    x_at, core, z_at, y_at = (at[i] for i in range(4))

    token_blocks = ring_gathered(tokens, "y")
    w_head = jnp.concatenate([w_query.T, w_key.T, w_value.T], axis=0)
    head_blocks = ring_gathered(w_head, "z")
    out_half = lax.dynamic_slice_in_dim(w_out, core * 1024, 1024, 1)
    out_mine = lax.all_gather(out_half, ("z", "y"), axis=0, tiled=True)
    piece = lax.dynamic_slice_in_dim(w_down, (x_at * 2 + core) * PIECE, PIECE, 1)
    gate_up = jnp.concatenate([w_gate.T, w_up.T], axis=0)
    gate_up = lax.dynamic_slice_in_dim(gate_up, core * 1024, 1024, 1)
    *qkv, group_normed = project(order, at, token_blocks, head_blocks, gain_first, ())
    qkv = exchanged(qkv, "z")
    gu_mine = lax.all_gather(after(gate_up, *qkv), "z", axis=0)
    down_piece = in_order([b[None] for b in gathered(piece, "z")], z_at)
    down_mine = gathered(down_piece, "x")
    cot_blocks = ring_gathered(out_grad, "y")

    positions = jnp.arange(SEQ, dtype=jnp.int32)
    start_row = lax.cummax(jnp.where(doc_start != 0, positions, 0))[None, :]
    mixed, numer, denom, qkv = attention_forward(order, at, qkv, start_row, ())
    mixed_tokens = lax.all_to_all(mixed, ("z", "y"), 0, 0).reshape(SEQ, TOK)
    out_mine = after(out_mine, mixed)
    out_weights = (out_mine, swapped(out_mine))
    mid_rows, second_normed = middle(order, at, mixed_tokens, tokens, gain_second, out_weights)

    second_blocks = ring_gathered(second_normed, "y")
    mixed_groups = mixed.reshape(4, 4, HEAD_V, TOK)
    mixed_heads = exchanged(
        [lax.dynamic_index_in_dim(mixed_groups, (z_at + d) % 4, 0, False) for d in range(4)], "z"
    )
    gu_mine, *down_mine, _ = lax.optimization_barrier((gu_mine, *down_mine, second_normed))
    gu_other = swapped(gu_mine)
    down_pieces = [*down_mine, *(swapped(b) for b in down_mine)]
    hidden, gate_delta, up_delta, s0, s1, *s2, s3 = feed(
        order, at, second_blocks, cot_blocks, gu_mine, gu_other, down_pieces, mixed_heads
    )
    arrived = ring_start(s2, "y")
    second_sums = (s0, *ring_end(arrived, s1, s3, "y"))
    gu_grads = swapped(
        feed_grads(order, at, (gate_delta, up_delta), second_blocks, wait=arrived)
    )
    b0, b1, *b2, b3 = down(order, at, hidden, down_pieces)
    gu_grads = feed_grads(order, at, (gate_delta, up_delta), second_blocks, gu_grads)
    gu_sum = lax.psum_scatter(
        gu_grads.reshape(16, 2 * HID, PIECE), ("x", "z"), scatter_dimension=0
    )

    grad_mid, grad_branch, grad_mixed, gain_second_part = turn(
        order, at, second_sums, mid_rows, out_grad, gain_second, out_weights
    )
    grad_mixed = lax.all_to_all(grad_mixed.reshape(16, HEAD_V, TOK), ("z", "y"), 0, 0)
    branch_blocks = ring_gathered(grad_branch, "y")
    down_grads = swapped(feed_grads(order, at, (hidden,), cot_blocks))
    down_grads = feed_grads(order, at, (hidden,), cot_blocks, down_grads)
    down_grads = [
        lax.dynamic_index_in_dim(down_grads, (z_at + d) % 4, 1, False) for d in range(4)
    ]
    grads = attention_backward(order, at, qkv, grad_mixed, numer, denom, start_row)
    grads = exchanged(grads, "z")

    def added(blocks):
        total = (blocks[0].astype(F32) + blocks[1].astype(F32)) + (
            blocks[2].astype(F32) + blocks[3].astype(F32)
        )
        return total.astype(BF16)

    def summed(blocks):
        part = added(exchanged(blocks, "z"))
        return added(
            exchanged(
                [lax.dynamic_index_in_dim(part, (x_at + d) % 4, 0, False) for d in range(4)], "x"
            )
        )

    down_sum = summed(down_grads)
    outs = out_grads(order, at, mixed_heads, branch_blocks)
    f0, f1, *f2, f3, gain_first_part = first_part(order, at, grads, head_blocks, token_blocks)
    from_back, from_ahead = ring_end(ring_start(f2, "y"), f1, f3, "y")
    mine, other = head_grads(order, at, grads, group_normed, outs)
    gains = jnp.concatenate([gain_first_part, gain_second_part], axis=0)
    blocks = gathered(gains, "y")
    gains = (blocks[0] + blocks[1]) + (blocks[2] + blocks[3])
    gains = (gains + swapped(gains)).astype(BF16).reshape(2, 4, 2, PIECE)
    gains = lax.dynamic_index_in_dim(gains, core, 2, False)
    gains = jnp.pad(jnp.transpose(gains, (1, 0, 2)), ((0, 0), (0, 14), (0, 0)))
    both = (mine.astype(F32) + swapped(other).astype(F32)).astype(BF16)
    head_sum = summed([jnp.concatenate([both[d], gains], axis=1) for d in range(4)])

    grad_first = f0.astype(F32) + from_back.astype(F32) + from_ahead.astype(F32)
    b_back, b_ahead = ring_end(ring_start(b2, "y"), b1, b3, "y")
    block_out = mid_rows + (b0.astype(F32) + b_back.astype(F32) + b_ahead.astype(F32))
    x_rows = tokens.astype(F32)
    first_inv = inverse_rms(x_rows)
    input_grad = grad_mid + norm_back(grad_first, x_rows * first_inv, first_inv, gain_first)

    ffn_sum = jnp.concatenate([gu_sum, down_sum], axis=0)
    grad_gate, grad_up, grad_down = collect(
        order, at, gathered(ffn_sum, "x"), "collect_feed", HID, HID, HID
    )
    grad_query, grad_key, grad_value, grad_out, gains = collect(
        order, at, gathered(head_sum, "x"), "collect_heads", FEAT, FEAT, HEAD_V, HEAD_V, 2
    )
    return (
        block_out,
        input_grad,
        gains[0],
        grad_query.T,
        grad_key.T,
        grad_value.T,
        grad_out,
        gains[1],
        grad_gate.T,
        grad_up.T,
        grad_down,
    )


def solution(mesh):
    fine = Mesh(mesh.devices.reshape(4, 2, 4, 4), AXES)
    rows, dp, mp = P(AXES, None), P(("x", "core")), ("z", "y")
    return jax.shard_map(
        body,
        mesh=fine,
        in_specs=(
            rows,
            dp,
            P(),
            P(None, mp),
            P(None, mp),
            P(None, mp),
            P(mp, None),
            P(),
            P(None, mp),
            P(None, mp),
            P(mp, None),
            rows,
        ),
        out_specs=(
            rows,
            rows,
            P(),
            P(None, mp),
            P(None, mp),
            P(None, mp),
            P(mp, None),
            P(),
            P(None, mp),
            P(None, mp),
            P(mp, None),
        ),
        check_vma=False,
    )
```

time: 891 us -> 521 us (0.58)
  waiting for transfers between devices: 551 us -> 199 us
  matrix products: 186 us -> 0 us
  Pallas kernels: 0 us -> 120 us
  starting transfers between devices: 0.83 us -> 112 us
  blocking collectives: 65.8 us -> 16.7 us
  loops' own time: 16.2 us -> 0 us
  local copies, waits for them, and re-layouts: 10 us -> 25.6 us
  other arithmetic: 37.8 us -> 24 us
    reduce_scatter x4 -> x0, waiting for transfers between devices: 264 us -> none  [the longest x1 84.9 us: body(): lax.psum_scatter(rows_product(rows_of(mixed_out, jnp.int32(0), rows * lax...]
    all_gather x4 -> x2, waiting for transfers between devices: 250 us -> 12.9 us  [the longest x1 12.9 us: body(): gu_mine = lax.all_gather(after(gate_up, *qkv), 'z', axis=0)]
    ppermute x0 -> x86, waiting for transfers between devices: none -> 186 us  [the longest x68 185 us: shifted(): return lax.ppermute(array, axis, [(i, (i + by) % 4) for i in range(4)])]
    dot_general x49 -> x0, matrix products: 186 us -> none  [the longest x7 70.7 us: against(): return jnp.einsum('ta,ba->tb', left, right, preferred_element_type=F32)]
    pallas_call x0 -> x16, Pallas kernels: none -> 120 us  [call(): pl.pallas_call(kernel, out_shape=out_shape, scratch_shapes=list(scratch),...]
    ppermute x0 -> x86, starting transfers between devices: none -> 108 us  [the longest x68 105 us: shifted(): return lax.ppermute(array, axis, [(i, (i + by) % 4) for i in range(4)])]
    psum x1 -> x0, blocking collectives: 65.8 us -> none  [body(): gain_totals = lax.psum((gain_first_part, gain_second_part), ('dp', 'mp'))]
    psum x1 -> x0, waiting for transfers between devices: 36.9 us -> none  [body(): lax.psum(grad_query.astype(jnp.bfloat16), 'dp').astype(jnp.float32)]
  transfers between devices with their start and end apart: 9 -> 90, of which waited for: 9 -> 41; matrix products, arithmetic and copies ran while one was open for 11% -> 6% of each run, Pallas kernels for 0% -> 15%
where the time goes in v1:
time: 521 us; the launch traced here: 512 us
  waiting for transfers between devices  199 us (38%)
  Pallas kernels  120 us (23%)
  starting transfers between devices  112 us (21%)
  local copies, waits for them, and re-layouts  25.6 us (5%)
  other arithmetic  24 us (5%)
  blocking collectives  16.7 us (3%)
  between operations  15.1 us (3%)
    ppermute x68, waiting for transfers between devices, shifted(): return lax.ppermute(array, axis, [(i, (i + by) % 4) for i in range(4)])  185 us
    pallas_call x16, Pallas kernels, call(): pl.pallas_call(kernel, out_shape=out_shape, scratch_shapes=list(scratch),...  120 us
    ppermute x68, starting transfers between devices, shifted(): return lax.ppermute(array, axis, [(i, (i + by) % 4) for i in range(4)])  105 us
    all_to_all x1, blocking collectives, body(): mixed_tokens = lax.all_to_all(mixed, ('z', 'y'), 0, 0).reshape(SEQ, TOK)  16.7 us
    unnamed x155, local copies, waits for them, and re-layouts  16 us
    all_gather x1, waiting for transfers between devices, body(): gu_mine = lax.all_gather(after(gate_up, *qkv), 'z', axis=0)  12.9 us
  transfers between devices with their start and end apart: 90, of which 41 were waited for; matrix products, arithmetic and copies ran while one was open for 6% of the time, Pallas kernels for 15%

profile of v1, /device:TPU:0, one launch (start us, length us, event | category | flops | bytes accessed | tf_op | source)
XLA Modules:
  0.0 512.0 jit_solution(226868622411412078)
XLA Ops:
  18.0 12.8 %collective-permute-done.5.refs_9_.refs_8_ = bf16[160,2048]{1,0:T(8,128)(2,1)S(1)} collective-permute-done((bf16[160,2048]{1,0:T(8,128)(2,1)S(1)}, bf16[160,2048]{1,0:T(8,128)(2,1)S(1)}, u32[]{:S(2)}, u32[]{:S(2)}) %collective-permute-start.5) | collective-permute-done | bytes 655392 | tf_op jit(solution)/shard_map/ppermute | solution.py:24
  45.5 7.0 %project.1 = (bf16[160,512]{1,0:T(8,128)(2,1)S(1)}, bf16[160,512]{1,0:T(8,128)(2,1)S(1)}, bf16[160,512]{1,0:T(8,128)(2,1)S(1)}, bf16[160,512]{1,0:T(8,128)(2,1)S(1)}, bf16[512,2048]{1,0:T(8,128)(2,1)}) custom-call(s32[4]{0:T(128)S(1)} %pad_add_fusion.at_ref.refs_0_, bf16[128,2048]{1,0:T(8,128)(2,1)} %refs_9_.1, bf16[128,2048]{1,0:T(8,128)(2,1)} %copy-done.46, ...), custom_call_target="tpu_custom_call" | custom-call | flops 1 | bytes 1 | tf_op jit(solution)/shard_map/project/pallas_call | solution.py:218
  57.9 5.8 %collective-permute-done.10.q3 = bf16[160,512]{1,0:T(8,128)(2,1)S(1)} collective-permute-done((bf16[160,512]{1,0:T(8,128)(2,1)S(1)}, bf16[160,512]{1,0:T(8,128)(2,1)S(1)}, u32[]{:S(2)}, u32[]{:S(2)}) %collective-permute-start.10) | collective-permute-done | bytes 163872 | tf_op jit(solution)/shard_map/ppermute | solution.py:24
  63.7 4.2 collective-permute-done.8.q1
  71.6 5.6 %attention_forward.1 = (bf16[16,128,128]{2,1,0:T(8,128)(2,1)S(1)}, f32[4,128,512]{2,1,0:T(8,128)}, f32[4,1,512]{2,1,0:T(1,128)S(1)}, bf16[4,160,512]{2,1,0:T(8,128)(2,1)S(1)}) custom-call(s32[4]{0:T(128)S(1)} %pad_add_fusion.at_ref.refs_0_, bf16[160,512]{1,0:T(8,128)(2,1)S(1)} %copy-done.26, bf16[160,512]{1,0:T(8,128)(2,1)S(1)} %collective-permute-done.8.q1, ...), custom_call_target="tpu_custom_call" | custom-call | flops 1 | bytes 1 | tf_op jit(solution)/shard_map/attention_forward/pallas_call | solution.py:218
  97.1 16.7 %all_to_all.10 = bf16[16,128,128]{2,1,0:T(8,128)(2,1)S(1)} all-to-all(bf16[16,128,128]{2,1,0:T(8,128)(2,1)S(1)} %get-tuple-element.88), channel_id=1, replica_groups=mesh['x'=4,'core'=2,'z'=4,'y'=4] {'z','y'}, dimensions={0} | all-to-all | bytes 1048576 | tf_op jit(solution)/shard_map/all_to_all | solution.py:656
  113.9 5.8 %middle.1 = (f32[128,2048]{1,0:T(8,128)}, bf16[128,2048]{1,0:T(8,128)(2,1)S(1)}) custom-call(s32[4]{0:T(128)S(1)} %pad_add_fusion.at_ref.refs_0_, bf16[2048,128]{1,0:T(8,128)(2,1)S(1)} %bitcast.91, bf16[128,2048]{1,0:T(8,128)(2,1)S(1)} %copy-done.3, f32[1,2048]{1,0:T(1,128)S(1)} %bitcast.97, bf16[2048,1024]{1,0:T(8,128)(2,1)} %all-gather.4.cloned.1.call-done.own_ref, ...), custom_call_target="tpu_custom_call" | custom-call | flops 1 | bytes 1 | tf_op jit(solution)/shard_map/middle/pallas_call | solution.py:218
  119.7 6.7 %collective-permute-done.26.refs_13_.refs_1_ = bf16[4,352,256]{2,1,0:T(8,128)(2,1)S(1)} collective-permute-done((bf16[4,352,256]{2,1,0:T(8,128)(2,1)S(1)}, bf16[4,352,256]{2,1,0:T(8,128)(2,1)S(1)}, u32[]{:S(2)}, u32[]{:S(2)}) %collective-permute-start.26) | collective-permute-done | bytes 720928 | tf_op jit(solution)/shard_map/ppermute | solution.py:24
  130.2 12.9 %all-gather.6.cloned.1.call-done = bf16[2816,1024]{1,0:T(8,128)(2,1)} async-done(((bf16[704,1024]{1,0:T(8,128)(2,1)}), bf16[2816,1024]{1,0:T(8,128)(2,1)}) %all-gather.6.cloned.1.call-update) | async-done | bytes 5767184 | tf_op jit(solution)/shard_map/all_gather | solution.py:648
  146.4 12.4 %collective-permute-done.20.refs_9_.refs_6_ = bf16[128,2048]{1,0:T(8,128)(2,1)S(1)} collective-permute-done((bf16[128,2048]{1,0:T(8,128)(2,1)S(1)}, bf16[128,2048]{1,0:T(8,128)(2,1)S(1)}, u32[]{:S(2)}, u32[]{:S(2)}) %collective-permute-start.20) | collective-permute-done | bytes 524320 | tf_op jit(solution)/shard_map/ppermute | solution.py:24
  164.5 6.5 %collective-permute-done.21.refs_7_.refs_4_ = bf16[64,2048]{1,0:T(8,128)(2,1)S(1)} collective-permute-done((bf16[64,2048]{1,0:T(8,128)(2,1)}, bf16[64,2048]{1,0:T(8,128)(2,1)S(1)}, u32[]{:S(2)}, u32[]{:S(2)}) %collective-permute-start.21) | collective-permute-done | bytes 262176 | tf_op jit(solution)/shard_map/ppermute | solution.py:24
  186.0 6.7 %collective-permute-done.17.refs_2_.refs_5_ = bf16[64,2048]{1,0:T(8,128)(2,1)S(1)} collective-permute-done((bf16[64,2048]{1,0:T(8,128)(2,1)S(1)}, bf16[64,2048]{1,0:T(8,128)(2,1)S(1)}, u32[]{:S(2)}, u32[]{:S(2)}) %collective-permute-start.17) | collective-permute-done | bytes 262176 | tf_op jit(solution)/shard_map/ppermute | solution.py:24
  192.7 25.9 %feed.1 = (bf16[4,352,512]{2,1,0:T(8,128)(2,1)}, bf16[4,352,512]{2,1,0:T(8,128)(2,1)}, bf16[4,352,512]{2,1,0:T(8,128)(2,1)}, bf16[128,2048]{1,0:T(8,128)(2,1)}, ...) custom-call(s32[4]{0:T(128)S(1)} %pad_add_fusion.at_ref.refs_0_, ...), custom_call_target="tpu_custom_call" | custom-call | flops 1 | bytes 1 | tf_op jit(solution)/shard_map/feed/pallas_call | solution.py:218
  221.7 5.1 %collective-permute-done.35 = bf16[64,2048]{1,0:T(8,128)(2,1)S(1)} collective-permute-done((bf16[64,2048]{1,0:T(8,128)(2,1)S(1)}, bf16[64,2048]{1,0:T(8,128)(2,1)S(1)}, u32[]{:S(2)}, u32[]{:S(2)}) %collective-permute-start.35) | collective-permute-done | bytes 262176 | tf_op jit(solution)/shard_map/ppermute | solution.py:24
  231.3 7.0 %feed_grads.2 = bf16[4,4,704,256]{3,2,1,0:T(8,128)(2,1)} custom-call(s32[4]{0:T(128)S(1)} %pad_add_fusion.at_ref.refs_0_, bf16[4,352,512]{2,1,0:T(8,128)(2,1)} %get-tuple-element.113.refs_1_, bf16[4,352,512]{2,1,0:T(8,128)(2,1)} %get-tuple-element.105.refs_2_, bf16[128,2048]{1,0:T(8,128)(2,1)S(1)} %copy-done.13, bf16[128,2048]{1,0:T(8,128)(2,1)S(1)} %copy-done.10, ...), custom_call_target="tpu_custom_call" | custom-call | flops 1 | bytes 1 | tf_op jit(solution)/shard_map/feed_grads/pallas_call | solution.py:218
  238.6 8.6 %down.1 = (bf16[128,2048]{1,0:T(8,128)(2,1)S(1)}, bf16[128,2048]{1,0:T(8,128)(2,1)S(1)}, bf16[64,2048]{1,0:T(8,128)(2,1)}, bf16[64,2048]{1,0:T(8,128)(2,1)}, bf16[128,2048]{1,0:T(8,128)(2,1)}) custom-call(s32[4]{0:T(128)S(1)} %pad_add_fusion.at_ref.refs_0_, bf16[4,352,512]{2,1,0:T(8,128)(2,1)} %get-tuple-element.120.hidden_ref.refs_1_, ...), custom_call_target="tpu_custom_call" | custom-call | flops 1 | bytes 1 | tf_op jit(solution)/shard_map/down/pallas_call | solution.py:218
  250.8 8.4 %feed_grads_own.2 = bf16[4,4,704,256]{3,2,1,0:T(8,128)(2,1)} custom-call(s32[4]{0:T(128)S(1)} %pad_add_fusion.at_ref.refs_0_, bf16[4,352,512]{2,1,0:T(8,128)(2,1)} %get-tuple-element.113.refs_1_, bf16[4,352,512]{2,1,0:T(8,128)(2,1)} %get-tuple-element.105.refs_2_, bf16[128,2048]{1,0:T(8,128)(2,1)S(1)} %copy-done.13, bf16[128,2048]{1,0:T(8,128)(2,1)S(1)} %copy-done.11, ...), custom_call_target="tpu_custom_call" | custom-call | flops 1 | bytes 1 | tf_op jit(solution)/shard_map/feed_grads_own/pallas_call | solution.py:218
  262.6 11.8 %collective-permute-done.42.s3 = bf16[128,2048]{1,0:T(8,128)(2,1)S(1)} collective-permute-done((bf16[128,2048]{1,0:T(8,128)(2,1)S(1)}, bf16[128,2048]{1,0:T(8,128)(2,1)S(1)}, u32[]{:S(2)}, u32[]{:S(2)}) %collective-permute-start.42) | collective-permute-done | bytes 524320 | tf_op jit(solution)/shard_map/ppermute | solution.py:24
  276.6 7.9 %turn.1 = (f32[128,2048]{1,0:T(8,128)}, bf16[128,2048]{1,0:T(8,128)(2,1)}, bf16[2048,128]{1,0:T(8,128)(2,1)S(1)}, f32[1,2048]{1,0:T(1,128)S(1)}) custom-call(s32[4]{0:T(128)S(1)} %pad_add_fusion.at_ref.refs_0_, bf16[128,2048]{1,0:T(8,128)(2,1)S(1)} %copy-done.23, bf16[128,2048]{1,0:T(8,128)(2,1)} %copy-done.68, bf16[128,2048]{1,0:T(8,128)(2,1)} %copy-done.67, ...), custom_call_target="tpu_custom_call" | custom-call | flops 1 | bytes 1 | tf_op jit(solution)/shard_map/turn/pallas_call | solution.py:218
  285.3 5.2 %feed_grads.3 = bf16[4,4,352,256]{3,2,1,0:T(8,128)(2,1)} custom-call(s32[4]{0:T(128)S(1)} %pad_add_fusion.at_ref.refs_0_, bf16[4,352,512]{2,1,0:T(8,128)(2,1)} %get-tuple-element.120.hidden_ref.refs_1_, bf16[128,2048]{1,0:T(8,128)(2,1)S(1)} %copy-done.6, bf16[128,2048]{1,0:T(8,128)(2,1)S(1)} %copy-done.8, ...), custom_call_target="tpu_custom_call" | custom-call | flops 1 | bytes 1 | tf_op jit(solution)/shard_map/feed_grads/pallas_call | solution.py:218
  302.9 11.6 %collective-permute-done.45.b3 = bf16[128,2048]{1,0:T(8,128)(2,1)} collective-permute-done((bf16[128,2048]{1,0:T(8,128)(2,1)}, bf16[128,2048]{1,0:T(8,128)(2,1)}, u32[]{:S(2)}, u32[]{:S(2)}) %collective-permute-start.45) | collective-permute-done | bytes 524320 | tf_op jit(solution)/shard_map/ppermute | solution.py:24
  323.0 5.7 %feed_grads_own.3 = bf16[4,4,352,256]{3,2,1,0:T(8,128)(2,1)} custom-call(s32[4]{0:T(128)S(1)} %pad_add_fusion.at_ref.refs_0_, bf16[4,352,512]{2,1,0:T(8,128)(2,1)} %get-tuple-element.120.hidden_ref.refs_1_, bf16[128,2048]{1,0:T(8,128)(2,1)S(1)} %copy-done.6, bf16[128,2048]{1,0:T(8,128)(2,1)S(1)} %copy-done.8, ...), custom_call_target="tpu_custom_call" | custom-call | flops 1 | bytes 1 | tf_op jit(solution)/shard_map/feed_grads_own/pallas_call | solution.py:218
  328.8 8.0 %attention_backward.1 = (bf16[160,512]{1,0:T(8,128)(2,1)S(1)}, bf16[160,512]{1,0:T(8,128)(2,1)S(1)}, bf16[160,512]{1,0:T(8,128)(2,1)S(1)}, bf16[160,512]{1,0:T(8,128)(2,1)S(1)}) custom-call(s32[4]{0:T(128)S(1)} %pad_add_fusion.at_ref.refs_0_, bf16[4,160,512]{2,1,0:T(8,128)(2,1)S(1)} %copy-done.22, bf16[16,128,128]{2,1,0:T(8,128)(2,1)S(1)} %all-to-all-done.1.cot_ref, ...), custom_call_target="tpu_custom_call" | custom-call | flops 1 | bytes 1 | tf_op jit(solution)/shard_map/attention_backward/pallas_call | solution.py:218
  347.2 6.7 %first_part.1 = (bf16[128,2048]{1,0:T(8,128)(2,1)}, bf16[128,2048]{1,0:T(8,128)(2,1)}, bf16[64,2048]{1,0:T(8,128)(2,1)S(1)}, bf16[64,2048]{1,0:T(8,128)(2,1)S(1)...) custom-call(s32[4]{0:T(128)S(1)} %pad_add_fusion.at_ref.refs_0_, bf16[160,512]{1,0:T(8,128)(2,1)S(1)} %get-tuple-element.138.refs_0_.g0, ...), custom_call_target="tpu_custom_call" | custom-call | flops 1 | bytes 1 | tf_op jit(solution)/shard_map/first_part/pallas_call | solution.py:218
  356.9 5.9 %head_grads.1 = (bf16[4,4,288,256]{3,2,1,0:T(8,128)(2,1)}, bf16[4,4,288,256]{3,2,1,0:T(8,128)(2,1)}) custom-call(s32[4]{0:T(128)S(1)} %pad_add_fusion.at_ref.refs_0_, bf16[160,512]{1,0:T(8,128)(2,1)S(1)} %get-tuple-element.138.refs_0_.g0, bf16[160,512]{1,0:T(8,128)(2,1)S(1)} %collective-permute-done.48.refs_1_.g1, ...), custom_call_target="tpu_custom_call" | custom-call | flops 1 | bytes 1 | tf_op jit(solution)/shard_map/head_grads/pallas_call | solution.py:218
  369.9 7.0 %collective-permute-done.51 = bf16[64,2048]{1,0:T(8,128)(2,1)} collective-permute-done((bf16[64,2048]{1,0:T(8,128)(2,1)S(1)}, bf16[64,2048]{1,0:T(8,128)(2,1)}, u32[]{:S(2)}, u32[]{:S(2)}) %collective-permute-start.51) | collective-permute-done | bytes 262176 | tf_op jit(solution)/shard_map/ppermute | solution.py:24
  383.8 15.6 %collective-permute-done.67 = bf16[4,352,256]{2,1,0:T(8,128)(2,1)} collective-permute-done((bf16[4,352,256]{2,1,0:T(8,128)(2,1)S(1)}, bf16[4,352,256]{2,1,0:T(8,128)(2,1)}, u32[]{:S(2)}, u32[]{:S(2)}) %collective-permute-start.67) | collective-permute-done | bytes 720928 | tf_op jit(solution)/shard_map/ppermute | solution.py:24
  424.5 12.6 %collective-permute-done.61 = bf16[4,304,256]{2,1,0:T(8,128)(2,1)S(1)} collective-permute-done((bf16[4,304,256]{2,1,0:T(8,128)(2,1)S(1)}, bf16[4,304,256]{2,1,0:T(8,128)(2,1)S(1)}, u32[]{:S(2)}, u32[]{:S(2)}) %collective-permute-start.61) | collective-permute-done | bytes 622624 | tf_op jit(solution)/shard_map/ppermute | solution.py:24
  459.0 10.5 %collective-permute-done.72.refs_1_ = bf16[1056,256]{1,0:T(8,128)(2,1)S(1)} collective-permute-done((bf16[1056,256]{1,0:T(8,128)(2,1)S(1)}, bf16[1056,256]{1,0:T(8,128)(2,1)S(1)}, u32[]{:S(2)}, u32[]{:S(2)}) %collective-permute-start.72) | collective-permute-done | bytes 540704 | tf_op jit(solution)/shard_map/ppermute | solution.py:24
  481.6 4.3 collective-permute-start.81
  485.9 4.3 collective-permute-done.81.refs_3_
  494.0 5.8 %collect_feed.1 = (f32[352,2048]{1,0:T(8,128)}, f32[352,2048]{1,0:T(8,128)}, f32[352,2048]{1,0:T(8,128)}) custom-call(s32[4]{0:T(128)S(1)} %pad_add_fusion.at_ref.refs_0_, bf16[1056,256]{1,0:T(8,128)(2,1)S(1)} %pad_maximum_fusion.3.refs_0_, bf16[1056,256]{1,0:T(8,128)(2,1)S(1)} %collective-permute-done.72.refs_1_, ...), custom_call_target="tpu_custom_call" | custom-call | flops 1 | bytes 1 | tf_op jit(solution)/shard_map/collect_feed/pallas_call | solution.py:218
  (384 shorter events, 216.0 us)
Async XLA Ops:
  7.2 70.0 %all-gather.4.cloned.1.call-start = ((), (), s32[]{:S(2)}) async-start(), calls=%async_computation.3 | async-start | bytes 4456448 | tf_op jit(solution)/shard_map/all_gather | solution.py:642
  9.1 134.1 %all-gather.6.cloned.1.call-start = ((), (), s32[]{:S(2)}) async-start(), calls=%async_computation.4 | async-start | bytes 7208960 | tf_op jit(solution)/shard_map/all_gather | solution.py:648
  10.5 20.3 %collective-permute-start.5 = (bf16[160,2048]{1,0:T(8,128)(2,1)S(1)}, bf16[160,2048]{1,0:T(8,128)(2,1)S(1)}, u32[]{:S(2)}, u32[]{:S(2)}) collective-permute-start(bf16[160,2048]{1,0:T(8,128)(2,1)S(1)} %pad_maximum_fusion.2.refs_5_.refs_4_), channel_id=1, source_target_pairs={{0,4},{4,8},{8,12},{12,0},{1,5},{5,9},{9,13},{13,1},{2,6},{6,10},{... | collective-permute-start | bytes 1966088 | tf_op jit(solution)/shard_map/ppermute | solution.py:24
  14.8 21.0 %collective-permute-start.1 = (bf16[128,2048]{1,0:T(8,128)(2,1)S(1)}, bf16[128,2048]{1,0:T(8,128)(2,1)S(1)}, u32[]{:S(2)}, u32[]{:S(2)}) collective-permute-start(bf16[128,2048]{1,0:T(8,128)(2,1)S(1)} %copy-done.2), channel_id=1, source_target_pairs={{0,1},{1,2},{2,3},{3,0},{4,5},{5,6},{6,7},{7,4},{8,9},{9,10},{10,1... | collective-permute-start | bytes 1572872 | tf_op jit(solution)/shard_map/ppermute | solution.py:24
  16.4 21.8 %collective-permute-start = (bf16[128,2048]{1,0:T(8,128)(2,1)S(1)}, bf16[128,2048]{1,0:T(8,128)(2,1)S(1)}, u32[]{:S(2)}, u32[]{:S(2)}) collective-permute-start(bf16[128,2048]{1,0:T(8,128)(2,1)S(1)} %copy-done.2), channel_id=1, source_target_pairs={{0,3},{1,0},{2,1},{3,2},{4,7},{5,4},{6,5},{7,6},{8,11},{9,8},{10,9... | collective-permute-start | bytes 1572872 | tf_op jit(solution)/shard_map/ppermute | solution.py:24
  70.8 372.9 %reduce-scatter.4.cloned.1.call-start = ((), (), s32[]{:S(2)}) async-start(), calls=%async_computation.5 | async-start | bytes 6127616
  77.3 36.6 %collective-permute-start.11 = (bf16[2048,1024]{1,0:T(8,128)(2,1)}, bf16[2048,1024]{1,0:T(8,128)(2,1)}, u32[]{:S(2)}, u32[]{:S(2)}) collective-permute-start(bf16[2048,1024]{1,0:T(8,128)(2,1)} %all-gather.4.cloned.1.call-done.own_ref), channel_id=1, source_target_pairs={{0,16},{16,0},{1,17},{17,1},{2,18},{18,2},{3,19},{19,3},{4,20},{20... | collective-permute-start | bytes 12582920 | tf_op jit(solution)/shard_map/ppermute | solution.py:28
  92.5 34.0 %collective-permute-start.26 = (bf16[4,352,256]{2,1,0:T(8,128)(2,1)S(1)}, bf16[4,352,256]{2,1,0:T(8,128)(2,1)S(1)}, u32[]{:S(2)}, u32[]{:S(2)}) collective-permute-start(bf16[4,352,256]{2,1,0:T(8,128)(2,1)S(1)} %pad_maximum_fusion.1.refs_12_.refs_0_), channel_id=1, source_target_pairs={{0,96},{32,0},{64,32},{96,64},{1,97},{33,1},{65,33},{97,65},{2,98}... | collective-permute-start | bytes 2162696 | tf_op jit(solution)/shard_map/ppermute | solution.py:24
  95.5 30.9 %collective-permute-start.27 = (bf16[4,352,256]{2,1,0:T(8,128)(2,1)S(1)}, bf16[4,352,256]{2,1,0:T(8,128)(2,1)S(1)}, u32[]{:S(2)}, u32[]{:S(2)}) collective-permute-start(bf16[4,352,256]{2,1,0:T(8,128)(2,1)S(1)} %pad_maximum_fusion.1.refs_12_.refs_0_), channel_id=1, source_target_pairs={{0,64},{32,96},{64,0},{96,32},{1,65},{33,97},{65,1},{97,33},{2,66}... | collective-permute-start | bytes 2162696 | tf_op jit(solution)/shard_map/ppermute | solution.py:24
  96.2 34.0 %collective-permute-start.28 = (bf16[4,352,256]{2,1,0:T(8,128)(2,1)S(1)}, bf16[4,352,256]{2,1,0:T(8,128)(2,1)}, u32[]{:S(2)}, u32[]{:S(2)}) collective-permute-start(bf16[4,352,256]{2,1,0:T(8,128)(2,1)S(1)} %pad_maximum_fusion.1.refs_12_.refs_0_), channel_id=1, source_target_pairs={{0,32},{32,64},{64,96},{96,0},{1,33},{33,65},{65,97},{97,1},{2,34}... | collective-permute-start | bytes 2162696 | tf_op jit(solution)/shard_map/ppermute | solution.py:24
  143.1 49.5 %collective-permute-start.29 = (bf16[4,704,1024]{2,1,0:T(8,128)(2,1)}, bf16[4,704,1024]{2,1,0:T(8,128)(2,1)}, u32[]{:S(2)}, u32[]{:S(2)}) collective-permute-start(bf16[4,704,1024]{2,1,0:T(8,128)(2,1)} %bitcast.100), channel_id=1, source_target_pairs={{0,16},{16,0},{1,17},{17,1},{2,18},{18,2},{3,19},{19,3},{4,20},{20... | collective-permute-start | bytes 17301512 | tf_op jit(solution)/shard_map/ppermute | solution.py:28
  290.5 32.6 %collective-permute-start.43 = (bf16[4,4,352,256]{3,2,1,0:T(8,128)(2,1)}, bf16[4,4,352,256]{3,2,1,0:T(8,128)(2,1)}, u32[]{:S(2)}, u32[]{:S(2)}) collective-permute-start(bf16[4,4,352,256]{3,2,1,0:T(8,128)(2,1)} %feed_grads.3), channel_id=1, source_target_pairs={{0,16},{16,0},{1,17},{17,1},{2,18},{18,2},{3,19},{19,3},{4,20},{20... | collective-permute-start | bytes 8650760 | tf_op jit(solution)/shard_map/ppermute | solution.py:28
  290.8 23.6 %collective-permute-start.45 = (bf16[128,2048]{1,0:T(8,128)(2,1)}, bf16[128,2048]{1,0:T(8,128)(2,1)}, u32[]{:S(2)}, u32[]{:S(2)}) collective-permute-start(bf16[128,2048]{1,0:T(8,128)(2,1)} %get-tuple-element.127.b0), channel_id=1, source_target_pairs={{0,1},{1,2},{2,3},{3,0},{4,5},{5,6},{6,7},{7,4},{8,9},{9,10},{10,1... | collective-permute-start | bytes 1572872 | tf_op jit(solution)/shard_map/ppermute | solution.py:24
  291.0 25.1 %collective-permute-start.44 = (bf16[128,2048]{1,0:T(8,128)(2,1)}, bf16[128,2048]{1,0:T(8,128)(2,1)}, u32[]{:S(2)}, u32[]{:S(2)}) collective-permute-start(bf16[128,2048]{1,0:T(8,128)(2,1)} %get-tuple-element.127.b0), channel_id=1, source_target_pairs={{0,3},{1,0},{2,1},{3,2},{4,7},{5,4},{6,5},{7,6},{8,11},{9,8},{10,9... | collective-permute-start | bytes 1572872 | tf_op jit(solution)/shard_map/ppermute | solution.py:24
  294.1 27.1 %collective-permute-start.38 = (bf16[64,2048]{1,0:T(8,128)(2,1)}, bf16[64,2048]{1,0:T(8,128)(2,1)}, u32[]{:S(2)}, u32[]{:S(2)}) collective-permute-start(bf16[64,2048]{1,0:T(8,128)(2,1)} %get-tuple-element.111), channel_id=1, source_target_pairs={{0,3},{1,0},{2,1},{3,2},{4,7},{5,4},{6,5},{7,6},{8,11},{9,8},{10,9... | collective-permute-start | bytes 786440 | tf_op jit(solution)/shard_map/ppermute | solution.py:24
  295.7 33.0 %all-to-all-start.1 = ((bf16[16,128,128]{2,1,0:T(8,128)(2,1)}), bf16[16,128,128]{2,1,0:T(8,128)(2,1)S(1)}, u32[]{:S(2)}, u32[]{:S(2)}) async-start(bf16[16,128,128]{2,1,0:T(8,128)(2,1)} %bitcast.93), calls=%async_computation.1 | async-start | bytes 1048576 | tf_op jit(solution)/shard_map/all_to_all | solution.py:686
  316.1 26.1 %collective-permute-start.46 = (bf16[64,2048]{1,0:T(8,128)(2,1)}, bf16[64,2048]{1,0:T(8,128)(2,1)}, u32[]{:S(2)}, u32[]{:S(2)}) collective-permute-start(bf16[64,2048]{1,0:T(8,128)(2,1)} %slice.131), channel_id=1, source_target_pairs={{0,1},{1,2},{2,3},{3,0},{4,5},{5,6},{6,7},{7,4},{8,9},{9,10},{10,1... | collective-permute-start | bytes 786440 | tf_op jit(solution)/shard_map/ppermute | solution.py:24
  317.8 24.5 %collective-permute-start.47 = (bf16[64,2048]{1,0:T(8,128)(2,1)}, bf16[64,2048]{1,0:T(8,128)(2,1)}, u32[]{:S(2)}, u32[]{:S(2)}) collective-permute-start(bf16[64,2048]{1,0:T(8,128)(2,1)} %slice.132), channel_id=1, source_target_pairs={{0,3},{1,0},{2,1},{3,2},{4,7},{5,4},{6,5},{7,6},{8,11},{9,8},{10,9... | collective-permute-start | bytes 786440 | tf_op jit(solution)/shard_map/ppermute | solution.py:24
  362.8 40.4 %collective-permute-start.55 = (bf16[4,4,288,256]{3,2,1,0:T(8,128)(2,1)}, bf16[4,4,288,256]{3,2,1,0:T(8,128)(2,1)}, u32[]{:S(2)}, u32[]{:S(2)}) collective-permute-start(bf16[4,4,288,256]{3,2,1,0:T(8,128)(2,1)} %get-tuple-element.142), channel_id=1, source_target_pairs={{0,16},{16,0},{1,17},{17,1},{2,18},{18,2},{3,19},{19,3},{4,20},{20... | collective-permute-start | bytes 7077896 | tf_op jit(solution)/shard_map/ppermute | solution.py:28
  363.6 20.2 %collective-permute-start.66 = (bf16[4,352,256]{2,1,0:T(8,128)(2,1)S(1)}, bf16[4,352,256]{2,1,0:T(8,128)(2,1)}, u32[]{:S(2)}, u32[]{:S(2)}) collective-permute-start(bf16[4,352,256]{2,1,0:T(8,128)(2,1)S(1)} %get-tuple-element.188), channel_id=1, source_target_pairs={{0,4},{4,8},{8,12},{12,0},{1,5},{5,9},{9,13},{13,1},{2,6},{6,10},{... | collective-permute-start | bytes 2162696 | tf_op jit(solution)/shard_map/ppermute | solution.py:24
  364.4 35.0 %collective-permute-start.67 = (bf16[4,352,256]{2,1,0:T(8,128)(2,1)S(1)}, bf16[4,352,256]{2,1,0:T(8,128)(2,1)}, u32[]{:S(2)}, u32[]{:S(2)}) collective-permute-start(bf16[4,352,256]{2,1,0:T(8,128)(2,1)S(1)} %get-tuple-element.190), channel_id=1, source_target_pairs={{0,8},{4,12},{8,0},{12,4},{1,9},{5,13},{9,1},{13,5},{2,10},{6,14},... | collective-permute-start | bytes 2162696 | tf_op jit(solution)/shard_map/ppermute | solution.py:24
  367.8 31.6 %collective-permute-start.68 = (bf16[4,352,256]{2,1,0:T(8,128)(2,1)S(1)}, bf16[4,352,256]{2,1,0:T(8,128)(2,1)}, u32[]{:S(2)}, u32[]{:S(2)}) collective-permute-start(bf16[4,352,256]{2,1,0:T(8,128)(2,1)S(1)} %get-tuple-element.189), channel_id=1, source_target_pairs={{0,12},{4,0},{8,4},{12,8},{1,13},{5,1},{9,5},{13,9},{2,14},{6,2},{... | collective-permute-start | bytes 2162696 | tf_op jit(solution)/shard_map/ppermute | solution.py:24
  406.9 30.1 %collective-permute-start.61 = (bf16[4,304,256]{2,1,0:T(8,128)(2,1)S(1)}, bf16[4,304,256]{2,1,0:T(8,128)(2,1)S(1)}, u32[]{:S(2)}, u32[]{:S(2)}) collective-permute-start(bf16[4,304,256]{2,1,0:T(8,128)(2,1)S(1)} %get-tuple-element.224), channel_id=1, source_target_pairs={{0,8},{4,12},{8,0},{12,4},{1,9},{5,13},{9,1},{13,5},{2,10},{6,14},... | collective-permute-start | bytes 1867784 | tf_op jit(solution)/shard_map/ppermute | solution.py:24
  410.1 27.0 %collective-permute-start.62 = (bf16[4,304,256]{2,1,0:T(8,128)(2,1)S(1)}, bf16[4,304,256]{2,1,0:T(8,128)(2,1)S(1)}, u32[]{:S(2)}, u32[]{:S(2)}) collective-permute-start(bf16[4,304,256]{2,1,0:T(8,128)(2,1)S(1)} %get-tuple-element.225), channel_id=1, source_target_pairs={{0,12},{4,0},{8,4},{12,8},{1,13},{5,1},{9,5},{13,9},{2,14},{6,2},{... | collective-permute-start | bytes 1867784 | tf_op jit(solution)/shard_map/ppermute | solution.py:24
  418.0 26.7 %collective-permute-start.37 = (bf16[128,2048]{1,0:T(8,128)(2,1)}, bf16[128,2048]{1,0:T(8,128)(2,1)}, u32[]{:S(2)}, u32[]{:S(2)}) collective-permute-start(bf16[128,2048]{1,0:T(8,128)(2,1)} %pad_maximum_fusion.4), channel_id=1, source_target_pairs={{0,1},{1,2},{2,3},{3,0},{4,5},{5,6},{6,7},{7,4},{8,9},{9,10},{10,1... | collective-permute-start | bytes 1572872 | tf_op jit(solution)/shard_map/ppermute | solution.py:24
  421.0 32.7 %collective-permute-start.39 = (bf16[128,2048]{1,0:T(8,128)(2,1)}, bf16[128,2048]{1,0:T(8,128)(2,1)}, u32[]{:S(2)}, u32[]{:S(2)}) collective-permute-start(bf16[128,2048]{1,0:T(8,128)(2,1)} %pad_maximum_fusion.5), channel_id=1, source_target_pairs={{0,3},{1,0},{2,1},{3,2},{4,7},{5,4},{6,5},{7,6},{8,11},{9,8},{10,9... | collective-permute-start | bytes 1572872 | tf_op jit(solution)/shard_map/ppermute | solution.py:24
  448.8 20.8 %collective-permute-start.72 = (bf16[1056,256]{1,0:T(8,128)(2,1)S(1)}, bf16[1056,256]{1,0:T(8,128)(2,1)S(1)}, u32[]{:S(2)}, u32[]{:S(2)}) collective-permute-start(bf16[1056,256]{1,0:T(8,128)(2,1)S(1)} %pad_maximum_fusion.3.refs_0_), channel_id=1, source_target_pairs={{0,96},{32,0},{64,32},{96,64},{1,97},{33,1},{65,33},{97,65},{2,98}... | collective-permute-start | bytes 1622024 | tf_op jit(solution)/shard_map/ppermute | solution.py:24
  453.8 21.1 %collective-permute-start.79 = (bf16[304,256]{1,0:T(8,128)(2,1)S(1)}, bf16[304,256]{1,0:T(8,128)(2,1)S(1)}, u32[]{:S(2)}, u32[]{:S(2)}) collective-permute-start(bf16[304,256]{1,0:T(8,128)(2,1)S(1)} %fusion.18.refs_0_), channel_id=1, source_target_pairs={{0,96},{32,0},{64,32},{96,64},{1,97},{33,1},{65,33},{97,65},{2,98}... | collective-permute-start | bytes 466952 | tf_op jit(solution)/shard_map/ppermute | solution.py:24
  458.1 32.1 %collective-permute-start.74 = (bf16[1056,256]{1,0:T(8,128)(2,1)S(1)}, bf16[1056,256]{1,0:T(8,128)(2,1)S(1)}, u32[]{:S(2)}, u32[]{:S(2)}) collective-permute-start(bf16[1056,256]{1,0:T(8,128)(2,1)S(1)} %pad_maximum_fusion.3.refs_0_), channel_id=1, source_target_pairs={{0,32},{32,64},{64,96},{96,0},{1,33},{33,65},{65,97},{97,1},{2,34}... | collective-permute-start | bytes 1622024 | tf_op jit(solution)/shard_map/ppermute | solution.py:24
  459.0 31.8 %collective-permute-start.75 = (bf16[1056,256]{1,0:T(8,128)(2,1)S(1)}, bf16[1056,256]{1,0:T(8,128)(2,1)S(1)}, u32[]{:S(2)}, u32[]{:S(2)}) collective-permute-start(bf16[1056,256]{1,0:T(8,128)(2,1)S(1)} %pad_maximum_fusion.3.refs_0_), channel_id=1, source_target_pairs={{0,16},{16,0},{1,17},{17,1},{2,18},{18,2},{3,19},{19,3},{4,20},{20... | collective-permute-start | bytes 1622024 | tf_op jit(solution)/shard_map/ppermute | solution.py:28
  469.5 21.3 %collective-permute-start.76 = (bf16[1056,256]{1,0:T(8,128)(2,1)S(1)}, bf16[1056,256]{1,0:T(8,128)(2,1)S(1)}, u32[]{:S(2)}, u32[]{:S(2)}) collective-permute-start(bf16[1056,256]{1,0:T(8,128)(2,1)S(1)} %collective-permute-done.72.refs_1_), channel_id=1, source_target_pairs={{0,16},{16,0},{1,17},{17,1},{2,18},{18,2},{3,19},{19,3},{4,20},{20... | collective-permute-start | bytes 1622024 | tf_op jit(solution)/shard_map/ppermute | solution.py:28
  469.5 21.7 %collective-permute-start.77 = (bf16[1056,256]{1,0:T(8,128)(2,1)S(1)}, bf16[1056,256]{1,0:T(8,128)(2,1)S(1)}, u32[]{:S(2)}, u32[]{:S(2)}) collective-permute-start(bf16[1056,256]{1,0:T(8,128)(2,1)S(1)} %collective-permute-done.73.refs_2_), channel_id=1, source_target_pairs={{0,16},{16,0},{1,17},{17,1},{2,18},{18,2},{3,19},{19,3},{4,20},{20... | collective-permute-start | bytes 1622024 | tf_op jit(solution)/shard_map/ppermute | solution.py:28
  (134 other events, 1598.6 us)
Sparse Core Ops, SparseCore 0:
  10.8 62.9 all-gather.3
  76.0 67.0 all-gather.5
  259.3 80.0 reduce-scatter.3

commit v2 on v1

v2 whole, which is shorter than its diff:
```python
import jax
import jax.numpy as jnp
from jax import lax
from jax.experimental import pallas as pl
from jax.experimental.pallas import tpu as pltpu
from jax.sharding import Mesh, PartitionSpec as P

FEAT = 16
HEAD_V = 128
EPS = 1e-05
F32 = jnp.float32
BF16 = jnp.bfloat16
TOK = 128
GROUP = 512
SEQ = 2048
HEAD_ROWS = 2 * FEAT + HEAD_V
AXES = ("x", "core", "z", "y")
D = 2048
HID = 352
PIECE = 256


def shifted(array, axis, by):
    return lax.ppermute(array, axis, [(i, (i + by) % 4) for i in range(4)])


def swapped(array):
    return lax.ppermute(array, "core", [(0, 1), (1, 0)])


def swapped_each(arrays):
    return [swapped(array) for array in arrays]


def gathered(array, axis):
    return [
        array,
        shifted(array, axis, 3),
        shifted(array, axis, 2),
        shifted(array, axis, 1),
    ]


def ring_gathered(array, axis):
    half = array.shape[0] // 2
    ahead, back = shifted(array, axis, 3), shifted(array, axis, 1)
    return [array, ahead, shifted(back[:half], axis, 1), shifted(ahead[half:], axis, 3), back]


def ring_start(opposite, axis):
    return shifted(opposite[0], axis, 1), shifted(opposite[1], axis, 3)


def ring_end(arrived, ahead, back, axis):
    half = ahead.shape[0] // 2
    first, second = arrived
    ahead = jnp.concatenate([ahead[:half] + first, ahead[half:]], axis=0)
    back = jnp.concatenate([back[:half], back[half:] + second], axis=0)
    return shifted(ahead, axis, 1), shifted(back, axis, 3)


def exchanged(blocks, axis):
    return [
        blocks[0],
        shifted(blocks[1], axis, 1),
        shifted(blocks[2], axis, 2),
        shifted(blocks[3], axis, 3),
    ]


def in_order(blocks, at):
    stacked = jnp.stack(blocks)
    return jnp.concatenate(
        [lax.dynamic_index_in_dim(stacked, (j - at) % 4, 0, keepdims=False) for j in range(4)], axis=0
    )


def nn(left, right):
    return jnp.dot(left, right, preferred_element_type=F32)


def nt(left, right):
    return lax.dot_general(left, right, (((1,), (1,)), ((), ())), preferred_element_type=F32)


def tn(left, right):
    return lax.dot_general(left, right, (((0,), (0,)), ((), ())), preferred_element_type=F32)


def pair_mask(start_row, si, ti, first, rows):
    row = lax.broadcasted_iota(jnp.int32, (rows, GROUP), 0) + (si * GROUP + first)
    mask = row >= start_row
    if si == ti:
        column = lax.broadcasted_iota(jnp.int32, (rows, GROUP), 1) + ti * GROUP
        mask = mask & (row <= column)
    return mask


def forward_kernel(
    at_ref,
    q0,
    q1,
    q2,
    q3,
    start_ref,
    m0,
    m1,
    m2,
    m3,
    numer_ref,
    denom_ref,
    qkv_ref,
    mixed_ref,
    keys,
):
    for d, ref in enumerate((q0, q1, q2, q3)):
        qkv_ref[(at_ref[2] + 4 - d) % 4] = ref[...]
    for si in range(4):
        keys[si] = jnp.transpose(qkv_ref[si, FEAT : 2 * FEAT, :].astype(F32)).astype(BF16)
    for ti in range(4):
        query = (qkv_ref[ti, 0:FEAT, :].astype(F32) * (FEAT**-0.5)).astype(BF16)
        start_row = start_ref[:, ti * GROUP : (ti + 1) * GROUP]
        numer = jnp.zeros((HEAD_V, GROUP), F32)
        denom = jnp.zeros((1, GROUP), F32)
        for si in range(ti + 1):
            one = nn(keys[si], query) + 1.0
            weight = jnp.where(
                pair_mask(start_row, si, ti, 0, GROUP), 0.5 * (one * one) + 0.5, 0.0
            )
            denom = denom + jnp.sum(weight, axis=0, keepdims=True)
            numer = numer + nn(qkv_ref[si, 2 * FEAT :, :], weight.astype(BF16))
        numer_ref[ti] = numer
        denom_ref[ti] = denom
        mixed_ref[ti] = (numer / denom).astype(BF16)
    for d, ref in enumerate((m0, m1, m2, m3)):
        ref[...] = mixed_ref[(at_ref[2] + d) % 4]


def attention_forward(order, at, qkv, start_row, wait):
    return order.call(
        forward_kernel,
        "attention_forward",
        (like(HEAD_V, GROUP),) * 4
        + (
            like(4, HEAD_V, GROUP, dtype=F32),
            like(4, 1, GROUP, dtype=F32),
            like(4, HEAD_ROWS, GROUP),
        ),
        (at, *qkv, start_row),
        [pltpu.VMEM((4, HEAD_V, GROUP), BF16), pltpu.VMEM((4, GROUP, FEAT), BF16)],
        wait,
        in_specs=[SMEM] + [WHOLE] * 5,
        out_specs=(WHOLE,) * 7,
    )


def backward_kernel(
    at_ref,
    c0,
    c1,
    c2,
    c3,
    qkv_ref,
    numer_ref,
    denom_ref,
    start_ref,
    g0,
    g1,
    g2,
    g3,
    out_ref,
    cot_ref,
    keys,
    values,
    key_sum,
    value_sum,
):
    for d, ref in enumerate((c0, c1, c2, c3)):
        cot_ref[(at_ref[2] + 4 - d) % 4] = ref[...]
    for si in range(4):
        keys[si] = jnp.transpose(qkv_ref[si, FEAT : 2 * FEAT, :].astype(F32)).astype(BF16)
        values[si] = jnp.transpose(qkv_ref[si, 2 * FEAT :, :].astype(F32)).astype(BF16)
    key_sum[...] = jnp.zeros_like(key_sum)
    value_sum[...] = jnp.zeros_like(value_sum)
    for ti in range(4):
        query_f32 = qkv_ref[ti, 0:FEAT, :].astype(F32) * (FEAT**-0.5)
        query = query_f32.astype(BF16)
        query_rows = jnp.transpose(query_f32).astype(BF16)
        start_row = start_ref[:, ti * GROUP : (ti + 1) * GROUP]
        inverse = 1.0 / denom_ref[ti]
        cot = cot_ref[ti].astype(F32)
        cot_denom = -jnp.sum(cot * numer_ref[ti], axis=0, keepdims=True) * (inverse * inverse)
        cot_f32 = cot * inverse
        cot_numer = cot_f32.astype(BF16)
        cot_rows = jnp.transpose(cot_f32).astype(BF16)
        query_sum = jnp.zeros((FEAT, GROUP), F32)
        for si in range(ti + 1):
            one = nn(keys[si], query) + 1.0
            mask = pair_mask(start_row, si, ti, 0, GROUP)
            weight = jnp.where(mask, 0.5 * (one * one) + 0.5, 0.0).astype(BF16)
            value_sum[si] += nn(weight, cot_rows)
            cot_weight = nn(values[si], cot_numer) + cot_denom
            cot_score = jnp.where(mask, cot_weight * one, 0.0).astype(BF16)
            key_sum[si] += nn(cot_score, query_rows)
            query_sum = query_sum + nn(qkv_ref[si, FEAT : 2 * FEAT, :], cot_score)
        out_ref[ti, 0:FEAT, :] = (query_sum * (FEAT**-0.5)).astype(BF16)
    for si in range(4):
        out_ref[si, FEAT : 2 * FEAT, :] = jnp.transpose(key_sum[si]).astype(BF16)
        out_ref[si, 2 * FEAT :, :] = jnp.transpose(value_sum[si]).astype(BF16)
    for d, ref in enumerate((g0, g1, g2, g3)):
        ref[...] = out_ref[(at_ref[2] + d) % 4]


def attention_backward(order, at, qkv, cot, numer, denom, start_row, wait):
    return order.call(
        backward_kernel,
        "attention_backward",
        (like(HEAD_ROWS, GROUP),) * 4,
        (at, *cot, qkv, numer, denom, start_row),
        [
            pltpu.VMEM((4, HEAD_ROWS, GROUP), BF16),
            pltpu.VMEM((4, HEAD_V, GROUP), BF16),
            pltpu.VMEM((4, GROUP, FEAT), BF16),
            pltpu.VMEM((4, GROUP, HEAD_V), BF16),
            pltpu.VMEM((4, GROUP, FEAT), F32),
            pltpu.VMEM((4, GROUP, HEAD_V), F32),
        ],
        wait,
        in_specs=[SMEM] + [WHOLE] * 8,
        out_specs=(WHOLE,) * 4,
    )


VMEM_LIMIT = 52 * 2**20


class Order:
    def __init__(self):
        self.last = ()

    def call(self, kernel, name, out_shape, args, scratch=(), wait=(), **specs):
        at, first, *rest = args
        first = lax.optimization_barrier((first, *self.last, *wait))[0]
        if "grid_spec" not in specs:
            specs["scratch_shapes"] = list(scratch)
        out = pl.pallas_call(
            kernel,
            out_shape=out_shape,
            compiler_params=pltpu.CompilerParams(vmem_limit_bytes=VMEM_LIMIT),
            cost_estimate=pl.CostEstimate(flops=1, bytes_accessed=1, transcendentals=0),
            name=name,
            **specs,
        )(at, first, *rest)
        self.last = (out[0] if isinstance(out, (tuple, list)) else out,)
        return out


SMEM = pl.BlockSpec(memory_space=pltpu.SMEM)
WHOLE = pl.BlockSpec(memory_space=pltpu.VMEM)


def spec(*shape, at=None):
    def index(i):
        return tuple(i if k == at else 0 for k in range(len(shape)))

    return pl.BlockSpec(shape, index)


def like(*shape, dtype=BF16):
    return jax.ShapeDtypeStruct(shape, dtype)


def piece_at(at_ref, place, own_core):
    core = at_ref[1] if own_core else 1 - at_ref[1]
    return pl.multiple_of(((at_ref[0] + place) % 4 * 2 + core) * PIECE, PIECE)


def inverse_rms(rows):
    return lax.rsqrt(jnp.mean(rows * rows, axis=1, keepdims=True) + EPS)


def norm_back(grad_normed, unit, inverse, gains):
    scaled = grad_normed * gains
    return inverse * (scaled - unit * jnp.mean(scaled * unit, axis=1, keepdims=True))


RING_ROWS = ((0, 0, TOK), (1, 0, TOK), (2, 0, TOK // 2), (2, TOK // 2, TOK // 2), (3, 0, TOK))


HALF_ROWS = (HEAD_ROWS + HEAD_V // 2) // 2


def project_kernel(at_ref, *refs):
    tokens, weights, gain_ref = refs[:5], refs[5:10], refs[10]
    outs, normed_ref = refs[11:15], refs[15]
    for token_ref, (d, first, count) in zip(tokens, RING_ROWS):
        rows = token_ref[...].astype(F32)
        normed = (rows * inverse_rms(rows) * gain_ref[...]).astype(BF16)
        at = pl.multiple_of((at_ref[3] + d) % 4 * TOK, TOK) + first
        normed_ref[pl.ds(pl.multiple_of(at, count), count), :] = normed
    normed = normed_ref[...]
    for d, w_ref in ((0, weights[0]), (1, weights[1]), (3, weights[4])):
        outs[d][...] = nt(w_ref[:HEAD_ROWS, :], normed).astype(BF16)
    outs[2][:HALF_ROWS, :] = nt(weights[2][...], normed).astype(BF16)
    outs[2][HALF_ROWS:, :] = nt(weights[3][: HEAD_ROWS - HALF_ROWS, :], normed).astype(BF16)


def project(order, at, token_blocks, head_blocks, gain, wait):
    return order.call(
        project_kernel,
        "project",
        (like(HEAD_ROWS, GROUP),) * 4 + (like(GROUP, D),),
        (at, *token_blocks, *head_blocks, gain[None, :]),
        wait=wait,
        in_specs=[SMEM] + [WHOLE] * 11,
        out_specs=(WHOLE,) * 5,
    )


def half_at(at_ref, own):
    core = at_ref[1] if own else 1 - at_ref[1]
    return pl.ds(pl.multiple_of(core * 1024, 1024), 1024)


RING_LIKE = tuple(like(count, D) for _, _, count in RING_ROWS)


def at_place(at_ref, d):
    return pl.ds(pl.multiple_of((at_ref[3] + d) % 4 * TOK, TOK), TOK)


def out_kernel(at_ref, m0, m1, m2, m3, own_ref, other_ref, *refs):
    outs, (mixed, rows, weights) = refs[:5], refs[5:]
    for d, mixed_ref in enumerate((m0, m3, m2, m1)):
        mixed[:, d * HEAD_V : (d + 1) * HEAD_V] = jnp.transpose(mixed_ref[...].astype(F32)).astype(
            BF16
        )
        head_weights(at_ref, own_ref, other_ref, weights, d)
    rows[...] = nn(mixed[...], weights[...]).astype(BF16)
    for out_ref, (d, first, count) in zip(outs, RING_ROWS):
        at = pl.multiple_of((at_ref[3] + d) % 4 * TOK + first, count)
        out_ref[...] = rows[pl.ds(at, count), :]


def head_weights(at_ref, own_ref, other_ref, weights, d):
    half = HEAD_V // 2
    for core, w_ref in ((at_ref[1], own_ref), (1 - at_ref[1], other_ref)):
        first = pl.multiple_of(d * HEAD_V + core * half, half)
        weights[pl.ds(first, half), :] = w_ref[d]


def out_projection(order, at, mixed, weights, wait):
    return order.call(
        out_kernel,
        "out_projection",
        RING_LIKE,
        (at, *mixed, *weights),
        [
            pltpu.VMEM((GROUP, GROUP), BF16),
            pltpu.VMEM((GROUP, D), BF16),
            pltpu.VMEM((GROUP, D), BF16),
        ],
        wait,
        in_specs=[SMEM] + [WHOLE] * 6,
        out_specs=(WHOLE,) * 5,
    )


def middle_kernel(at_ref, p0, p1, p3, token_ref, gain_ref, mid_ref, normed_ref):
    branch = p0[...].astype(F32) + p1[...].astype(F32) + p3[...].astype(F32)
    mid = token_ref[...].astype(F32) + branch
    mid_ref[...] = mid
    normed_ref[...] = (mid * inverse_rms(mid) * gain_ref[...]).astype(BF16)


def middle(order, at, parts, tokens, gain, wait):
    return order.call(
        middle_kernel,
        "middle",
        (like(TOK, D, dtype=F32), like(TOK, D)),
        (at, *parts, tokens, gain[None, :]),
        wait=wait,
        in_specs=[SMEM] + [WHOLE] * 5,
        out_specs=(WHOLE, WHOLE),
    )


RING = ((0, TOK), (TOK, TOK), (2 * TOK, TOK // 2), (2 * TOK + TOK // 2, TOK // 2), (3 * TOK, TOK))
RING_SPECS = [spec(count, D) for _, count in RING]


def feed_kernel(at_ref, *refs):
    blocks, cot_refs, weight_refs = refs[:5], refs[5:10], refs[10:12]
    (hidden_ref, gate_ref, up_ref), outs = refs[12:15], refs[15:20]
    rows, cots, weights, downs, total, gate_up_sems, down_sems = refs[20:]

    def gate_up_copy(z, own):
        return pltpu.make_async_copy(
            weight_refs[own].at[z, pl.ds(0, 2 * HID)], weights.at[z, own], gate_up_sems.at[z, own]
        )

    def down_copy(z, own):
        return pltpu.make_async_copy(
            weight_refs[own].at[z, pl.ds(2 * HID, HID)],
            downs.at[z, :, pl.ds(own * 1024, 1024)],
            down_sems.at[z, own],
        )

    for z in range(4):
        for own in (0, 1):
            gate_up_copy(z, own).start()
            down_copy(z, own).start()
    for (first, count), block, cot_ref in zip(RING, blocks, cot_refs):
        at = slice(first, first + count)
        for own in (0, 1):
            rows[own, at, :] = block[:, half_at(at_ref, own == 0)]
            cots[at, own * 1024 : (own + 1) * 1024] = cot_ref[:, half_at(at_ref, own == 0)]
    for z in range(4):
        for own in (0, 1):
            gate_up_copy(z, own).wait()
            down_copy(z, own).wait()
        both_rows = nt(weights[z, 0], rows[0]) + nt(weights[z, 1], rows[1])
        gate_rows, up_rows = both_rows[:HID], both_rows[HID:]
        grad_hidden = nt(downs[z], cots[...])
        sigmoid_gate = 1.0 / (1.0 + jnp.exp(-gate_rows))
        silu_gate = gate_rows * sigmoid_gate
        hidden_ref[z] = (silu_gate * up_rows).astype(BF16)
        up_delta = (grad_hidden * silu_gate).astype(BF16)
        gate_delta = (
            grad_hidden * up_rows * (sigmoid_gate + silu_gate * (1.0 - sigmoid_gate))
        ).astype(BF16)
        gate_ref[z] = gate_delta
        up_ref[z] = up_delta
        both_delta = jnp.concatenate([gate_delta, up_delta], axis=0)
        for own in (0, 1):
            part = tn(both_delta, weights[z, own])
            if z == 0:
                total[own] = part
            elif z < 3:
                total[own] += part
            else:
                part = (part + total[own]).astype(BF16)
                for (first, count), out_ref in zip(RING, outs):
                    out_ref[:, half_at(at_ref, own == 0)] = part[first : first + count]


def feed(order, at, second_blocks, cot_blocks, weights):
    deltas = like(4, HID, GROUP)
    return order.call(
        feed_kernel,
        "feed",
        (deltas, deltas, deltas) + RING_LIKE,
        (at, *second_blocks, *cot_blocks, *weights),
        [
            pltpu.VMEM((2, GROUP, 1024), BF16),
            pltpu.VMEM((GROUP, D), BF16),
            pltpu.VMEM((4, 2, 2 * HID, 1024), BF16),
            pltpu.VMEM((4, HID, D), BF16),
            pltpu.VMEM((2, GROUP, 1024), F32),
            pltpu.SemaphoreType.DMA((4, 2)),
            pltpu.SemaphoreType.DMA((4, 2)),
        ],
        in_specs=[SMEM] + [WHOLE] * 10 + [pl.BlockSpec(memory_space=pl.ANY)] * 2,
        out_specs=(WHOLE,) * 8,
    )


def down_kernel(at_ref, hidden_ref, own_ref, other_ref, *refs):
    out_ref, rows, downs, sems = refs

    def copy(own):
        weight_ref = own_ref if own == 0 else other_ref
        return pltpu.make_async_copy(
            weight_ref.at[:, pl.ds(2 * HID, HID)], downs.at[own], sems.at[own]
        )

    copy(0).start()
    copy(1).start()
    for z in range(4):
        rows[z] = jnp.transpose(hidden_ref[z].astype(F32)).astype(BF16)
    for own in (0, 1):
        copy(own).wait()
        part = nn(rows[0], downs[own, 0])
        for z in range(1, 4):
            part = part + nn(rows[z], downs[own, z])
        part = part.astype(BF16)
        for b in range(4):
            block = part[b * TOK : (b + 1) * TOK]
            out_ref[(at_ref[3] + b) % 4, :, half_at(at_ref, own == 0)] = block


def down(order, at, hidden, weights, wait):
    return order.call(
        down_kernel,
        "down",
        like(4, TOK, D),
        (at, hidden, *weights),
        [
            pltpu.VMEM((4, GROUP, HID), BF16),
            pltpu.VMEM((2, 4, HID, 1024), BF16),
            pltpu.SemaphoreType.DMA((2,)),
        ],
        wait,
        in_specs=[SMEM, WHOLE] + [pl.BlockSpec(memory_space=pl.ANY)] * 2,
        out_specs=WHOLE,
    )


def feed_grads_kernel(own, count, at_ref, *refs):
    lefts, blocks, rows = refs[:count], refs[count : count + 5], refs[-1]
    others, out_ref = refs[count + 5 : -2], refs[-2]
    step = pl.program_id(0)

    @pl.when(step == 0)
    def _():
        core = at_ref[1] if own else 1 - at_ref[1]
        for (first, size), block in zip(RING, blocks):
            for k in range(4):
                columns = pl.ds(pl.multiple_of((k * 2 + core) * PIECE, PIECE), PIECE)
                rows[first : first + size, k * PIECE : (k + 1) * PIECE] = block[:, columns]

    for i, left_ref in enumerate(lefts):
        part = nn(left_ref[0], rows[...])
        at = slice(i * HID, (i + 1) * HID)
        for k in range(4):
            block = part[:, k * PIECE : (k + 1) * PIECE]
            if own:
                block = block + others[0][k, 0, at, :].astype(F32)
            out_ref[k, 0, at, :] = block.astype(BF16)


def feed_grads(order, at, lefts, blocks, ahead, other=(), wait=()):
    own, count = bool(other), len(lefts)
    rows = count * HID

    def place(i, at_ref):
        return (i + 4 - at_ref[2]) % 4 if ahead else i

    grads = pl.BlockSpec((4, 1, rows, PIECE), lambda i, at_ref: (0, place(i, at_ref), 0, 0))
    return order.call(
        lambda *refs: feed_grads_kernel(own, count, *refs),
        "feed_grads_own" if own else "feed_grads",
        (like(4, 4, rows, PIECE),),
        (at, *lefts, *blocks, *other),
        wait=wait,
        grid_spec=pltpu.PrefetchScalarGridSpec(
            num_scalar_prefetch=1,
            grid=(4,),
            in_specs=[pl.BlockSpec((1, HID, GROUP), lambda i, at_ref: (i, 0, 0))] * count
            + [pl.BlockSpec((size, D), lambda i, at_ref: (0, 0)) for _, size in RING]
            + ([grads] if own else []),
            out_specs=(grads,),
            scratch_shapes=[pltpu.VMEM((GROUP, 1024), BF16)],
        ),
    )


def turn_kernel(
    at_ref, s0, s1, s3, mid_ref, cot_ref, gain_ref, branch_ref, grad_mid_ref, gain_part_ref
):
    grad_second = s0[...].astype(F32) + s1[...].astype(F32) + s3[...].astype(F32)
    mid = mid_ref[...]
    inverse = inverse_rms(mid)
    unit = mid * inverse
    gain_part_ref[...] = jnp.sum(grad_second * unit, axis=0, keepdims=True)
    grad_mid = cot_ref[...].astype(F32) + norm_back(grad_second, unit, inverse, gain_ref[...])
    grad_mid_ref[...] = grad_mid
    branch_ref[...] = grad_mid.astype(BF16)


def turn(order, at, second_sums, mid_rows, out_grad, gain):
    return order.call(
        turn_kernel,
        "turn",
        (like(TOK, D), like(TOK, D, dtype=F32), like(1, D, dtype=F32)),
        (at, *second_sums, mid_rows, out_grad, gain[None, :]),
        in_specs=[SMEM] + [WHOLE] * 6,
        out_specs=(WHOLE,) * 3,
    )


def back_kernel(at_ref, b0, b1, b2a, b2b, b3, own_ref, other_ref, *refs):
    outs, rows_ref, weights = refs[:4], refs[4], refs[5]
    for block_ref, (d, first, count) in zip((b0, b1, b2a, b2b, b3), RING_ROWS):
        at = pl.ds(pl.multiple_of((at_ref[3] + d) % 4 * TOK + first, count), count)
        rows_ref[at, :] = block_ref[...]
    for d in range(4):
        head_weights(at_ref, own_ref, other_ref, weights, d)
    total = nt(weights[...], rows_ref[...]).astype(BF16)
    for d, out_ref in enumerate(outs):
        out_ref[...] = total[d * HEAD_V : (d + 1) * HEAD_V, :]


def back_projection(order, at, branch_blocks, weights):
    return order.call(
        back_kernel,
        "back_projection",
        (like(HEAD_V, GROUP),) * 4 + (like(GROUP, D),),
        (at, *branch_blocks, *weights),
        [pltpu.VMEM((GROUP, D), BF16)],
        in_specs=[SMEM] + [WHOLE] * 7,
        out_specs=(WHOLE,) * 5,
    )


def own_first(at_ref, out, block, rows):
    for own in (0, 1):
        for k in range(4):
            columns = pl.ds(piece_at(at_ref, k, own == 0), PIECE)
            piece = own * 4 + k
            out[rows, piece * PIECE : (piece + 1) * PIECE] = block[:, columns]


def out_grads_kernel(at_ref, m0, m1, m2, m3, branch_ref, out_ref, rows):
    own_first(at_ref, rows, branch_ref, slice(0, GROUP))
    for back, mixed_ref in enumerate((m0, m1, m2, m3)):
        out_ref[(4 - back) % 4] = nn(mixed_ref[...], rows[...]).astype(BF16)


def out_grads(order, at, mixed, branch_rows):
    return order.call(
        out_grads_kernel,
        "out_grads",
        like(4, HEAD_V, D),
        (at, *mixed, branch_rows),
        [pltpu.VMEM((GROUP, D), BF16)],
        in_specs=[SMEM] + [WHOLE] * 5,
        out_specs=WHOLE,
    )


BOTH_ROWS = HEAD_V + HEAD_ROWS + 16


def head_grads_kernel(at_ref, *refs):
    (g0, g1, g2, g3), weights, normed_ref, gain_ref = refs[:4], refs[4:9], refs[9], refs[10]
    out_grad_ref, second_ref, own_ref, other_ref, rows = refs[11:]
    own_first(at_ref, rows, normed_ref, slice(0, GROUP))
    rest = HEAD_ROWS - HALF_ROWS
    places = (
        (g0, ((weights[0], HEAD_ROWS),)),
        (g3, ((weights[1], HEAD_ROWS),)),
        (g2, ((weights[2], HALF_ROWS), (weights[3], rest))),
        (g1, ((weights[4], HEAD_ROWS),)),
    )
    for own in (0, 1):
        sent_ref = own_ref if own == 0 else other_ref
        for k in range(4):
            columns = pl.ds(piece_at(at_ref, k, own == 0), PIECE)
            piece = slice((own * 4 + k) * PIECE, (own * 4 + k + 1) * PIECE)
            gain_part = jnp.zeros((1, PIECE), F32)
            for d, (grads_ref, w_refs) in enumerate(places):
                part = nn(grads_ref[...], rows[:, piece])
                first = 0
                for w_ref, count in w_refs:
                    weighted = part[first : first + count] * w_ref[:count, columns].astype(F32)
                    gain_part = gain_part + jnp.sum(weighted, axis=0, keepdims=True)
                    first += count
                sent_ref[d, k, :HEAD_V] = out_grad_ref[d, :, piece]
                sent_ref[d, k, HEAD_V : HEAD_V + HEAD_ROWS] = part.astype(BF16)
            gain_part = gain_part / gain_ref[:, columns]
            gain_rows = jnp.where(
                lax.broadcasted_iota(jnp.int32, (16, PIECE), 0) == 0,
                gain_part,
                second_ref[:, columns],
            ).astype(BF16)
            for d in range(4):
                sent_ref[d, k, HEAD_V + HEAD_ROWS :] = gain_rows


def head_grads(order, at, grads, head_blocks, normed, gain, out_part, second_part, wait):
    both = like(4, 4, BOTH_ROWS, PIECE)
    return order.call(
        head_grads_kernel,
        "head_grads",
        (both, both),
        (at, *grads, *head_blocks, normed, gain[None, :], out_part, second_part),
        [pltpu.VMEM((GROUP, D), BF16)],
        wait,
        in_specs=[SMEM] + [WHOLE] * 13,
        out_specs=(WHOLE,) * 2,
    )


def add_kernel(at_ref, mine_ref, other_ref, *outs):
    for d, out_ref in enumerate(outs):
        out_ref[...] = (mine_ref[d].astype(F32) + other_ref[d].astype(F32)).astype(BF16)


def add_blocks(order, at, mine, other):
    return order.call(
        add_kernel,
        "add_blocks",
        (like(4, BOTH_ROWS, PIECE),) * 4,
        (at, mine, other),
        in_specs=[SMEM] + [WHOLE] * 2,
        out_specs=(WHOLE,) * 4,
    )


def first_kernel(at_ref, *refs):
    grads, (w0, w1, w2a, w2b, w3), outs = refs[:4], refs[4:9], refs[9:14]
    rest = HEAD_ROWS - HALF_ROWS
    for d in range(4):
        columns = at_place(at_ref, d)
        part = tn(grads[0][:, columns], w0[:HEAD_ROWS, :])
        part = part + tn(grads[3][:, columns], w1[:HEAD_ROWS, :])
        part = part + tn(grads[1][:, columns], w3[:HEAD_ROWS, :])
        part = part + tn(grads[2][:HALF_ROWS, columns], w2a[...])
        part = (part + tn(grads[2][HALF_ROWS:, columns], w2b[:rest, :])).astype(BF16)
        for out_ref, (place, first, count) in zip(outs, RING_ROWS):
            if place == d:
                out_ref[...] = part[first : first + count]


def first_part(order, at, grads, head_blocks, wait):
    return order.call(
        first_kernel,
        "first_part",
        RING_LIKE,
        (at, *grads, *head_blocks),
        wait=wait,
        in_specs=[SMEM] + [WHOLE] * 9,
        out_specs=(WHOLE,) * 5,
    )


def collect_kernel(turned, at_ref, *refs):
    outs = refs[5:]
    for own in (True, False):
        for d in range(4):
            columns = pl.ds(piece_at(at_ref, d, own), PIECE)
            first = 0
            for i, out_ref in enumerate(outs):
                rows = out_ref.shape[1 if i == turned else 0]
                at = slice(first, first - (-rows // 16 * 16))
                block = (refs[d][at, :] if own else refs[4][d, at, :]).astype(F32)[:rows]
                if i == turned:
                    out_ref[columns, :] = jnp.transpose(block)
                else:
                    out_ref[:, columns] = block
                first += -rows // 16 * -16


def collect(order, at, mine, name, *rows, turned=None):
    other = swapped(jnp.stack(mine))
    return order.call(
        lambda *refs: collect_kernel(turned, *refs),
        name,
        tuple(
            like(D, r, dtype=F32) if i == turned else like(r, D, dtype=F32)
            for i, r in enumerate(rows)
        ),
        (at, *mine, other),
        in_specs=[SMEM] + [WHOLE] * 5,
        out_specs=(WHOLE,) * len(rows),
    )


def after(array, *needed):
    return lax.optimization_barrier((array, *needed))[0]


def body(
    tokens,
    doc_start,
    gain_first,
    w_query,
    w_key,
    w_value,
    w_out,
    gain_second,
    w_gate,
    w_up,
    w_down,
    out_grad,
):
    order = Order()
    at = jnp.stack([lax.axis_index(a) for a in AXES]).astype(jnp.int32)
    x_at, core, z_at, y_at = (at[i] for i in range(4))

    token_blocks = ring_gathered(tokens, "y")
    out_half = lax.dynamic_slice_in_dim(w_out, core * (HEAD_V // 2), HEAD_V // 2, 0)
    w_head = jnp.concatenate([w_query.T, w_key.T, w_value.T, out_half], axis=0)
    head_blocks = ring_gathered(w_head, "z")
    feed_half = jnp.concatenate([w_gate.T, w_up.T, w_down], axis=0)
    feed_half = lax.dynamic_slice_in_dim(feed_half, core * 1024, 1024, 1)
    *qkv, group_normed = project(order, at, token_blocks, head_blocks, gain_first, ())
    feed_mine = lax.all_gather(after(feed_half, group_normed), "z", axis=0)
    qkv = exchanged(qkv, "z")
    out_mine = jnp.stack([block[-(HEAD_V // 2) :] for block in (*head_blocks[:2], *head_blocks[3:])])
    out_mine = after(out_mine, *qkv)
    out_weights = (out_mine, swapped(out_mine))
    cot_blocks = gathered(after(out_grad, *qkv), "y")

    positions = jnp.arange(SEQ, dtype=jnp.int32)
    start_row = lax.cummax(jnp.where(doc_start != 0, positions, 0))[None, :]
    *mixed, numer, denom, qkv = attention_forward(order, at, qkv, start_row, ())
    mixed = exchanged(mixed, "z")
    p0, p1, *p2, p3 = out_projection(order, at, mixed, out_weights, ())
    parts = (p0, *ring_end(ring_start(p2, "y"), p1, p3, "y"))
    mid_rows, second_normed = middle(order, at, parts, tokens, gain_second, cot_blocks)

    cot_blocks = [*cot_blocks[:2], cot_blocks[2][:64], cot_blocks[2][64:], cot_blocks[3]]
    second_blocks = ring_gathered(second_normed, "y")
    feed_mine = after(feed_mine, second_blocks[1], second_blocks[4])
    feed_weights = (feed_mine, swapped(feed_mine))
    hidden, gate_delta, up_delta, s0, s1, *s2, s3 = feed(
        order, at, second_blocks, cot_blocks, feed_weights
    )
    arrived = ring_start(s2, "y")
    second_sums = (s0, *ring_end(arrived, s1, s3, "y"))
    deltas = (gate_delta, up_delta)
    (gu_grads,) = feed_grads(order, at, deltas, second_blocks, False, wait=arrived)
    gu_grads = swapped(gu_grads)
    (down_grads,) = feed_grads(order, at, (hidden,), cot_blocks, True)
    down_grads = swapped(down_grads)

    grad_branch, grad_mid, gain_second_part = turn(
        order, at, second_sums, mid_rows, out_grad, gain_second
    )
    branch_blocks = ring_gathered(grad_branch, "y")
    (gu_grads,) = feed_grads(
        order,
        at,
        deltas,
        second_blocks,
        False,
        (gu_grads,),
        wait=(branch_blocks[1], branch_blocks[4]),
    )
    gu_sum = lax.psum_scatter(
        gu_grads.reshape(16, 2 * HID, PIECE), ("x", "z"), scatter_dimension=0
    )
    b_parts = down(order, at, hidden, feed_weights, ())
    *grad_mixed, branch_rows = back_projection(order, at, branch_blocks, out_weights)
    grad_mixed = exchanged(grad_mixed, "z")
    b_parts = lax.all_to_all(after(b_parts, branch_rows), "y", 0, 0)
    (down_grads,) = feed_grads(order, at, (hidden,), cot_blocks, True, (down_grads,))
    out_part = out_grads(order, at, mixed, branch_rows)
    grads = attention_backward(order, at, qkv, grad_mixed, numer, denom, start_row, ())
    grads = exchanged(grads, "z")

    def added(blocks):
        total = (blocks[0].astype(F32) + blocks[1].astype(F32)) + (
            blocks[2].astype(F32) + blocks[3].astype(F32)
        )
        return total.astype(BF16)

    mine, other = head_grads(
        order,
        at,
        grads,
        head_blocks,
        group_normed,
        gain_first,
        out_part,
        gain_second_part,
        (b_parts,),
    )
    down_grads = lax.all_to_all(after(down_grads, b_parts), "x", 0, 0)
    other = swapped(other)
    f0, f1, *f2, f3 = first_part(order, at, grads, head_blocks, ())
    head_part = added(exchanged(add_blocks(order, at, mine, other), "z"))
    from_back, from_ahead = ring_end(ring_start(f2, "y"), f1, f3, "y")
    head_sum = added(exchanged([head_part[d] for d in range(4)], "x"))
    down_part = jnp.sum(after(down_grads, head_part).astype(F32), axis=0).astype(BF16)
    down_sum = added(exchanged([down_part[d] for d in range(4)], "z"))
    grad_first = f0.astype(F32) + from_back.astype(F32) + from_ahead.astype(F32)
    block_out = mid_rows + jnp.sum(b_parts.astype(F32), axis=0)
    x_rows = tokens.astype(F32)
    first_inv = inverse_rms(x_rows)
    input_grad = grad_mid + norm_back(grad_first, x_rows * first_inv, first_inv, gain_first)

    grad_out, grad_query, grad_key, grad_value, gains = collect(
        order,
        at,
        gathered(head_sum, "x"),
        "collect_heads",
        HEAD_V,
        FEAT,
        FEAT,
        HEAD_V,
        2,
        turned=3,
    )
    gains = gathered(gains, "y")
    gains = (gains[0] + gains[1]) + (gains[2] + gains[3])
    ffn_sum = jnp.concatenate([gu_sum, down_sum], axis=0)
    grad_gate, grad_up, grad_down = collect(
        order, at, gathered(ffn_sum, "x"), "collect_feed", HID, HID, HID
    )
    return (
        block_out,
        input_grad,
        gains[0],
        grad_query.T,
        grad_key.T,
        grad_value,
        grad_out,
        gains[1],
        grad_gate.T,
        grad_up.T,
        grad_down,
    )


def solution(mesh):
    fine = Mesh(mesh.devices.reshape(4, 2, 4, 4), AXES)
    rows, dp, mp = P(AXES, None), P(("x", "core")), ("z", "y")
    return jax.shard_map(
        body,
        mesh=fine,
        in_specs=(
            rows,
            dp,
            P(),
            P(None, mp),
            P(None, mp),
            P(None, mp),
            P(mp, None),
            P(),
            P(None, mp),
            P(None, mp),
            P(mp, None),
            rows,
        ),
        out_specs=(
            rows,
            rows,
            P(),
            P(None, mp),
            P(None, mp),
            P(None, mp),
            P(mp, None),
            P(),
            P(None, mp),
            P(None, mp),
            P(mp, None),
        ),
        check_vma=False,
    )
```

time: 521 us -> 489 us (0.939)
  blocking collectives: 16.7 us -> 0 us
  starting transfers between devices: 112 us -> 98.7 us
    ppermute x68 -> x61, starting transfers between devices: 105 us -> 88.3 us  [shifted(): return lax.ppermute(array, axis, [(i, (i + by) % 4) for i in range(4)])]
    all_to_all x1 -> x0, blocking collectives: 16.7 us -> none  [body(): mixed_tokens = lax.all_to_all(mixed, ('z', 'y'), 0, 0).reshape(SEQ, TOK)]
    all_gather x2 -> x1, waiting for transfers between devices: 12.9 us -> 0.01 us  [body(): feed_mine = lax.all_gather(after(feed_half, group_normed), 'z', axis=0)]
    ppermute x68 -> x61, waiting for transfers between devices: 185 us -> 194 us  [shifted(): return lax.ppermute(array, axis, [(i, (i + by) % 4) for i in range(4)])]
    all_to_all x1 -> x2, starting transfers between devices: 3.57 us -> 9.43 us  [the longest x1 4.78 us: body(): down_grads = lax.all_to_all(after(down_grads, b_parts), 'x', 0, 0)]
    pallas_call x16 -> x19, Pallas kernels: 120 us -> 124 us  [call(): pl.pallas_call(kernel, out_shape=out_shape, compiler_params=pltpu.Compile...]
    unnamed x155 -> x117, local copies, waits for them, and re-layouts: 16 us -> 14.2 us
  transfers between devices with their start and end apart: 90 -> 72, of which waited for: 41 -> 35; matrix products, arithmetic and copies ran while one was open for 6% -> 6% of each run, Pallas kernels for 15% -> 15%
where the time goes in v2:
time: 489 us; the launch traced here: 481 us
  waiting for transfers between devices  198 us (40%)
  Pallas kernels  124 us (25%)
  starting transfers between devices  98.7 us (20%)
  local copies, waits for them, and re-layouts  25.2 us (5%)
  other arithmetic  19.7 us (4%)
  between operations  15.1 us (3%)
    ppermute x61, waiting for transfers between devices, shifted(): return lax.ppermute(array, axis, [(i, (i + by) % 4) for i in range(4)])  194 us
    pallas_call x19, Pallas kernels, call(): pl.pallas_call(kernel, out_shape=out_shape, compiler_params=pltpu.Compile...  124 us
    ppermute x61, starting transfers between devices, shifted(): return lax.ppermute(array, axis, [(i, (i + by) % 4) for i in range(4)])  88.3 us
    unnamed x117, local copies, waits for them, and re-layouts  14.2 us
  transfers between devices with their start and end apart: 72, of which 35 were waited for; matrix products, arithmetic and copies ran while one was open for 6% of the time, Pallas kernels for 15%

profile of v2, /device:TPU:0, one launch (start us, length us, event | category | flops | bytes accessed | tf_op | source)
XLA Modules:
  0.0 480.7 jit_solution(15996773791722609381)
XLA Ops:
  17.0 11.6 %collective-permute-done.1.refs_4_ = bf16[128,2048]{1,0:T(8,128)(2,1)S(1)} collective-permute-done((bf16[128,2048]{1,0:T(8,128)(2,1)}, bf16[128,2048]{1,0:T(8,128)(2,1)S(1)}, u32[]{:S(2)}, u32[]{:S(2)}) %collective-permute-start.1) | collective-permute-done | bytes 524320 | tf_op jit(solution)/shard_map/ppermute | solution.py:24
  43.7 4.3 collective-permute-done.7.refs_8_.refs_7_
  48.0 4.2 collective-permute-done.6.refs_7_.refs_6_
  52.2 7.0 %project.1 = (bf16[160,512]{1,0:T(8,128)(2,1)S(1)}, bf16[160,512]{1,0:T(8,128)(2,1)S(1)}, bf16[160,512]{1,0:T(8,128)(2,1)S(1)}, bf16[160,512]{1,0:T(8,128)(2,1)}, bf16[512,2048]{1,0:T(8,128)(2,1)}) custom-call(s32[4]{0:T(128)S(1)} %pad_add_fusion.at_ref.refs_0_, bf16[128,2048]{1,0:T(8,128)(2,1)} %token_ref.1, ...), custom_call_target="tpu_custom_call" | custom-call | flops 1 | bytes 1 | tf_op jit(solution)/shard_map/project/pallas_call | solution.py:246
  71.4 5.7 %attention_forward.1 = (bf16[128,512]{1,0:T(8,128)(2,1)S(1)}, bf16[128,512]{1,0:T(8,128)(2,1)S(1)}, bf16[128,512]{1,0:T(8,128)(2,1)S(1)}, bf16[128,512]{1,0:T(8,...) custom-call(s32[4]{0:T(128)S(1)} %pad_add_fusion.at_ref.refs_0_, ...), custom_call_target="tpu_custom_call" | custom-call | flops 1 | bytes 1 | tf_op jit(solution)/shard_map/attention_forward/pallas_call | solution.py:246
  82.4 6.4 %collective-permute-done.11.m1 = bf16[128,512]{1,0:T(8,128)(2,1)S(1)} collective-permute-done((bf16[128,512]{1,0:T(8,128)(2,1)S(1)}, bf16[128,512]{1,0:T(8,128)(2,1)S(1)}, u32[]{:S(2)}, u32[]{:S(2)}) %collective-permute-start.11) | collective-permute-done | bytes 131104 | tf_op jit(solution)/shard_map/ppermute | solution.py:24
  88.8 4.5 collective-permute-done.12.m2
  113.9 20.1 %collective-permute-done.18 = bf16[64,2048]{1,0:T(8,128)(2,1)S(1)} collective-permute-done((bf16[64,2048]{1,0:T(8,128)(2,1)S(1)}, bf16[64,2048]{1,0:T(8,128)(2,1)S(1)}, u32[]{:S(2)}, u32[]{:S(2)}) %collective-permute-start.18) | collective-permute-done | bytes 262176 | tf_op jit(solution)/shard_map/ppermute | solution.py:24
  134.3 6.8 %collective-permute-done.21.p3 = bf16[128,2048]{1,0:T(8,128)(2,1)S(1)} collective-permute-done((bf16[128,2048]{1,0:T(8,128)(2,1)S(1)}, bf16[128,2048]{1,0:T(8,128)(2,1)S(1)}, u32[]{:S(2)}, u32[]{:S(2)}) %collective-permute-start.21) | collective-permute-done | bytes 524320 | tf_op jit(solution)/shard_map/ppermute | solution.py:24
  141.1 8.3 %collective-permute-done.19.p1 = bf16[128,2048]{1,0:T(8,128)(2,1)S(1)} collective-permute-done((bf16[128,2048]{1,0:T(8,128)(2,1)S(1)}, bf16[128,2048]{1,0:T(8,128)(2,1)S(1)}, u32[]{:S(2)}, u32[]{:S(2)}) %collective-permute-start.19) | collective-permute-done | bytes 524320 | tf_op jit(solution)/shard_map/ppermute | solution.py:24
  153.9 11.2 %collective-permute-done.22.refs_1_.refs_4_ = bf16[128,2048]{1,0:T(8,128)(2,1)S(1)} collective-permute-done((bf16[128,2048]{1,0:T(8,128)(2,1)S(1)}, bf16[128,2048]{1,0:T(8,128)(2,1)S(1)}, u32[]{:S(2)}, u32[]{:S(2)}) %collective-permute-start.22) | collective-permute-done | bytes 524320 | tf_op jit(solution)/shard_map/ppermute | solution.py:24
  170.9 5.4 %collective-permute-done.24.refs_2_.refs_5_ = bf16[64,2048]{1,0:T(8,128)(2,1)S(1)} collective-permute-done((bf16[64,2048]{1,0:T(8,128)(2,1)S(1)}, bf16[64,2048]{1,0:T(8,128)(2,1)S(1)}, u32[]{:S(2)}, u32[]{:S(2)}) %collective-permute-start.24) | collective-permute-done | bytes 262176 | tf_op jit(solution)/shard_map/ppermute | solution.py:24
  183.4 23.5 %feed.1 = (bf16[4,352,512]{2,1,0:T(8,128)(2,1)}, bf16[4,352,512]{2,1,0:T(8,128)(2,1)}, bf16[4,352,512]{2,1,0:T(8,128)(2,1)}, bf16[128,2048]{1,0:T(8,128)(2,1)}, ...) custom-call(s32[4]{0:T(128)S(1)} %pad_add_fusion.at_ref.refs_0_, ...), custom_call_target="tpu_custom_call" | custom-call | flops 1 | bytes 1 | tf_op jit(solution)/shard_map/feed/pallas_call | solution.py:246
  209.2 6.3 %collective-permute-done.28 = bf16[64,2048]{1,0:T(8,128)(2,1)S(1)} collective-permute-done((bf16[64,2048]{1,0:T(8,128)(2,1)S(1)}, bf16[64,2048]{1,0:T(8,128)(2,1)S(1)}, u32[]{:S(2)}, u32[]{:S(2)}) %collective-permute-start.28) | collective-permute-done | bytes 262176 | tf_op jit(solution)/shard_map/ppermute | solution.py:24
  218.9 7.6 %feed_grads.2 = bf16[4,4,704,256]{3,2,1,0:T(8,128)(2,1)} custom-call(s32[4]{0:T(128)S(1)} %pad_add_fusion.at_ref.refs_0_, bf16[4,352,512]{2,1,0:T(8,128)(2,1)} %get-tuple-element.130.refs_1_, bf16[4,352,512]{2,1,0:T(8,128)(2,1)} %get-tuple-element.124.refs_2_, bf16[128,2048]{1,0:T(8,128)(2,1)S(1)} %copy-done.14, bf16[128,2048]{1,0:T(8,128)(2,1)S(1)} %copy-done.7, ...), custom_call_target="tpu_custom_call" | custom-call | flops 1 | bytes 1 | tf_op jit(solution)/shard_map/feed_grads/pallas_call | solution.py:246
  228.9 5.7 %feed_grads.3 = bf16[4,4,352,256]{3,2,1,0:T(8,128)(2,1)} custom-call(s32[4]{0:T(128)S(1)} %pad_add_fusion.at_ref.refs_0_, bf16[4,352,512]{2,1,0:T(8,128)(2,1)} %get-tuple-element.137.refs_1_.hidden_ref, bf16[128,2048]{1,0:T(8,128)(2,1)S(1)} %copy-done.4, bf16[128,2048]{1,0:T(8,128)(2,1)S(1)} %copy-done.12, ...), custom_call_target="tpu_custom_call" | custom-call | flops 1 | bytes 1 | tf_op jit(solution)/shard_map/feed_grads/pallas_call | solution.py:246
  234.6 6.5 %collective-permute-done.30.s3 = bf16[128,2048]{1,0:T(8,128)(2,1)} collective-permute-done((bf16[128,2048]{1,0:T(8,128)(2,1)S(1)}, bf16[128,2048]{1,0:T(8,128)(2,1)}, u32[]{:S(2)}, u32[]{:S(2)}) %collective-permute-start.30) | collective-permute-done | bytes 524320 | tf_op jit(solution)/shard_map/ppermute | solution.py:24
  247.9 10.6 %collective-permute-done.31.b1 = bf16[128,2048]{1,0:T(8,128)(2,1)S(1)} collective-permute-done((bf16[128,2048]{1,0:T(8,128)(2,1)S(1)}, bf16[128,2048]{1,0:T(8,128)(2,1)S(1)}, u32[]{:S(2)}, u32[]{:S(2)}) %collective-permute-start.31) | collective-permute-done | bytes 524320 | tf_op jit(solution)/shard_map/ppermute | solution.py:24
  263.0 9.0 %feed_grads_own.2 = bf16[4,4,704,256]{3,2,1,0:T(8,128)(2,1)} custom-call(s32[4]{0:T(128)S(1)} %pad_add_fusion.at_ref.refs_0_, bf16[4,352,512]{2,1,0:T(8,128)(2,1)} %get-tuple-element.130.refs_1_, bf16[4,352,512]{2,1,0:T(8,128)(2,1)} %get-tuple-element.124.refs_2_, bf16[128,2048]{1,0:T(8,128)(2,1)S(1)} %copy-done.15, bf16[128,2048]{1,0:T(8,128)(2,1)S(1)} %copy-done.8, ...), custom_call_target="tpu_custom_call" | custom-call | flops 1 | bytes 1 | tf_op jit(solution)/shard_map/feed_grads_own/pallas_call | solution.py:246
  277.5 8.8 %down.1 = bf16[4,128,2048]{2,1,0:T(8,128)(2,1)} custom-call(s32[4]{0:T(128)S(1)} %pad_add_fusion.at_ref.refs_0_, bf16[4,352,512]{2,1,0:T(8,128)(2,1)S(1)} %copy-done.2, bf16[4,1056,1024]{2,1,0:T(8,128)(2,1)} %bitcast.77, bf16[4,1056,1024]{2,1,0:T(8,128)(2,1)} %copy-done.31), custom_call_target="tpu_custom_call" | custom-call | flops 1 | bytes 1 | tf_op jit(solution)/shard_map/down/pallas_call | solution.py:246
  290.4 4.6 all-to-all-start
  299.1 6.2 %feed_grads_own.3 = bf16[4,4,352,256]{3,2,1,0:T(8,128)(2,1)} custom-call(s32[4]{0:T(128)S(1)} %pad_add_fusion.at_ref.refs_0_, bf16[4,352,512]{2,1,0:T(8,128)(2,1)} %get-tuple-element.137.refs_1_.hidden_ref, bf16[128,2048]{1,0:T(8,128)(2,1)S(1)} %copy-done.5, bf16[128,2048]{1,0:T(8,128)(2,1)S(1)} %copy-done.12, ...), custom_call_target="tpu_custom_call" | custom-call | flops 1 | bytes 1 | tf_op jit(solution)/shard_map/feed_grads_own/pallas_call | solution.py:246
  305.4 4.4 out_grads.1.refs_11_
  309.8 8.0 %attention_backward.1 = (bf16[160,512]{1,0:T(8,128)(2,1)S(1)}, bf16[160,512]{1,0:T(8,128)(2,1)S(1)}, bf16[160,512]{1,0:T(8,128)(2,1)S(1)}, bf16[160,512]{1,0:T(8,128)(2,1)S(1)}) custom-call(s32[4]{0:T(128)S(1)} %pad_add_fusion.at_ref.refs_0_, bf16[128,512]{1,0:T(8,128)(2,1)S(1)} %get-tuple-element.139.c0, bf16[128,512]{1,0:T(8,128)(2,1)S(1)} %collective-permute-done.37.c1, ...), custom_call_target="tpu_custom_call" | custom-call | flops 1 | bytes 1 | tf_op jit(solution)/shard_map/attention_backward/pallas_call | solution.py:246
  331.1 7.1 %head_grads.1 = (bf16[4,4,304,256]{3,2,1,0:T(8,128)(2,1)}, bf16[4,4,304,256]{3,2,1,0:T(8,128)(2,1)}) custom-call(s32[4]{0:T(128)S(1)} %pad_add_fusion.at_ref.refs_0_, bf16[160,512]{1,0:T(8,128)(2,1)S(1)} %get-tuple-element.153.refs_0_, bf16[160,512]{1,0:T(8,128)(2,1)S(1)} %collective-permute-done.40.refs_1_, ...), custom_call_target="tpu_custom_call" | custom-call | flops 1 | bytes 1 | tf_op jit(solution)/shard_map/head_grads/pallas_call | solution.py:246
  338.1 4.8 all-to-all-start.1
  342.9 5.6 %first_part.1 = (bf16[128,2048]{1,0:T(8,128)(2,1)}, bf16[128,2048]{1,0:T(8,128)(2,1)}, bf16[64,2048]{1,0:T(8,128)(2,1)S(1)}, bf16[64,2048]{1,0:T(8,128)(2,1)S(1)}, bf16[128,2048]{1,0:T(8,128)(2,1)}) custom-call(s32[4]{0:T(128)S(1)} %pad_add_fusion.at_ref.refs_0_, bf16[160,512]{1,0:T(8,128)(2,1)S(1)} %get-tuple-element.153.refs_0_, ...), custom_call_target="tpu_custom_call" | custom-call | flops 1 | bytes 1 | tf_op jit(solution)/shard_map/first_part/pallas_call | solution.py:246
  361.6 12.3 %collective-permute-done.48 = bf16[4,304,256]{2,1,0:T(8,128)(2,1)S(1)} collective-permute-done((bf16[4,304,256]{2,1,0:T(8,128)(2,1)S(1)}, bf16[4,304,256]{2,1,0:T(8,128)(2,1)S(1)}, u32[]{:S(2)}, u32[]{:S(2)}) %collective-permute-start.48) | collective-permute-done | bytes 622624 | tf_op jit(solution)/shard_map/ppermute | solution.py:24
  373.9 13.7 %collective-permute-done.49 = bf16[4,304,256]{2,1,0:T(8,128)(2,1)S(1)} collective-permute-done((bf16[4,304,256]{2,1,0:T(8,128)(2,1)S(1)}, bf16[4,304,256]{2,1,0:T(8,128)(2,1)S(1)}, u32[]{:S(2)}, u32[]{:S(2)}) %collective-permute-start.49) | collective-permute-done | bytes 622624 | tf_op jit(solution)/shard_map/ppermute | solution.py:24
  398.0 4.9 %collective-permute-done.62 = bf16[352,256]{1,0:T(8,128)(2,1)S(1)} collective-permute-done((bf16[352,256]{1,0:T(8,128)(2,1)S(1)}, bf16[352,256]{1,0:T(8,128)(2,1)S(1)}, u32[]{:S(2)}, u32[]{:S(2)}) %collective-permute-start.62) | collective-permute-done | bytes 180256 | tf_op jit(solution)/shard_map/ppermute | solution.py:24
  413.5 23.2 %collective-permute-done.52 = bf16[304,256]{1,0:T(8,128)(2,1)S(1)} collective-permute-done((bf16[304,256]{1,0:T(8,128)(2,1)S(1)}, bf16[304,256]{1,0:T(8,128)(2,1)S(1)}, u32[]{:S(2)}, u32[]{:S(2)}) %collective-permute-start.52) | collective-permute-done | bytes 155680 | tf_op jit(solution)/shard_map/ppermute | solution.py:24
  467.7 5.9 %collect_feed.1 = (f32[352,2048]{1,0:T(8,128)}, f32[352,2048]{1,0:T(8,128)}, f32[352,2048]{1,0:T(8,128)}) custom-call(s32[4]{0:T(128)S(1)} %pad_add_fusion.at_ref.refs_0_, bf16[1056,256]{1,0:T(8,128)(2,1)S(1)} %get-tuple-element.173.refs_1_, bf16[1056,256]{1,0:T(8,128)(2,1)S(1)} %collective-permute-done.64.refs_2_, ...), custom_call_target="tpu_custom_call" | custom-call | flops 1 | bytes 1 | tf_op jit(solution)/shard_map/collect_feed/pallas_call | solution.py:246
  (304 shorter events, 191.5 us)
Async XLA Ops:
  7.2 159.1 %all-gather.3.cloned.1.call-start = ((), (), s32[]{:S(2)}) async-start(), calls=%async_computation.3 | async-start | bytes 10813440 | tf_op jit(solution)/shard_map/all_gather | solution.py:789
  9.6 25.5 %collective-permute-start.4 = (bf16[224,2048]{1,0:T(8,128)(2,1)S(1)}, bf16[224,2048]{1,0:T(8,128)(2,1)S(1)}, u32[]{:S(2)}, u32[]{:S(2)}) collective-permute-start(bf16[224,2048]{1,0:T(8,128)(2,1)S(1)} %pad_maximum_fusion.2.refs_5_.refs_4_), channel_id=1, source_target_pairs={{0,12},{4,0},{8,4},{12,8},{1,13},{5,1},{9,5},{13,9},{2,14},{6,2},{... | collective-permute-start | bytes 2752520 | tf_op jit(solution)/shard_map/ppermute | solution.py:24
  13.8 26.0 %collective-permute-start.5 = (bf16[224,2048]{1,0:T(8,128)(2,1)S(1)}, bf16[224,2048]{1,0:T(8,128)(2,1)}, u32[]{:S(2)}, u32[]{:S(2)}) collective-permute-start(bf16[224,2048]{1,0:T(8,128)(2,1)S(1)} %pad_maximum_fusion.2.refs_5_.refs_4_), channel_id=1, source_target_pairs={{0,4},{4,8},{8,12},{12,0},{1,5},{5,9},{9,13},{13,1},{2,6},{6,10},{... | collective-permute-start | bytes 2752520 | tf_op jit(solution)/shard_map/ppermute | solution.py:24
  13.8 14.9 %collective-permute-start.1 = (bf16[128,2048]{1,0:T(8,128)(2,1)}, bf16[128,2048]{1,0:T(8,128)(2,1)S(1)}, u32[]{:S(2)}, u32[]{:S(2)}) collective-permute-start(bf16[128,2048]{1,0:T(8,128)(2,1)} %token_ref.1), channel_id=1, source_target_pairs={{0,1},{1,2},{2,3},{3,0},{4,5},{5,6},{6,7},{7,4},{8,9},{9,10},{10,1... | collective-permute-start | bytes 1572872 | tf_op jit(solution)/shard_map/ppermute | solution.py:24
  15.3 15.1 %collective-permute-start = (bf16[128,2048]{1,0:T(8,128)(2,1)}, bf16[128,2048]{1,0:T(8,128)(2,1)}, u32[]{:S(2)}, u32[]{:S(2)}) collective-permute-start(bf16[128,2048]{1,0:T(8,128)(2,1)} %token_ref.1), channel_id=1, source_target_pairs={{0,3},{1,0},{2,1},{3,2},{4,7},{5,4},{6,5},{7,6},{8,11},{9,8},{10,9... | collective-permute-start | bytes 1572872 | tf_op jit(solution)/shard_map/ppermute | solution.py:24
  59.3 343.8 %reduce-scatter.4.cloned.1.call-start = ((), (), s32[]{:S(2)}) async-start(), calls=%async_computation.4 | async-start | bytes 6127616
  70.2 24.3 %collective-permute-start.14 = (bf16[4,64,2048]{2,1,0:T(8,128)(2,1)S(1)}, bf16[4,64,2048]{2,1,0:T(8,128)(2,1)}, u32[]{:S(2)}, u32[]{:S(2)}) collective-permute-start(bf16[4,64,2048]{2,1,0:T(8,128)(2,1)S(1)} %pad_maximum_fusion.1.own_ref), channel_id=1, source_target_pairs={{0,16},{16,0},{1,17},{17,1},{2,18},{18,2},{3,19},{19,3},{4,20},{20... | collective-permute-start | bytes 3145736 | tf_op jit(solution)/shard_map/ppermute | solution.py:28
  78.0 15.3 %collective-permute-start.12 = (bf16[128,512]{1,0:T(8,128)(2,1)S(1)}, bf16[128,512]{1,0:T(8,128)(2,1)S(1)}, u32[]{:S(2)}, u32[]{:S(2)}) collective-permute-start(bf16[128,512]{1,0:T(8,128)(2,1)S(1)} %get-tuple-element.102), channel_id=1, source_target_pairs={{0,8},{4,12},{8,0},{12,4},{1,9},{5,13},{9,1},{13,5},{2,10},{6,14},... | collective-permute-start | bytes 393224 | tf_op jit(solution)/shard_map/ppermute | solution.py:24
  102.2 32.0 %collective-permute-start.15 = (bf16[128,2048]{1,0:T(8,128)(2,1)S(1)}, bf16[128,2048]{1,0:T(8,128)(2,1)S(1)}, u32[]{:S(2)}, u32[]{:S(2)}) collective-permute-start(bf16[128,2048]{1,0:T(8,128)(2,1)S(1)} %copy-done.3), channel_id=1, source_target_pairs={{0,3},{1,0},{2,1},{3,2},{4,7},{5,4},{6,5},{7,6},{8,11},{9,8},{10,9... | collective-permute-start | bytes 1572872 | tf_op jit(solution)/shard_map/ppermute | solution.py:24
  102.9 31.3 %collective-permute-start.16 = (bf16[128,2048]{1,0:T(8,128)(2,1)S(1)}, bf16[128,2048]{1,0:T(8,128)(2,1)S(1)}, u32[]{:S(2)}, u32[]{:S(2)}) collective-permute-start(bf16[128,2048]{1,0:T(8,128)(2,1)S(1)} %copy-done.3), channel_id=1, source_target_pairs={{0,2},{1,3},{2,0},{3,1},{4,6},{5,7},{6,4},{7,5},{8,10},{9,11},{10,... | collective-permute-start | bytes 1572872 | tf_op jit(solution)/shard_map/ppermute | solution.py:24
  102.9 31.3 %collective-permute-start.17 = (bf16[128,2048]{1,0:T(8,128)(2,1)S(1)}, bf16[128,2048]{1,0:T(8,128)(2,1)S(1)}, u32[]{:S(2)}, u32[]{:S(2)}) collective-permute-start(bf16[128,2048]{1,0:T(8,128)(2,1)S(1)} %copy-done.3), channel_id=1, source_target_pairs={{0,1},{1,2},{2,3},{3,0},{4,5},{5,6},{6,7},{7,4},{8,9},{9,10},{10,1... | collective-permute-start | bytes 1572872 | tf_op jit(solution)/shard_map/ppermute | solution.py:24
  104.2 29.8 %collective-permute-start.18 = (bf16[64,2048]{1,0:T(8,128)(2,1)S(1)}, bf16[64,2048]{1,0:T(8,128)(2,1)S(1)}, u32[]{:S(2)}, u32[]{:S(2)}) collective-permute-start(bf16[64,2048]{1,0:T(8,128)(2,1)S(1)} %get-tuple-element.109), channel_id=1, source_target_pairs={{0,1},{1,2},{2,3},{3,0},{4,5},{5,6},{6,7},{7,4},{8,9},{9,10},{10,1... | collective-permute-start | bytes 786440 | tf_op jit(solution)/shard_map/ppermute | solution.py:24
  110.1 30.9 %collective-permute-start.21 = (bf16[128,2048]{1,0:T(8,128)(2,1)S(1)}, bf16[128,2048]{1,0:T(8,128)(2,1)S(1)}, u32[]{:S(2)}, u32[]{:S(2)}) collective-permute-start(bf16[128,2048]{1,0:T(8,128)(2,1)S(1)} %pad_maximum_fusion.6), channel_id=1, source_target_pairs={{0,3},{1,0},{2,1},{3,2},{4,7},{5,4},{6,5},{7,6},{8,11},{9,8},{10,9... | collective-permute-start | bytes 1572872 | tf_op jit(solution)/shard_map/ppermute | solution.py:24
  134.1 15.2 %collective-permute-start.19 = (bf16[128,2048]{1,0:T(8,128)(2,1)S(1)}, bf16[128,2048]{1,0:T(8,128)(2,1)S(1)}, u32[]{:S(2)}, u32[]{:S(2)}) collective-permute-start(bf16[128,2048]{1,0:T(8,128)(2,1)S(1)} %pad_maximum_fusion.5), channel_id=1, source_target_pairs={{0,1},{1,2},{2,3},{3,0},{4,5},{5,6},{6,7},{7,4},{8,9},{9,10},{10,1... | collective-permute-start | bytes 1572872 | tf_op jit(solution)/shard_map/ppermute | solution.py:24
  226.5 34.1 %collective-permute-start.33 = (bf16[4,4,704,256]{3,2,1,0:T(8,128)(2,1)}, bf16[4,4,704,256]{3,2,1,0:T(8,128)(2,1)S(1)}, u32[]{:S(2)}, u32[]{:S(2)}) collective-permute-start(bf16[4,4,704,256]{3,2,1,0:T(8,128)(2,1)} %feed_grads.2), channel_id=1, source_target_pairs={{0,16},{16,0},{1,17},{17,1},{2,18},{18,2},{3,19},{19,3},{4,20},{20... | collective-permute-start | bytes 17301512 | tf_op jit(solution)/shard_map/ppermute | solution.py:28
  227.6 14.8 %collective-permute-start.29 = (bf16[128,2048]{1,0:T(8,128)(2,1)S(1)}, bf16[128,2048]{1,0:T(8,128)(2,1)S(1)}, u32[]{:S(2)}, u32[]{:S(2)}) collective-permute-start(bf16[128,2048]{1,0:T(8,128)(2,1)S(1)} %pad_maximum_fusion.7), channel_id=1, source_target_pairs={{0,1},{1,2},{2,3},{3,0},{4,5},{5,6},{6,7},{7,4},{8,9},{9,10},{10,1... | collective-permute-start | bytes 1572872 | tf_op jit(solution)/shard_map/ppermute | solution.py:24
  272.0 27.0 %collective-permute-start.36 = (bf16[4,4,352,256]{3,2,1,0:T(8,128)(2,1)}, bf16[4,4,352,256]{3,2,1,0:T(8,128)(2,1)}, u32[]{:S(2)}, u32[]{:S(2)}) collective-permute-start(bf16[4,4,352,256]{3,2,1,0:T(8,128)(2,1)} %feed_grads.3), channel_id=1, source_target_pairs={{0,16},{16,0},{1,17},{17,1},{2,18},{18,2},{3,19},{19,3},{4,20},{20... | collective-permute-start | bytes 8650760 | tf_op jit(solution)/shard_map/ppermute | solution.py:28
  290.4 32.8 %all-to-all-start = ((bf16[4,128,2048]{2,1,0:T(8,128)(2,1)}), bf16[4,128,2048]{2,1,0:T(8,128)(2,1)}, u32[]{:S(2)}, u32[]{:S(2)}) async-start(bf16[4,128,2048]{2,1,0:T(8,128)(2,1)} %down.1), calls=%async_computation | async-start | bytes 4194304 | tf_op jit(solution)/shard_map/all_to_all | solution.py:838
  295.0 14.7 %collective-permute-start.37 = (bf16[128,512]{1,0:T(8,128)(2,1)}, bf16[128,512]{1,0:T(8,128)(2,1)S(1)}, u32[]{:S(2)}, u32[]{:S(2)}) collective-permute-start(bf16[128,512]{1,0:T(8,128)(2,1)} %get-tuple-element.140), channel_id=1, source_target_pairs={{0,4},{4,8},{8,12},{12,0},{1,5},{5,9},{9,13},{13,1},{2,6},{6,10},{... | collective-permute-start | bytes 393224 | tf_op jit(solution)/shard_map/ppermute | solution.py:24
  338.1 15.0 %collective-permute-start.47 = (bf16[4,4,304,256]{3,2,1,0:T(8,128)(2,1)}, bf16[4,4,304,256]{3,2,1,0:T(8,128)(2,1)}, u32[]{:S(2)}, u32[]{:S(2)}) collective-permute-start(bf16[4,4,304,256]{3,2,1,0:T(8,128)(2,1)} %get-tuple-element.160), channel_id=1, source_target_pairs={{0,16},{16,0},{1,17},{17,1},{2,18},{18,2},{3,19},{19,3},{4,20},{20... | collective-permute-start | bytes 7471112 | tf_op jit(solution)/shard_map/ppermute | solution.py:28
  338.1 49.9 %all-to-all-start.1 = ((bf16[4,4,352,256]{3,2,1,0:T(8,128)(2,1)}), bf16[4,4,352,256]{3,2,1,0:T(8,128)(2,1)}, u32[]{:S(2)}, u32[]{:S(2)}) async-start(bf16[4,4,352,256]{3,2,1,0:T(8,128)(2,1)} %feed_grads_own.3), calls=%async_computation.1 | async-start | bytes 5767168 | tf_op jit(solution)/shard_map/all_to_all | solution.py:861
  356.6 17.4 %collective-permute-start.48 = (bf16[4,304,256]{2,1,0:T(8,128)(2,1)S(1)}, bf16[4,304,256]{2,1,0:T(8,128)(2,1)S(1)}, u32[]{:S(2)}, u32[]{:S(2)}) collective-permute-start(bf16[4,304,256]{2,1,0:T(8,128)(2,1)S(1)} %get-tuple-element.162), channel_id=1, source_target_pairs={{0,4},{4,8},{8,12},{12,0},{1,5},{5,9},{9,13},{13,1},{2,6},{6,10},{... | collective-permute-start | bytes 1867784 | tf_op jit(solution)/shard_map/ppermute | solution.py:24
  357.5 30.0 %collective-permute-start.49 = (bf16[4,304,256]{2,1,0:T(8,128)(2,1)S(1)}, bf16[4,304,256]{2,1,0:T(8,128)(2,1)S(1)}, u32[]{:S(2)}, u32[]{:S(2)}) collective-permute-start(bf16[4,304,256]{2,1,0:T(8,128)(2,1)S(1)} %get-tuple-element.163), channel_id=1, source_target_pairs={{0,8},{4,12},{8,0},{12,4},{1,9},{5,13},{9,1},{13,5},{2,10},{6,14},... | collective-permute-start | bytes 1867784 | tf_op jit(solution)/shard_map/ppermute | solution.py:24
  360.2 27.5 %collective-permute-start.50 = (bf16[4,304,256]{2,1,0:T(8,128)(2,1)}, bf16[4,304,256]{2,1,0:T(8,128)(2,1)S(1)}, u32[]{:S(2)}, u32[]{:S(2)}) collective-permute-start(bf16[4,304,256]{2,1,0:T(8,128)(2,1)} %get-tuple-element.164), channel_id=1, source_target_pairs={{0,12},{4,0},{8,4},{12,8},{1,13},{5,1},{9,5},{13,9},{2,14},{6,2},{... | collective-permute-start | bytes 1867784 | tf_op jit(solution)/shard_map/ppermute | solution.py:24
  404.2 36.8 %collective-permute-start.64 = (bf16[1056,256]{1,0:T(8,128)(2,1)S(1)}, bf16[1056,256]{1,0:T(8,128)(2,1)S(1)}, u32[]{:S(2)}, u32[]{:S(2)}) collective-permute-start(bf16[1056,256]{1,0:T(8,128)(2,1)S(1)} %get-tuple-element.173.refs_1_), channel_id=1, source_target_pairs={{0,96},{32,0},{64,32},{96,64},{1,97},{33,1},{65,33},{97,65},{2,98}... | collective-permute-start | bytes 1622024 | tf_op jit(solution)/shard_map/ppermute | solution.py:24
  407.2 35.5 %collective-permute-start.65 = (bf16[1056,256]{1,0:T(8,128)(2,1)S(1)}, bf16[1056,256]{1,0:T(8,128)(2,1)S(1)}, u32[]{:S(2)}, u32[]{:S(2)}) collective-permute-start(bf16[1056,256]{1,0:T(8,128)(2,1)S(1)} %get-tuple-element.173.refs_1_), channel_id=1, source_target_pairs={{0,64},{32,96},{64,0},{96,32},{1,65},{33,97},{65,1},{97,33},{2,66}... | collective-permute-start | bytes 1622024 | tf_op jit(solution)/shard_map/ppermute | solution.py:24
  408.0 35.2 %collective-permute-start.66 = (bf16[1056,256]{1,0:T(8,128)(2,1)S(1)}, bf16[1056,256]{1,0:T(8,128)(2,1)S(1)}, u32[]{:S(2)}, u32[]{:S(2)}) collective-permute-start(bf16[1056,256]{1,0:T(8,128)(2,1)S(1)} %get-tuple-element.173.refs_1_), channel_id=1, source_target_pairs={{0,32},{32,64},{64,96},{96,0},{1,33},{33,65},{65,97},{97,1},{2,34}... | collective-permute-start | bytes 1622024 | tf_op jit(solution)/shard_map/ppermute | solution.py:24
  408.9 27.8 %collective-permute-start.52 = (bf16[304,256]{1,0:T(8,128)(2,1)S(1)}, bf16[304,256]{1,0:T(8,128)(2,1)S(1)}, u32[]{:S(2)}, u32[]{:S(2)}) collective-permute-start(bf16[304,256]{1,0:T(8,128)(2,1)S(1)} %copy-done.56), channel_id=1, source_target_pairs={{0,64},{32,96},{64,0},{96,32},{1,65},{33,97},{65,1},{97,33},{2,66}... | collective-permute-start | bytes 466952 | tf_op jit(solution)/shard_map/ppermute | solution.py:24
  410.8 26.2 %collective-permute-start.53 = (bf16[304,256]{1,0:T(8,128)(2,1)S(1)}, bf16[304,256]{1,0:T(8,128)(2,1)S(1)}, u32[]{:S(2)}, u32[]{:S(2)}) collective-permute-start(bf16[304,256]{1,0:T(8,128)(2,1)S(1)} %copy-done.55), channel_id=1, source_target_pairs={{0,96},{32,0},{64,32},{96,64},{1,97},{33,1},{65,33},{97,65},{2,98}... | collective-permute-start | bytes 466952 | tf_op jit(solution)/shard_map/ppermute | solution.py:24
  436.7 18.1 %collective-permute-start.44 = (bf16[128,2048]{1,0:T(8,128)(2,1)S(1)}, bf16[128,2048]{1,0:T(8,128)(2,1)S(1)}, u32[]{:S(2)}, u32[]{:S(2)}) collective-permute-start(bf16[128,2048]{1,0:T(8,128)(2,1)S(1)} %pad_maximum_fusion.9), channel_id=1, source_target_pairs={{0,1},{1,2},{2,3},{3,0},{4,5},{5,6},{6,7},{7,4},{8,9},{9,10},{10,1... | collective-permute-start | bytes 1572872 | tf_op jit(solution)/shard_map/ppermute | solution.py:24
  437.0 17.8 %collective-permute-start.46 = (bf16[128,2048]{1,0:T(8,128)(2,1)S(1)}, bf16[128,2048]{1,0:T(8,128)(2,1)S(1)}, u32[]{:S(2)}, u32[]{:S(2)}) collective-permute-start(bf16[128,2048]{1,0:T(8,128)(2,1)S(1)} %pad_maximum_fusion.10), channel_id=1, source_target_pairs={{0,3},{1,0},{2,1},{3,2},{4,7},{5,4},{6,5},{7,6},{8,11},{9,8},{10,9... | collective-permute-start | bytes 1572872 | tf_op jit(solution)/shard_map/ppermute | solution.py:24
  447.4 19.0 %collective-permute-start.67 = (bf16[4,1056,256]{2,1,0:T(8,128)(2,1)S(1)}, bf16[4,1056,256]{2,1,0:T(8,128)(2,1)S(1)}, u32[]{:S(2)}, u32[]{:S(2)}) collective-permute-start(bf16[4,1056,256]{2,1,0:T(8,128)(2,1)S(1)} %pad_maximum_fusion), channel_id=1, source_target_pairs={{0,16},{16,0},{1,17},{17,1},{2,18},{18,2},{3,19},{19,3},{4,20},{20... | collective-permute-start | bytes 6488072 | tf_op jit(solution)/shard_map/ppermute | solution.py:28
  (98 other events, 1174.4 us)
Sparse Core Ops, SparseCore 0:
  59.4 90.1 all-gather.2
  272.2 84.7 reduce-scatter.3

commit v3 on v2

--- a/solution.py
+++ b/solution.py
@@ -786,22 +786,27 @@
     feed_half = jnp.concatenate([w_gate.T, w_up.T, w_down], axis=0)
     feed_half = lax.dynamic_slice_in_dim(feed_half, core * 1024, 1024, 1)
     *qkv, group_normed = project(order, at, token_blocks, head_blocks, gain_first, ())
-    feed_mine = lax.all_gather(after(feed_half, group_normed), "z", axis=0)
+    feed_half = after(feed_half, *token_blocks[2:4], *head_blocks[2:4])
+    feed_mine = lax.all_gather(feed_half, "z", axis=0)
     qkv = exchanged(qkv, "z")
     out_mine = jnp.stack([block[-(HEAD_V // 2) :] for block in (*head_blocks[:2], *head_blocks[3:])])
     out_mine = after(out_mine, *qkv)
     out_weights = (out_mine, swapped(out_mine))
-    cot_blocks = gathered(after(out_grad, *qkv), "y")
+    cot_rows = jnp.broadcast_to(after(out_grad, group_normed)[None], (4, TOK, D))
+    cot_rows = lax.all_to_all(cot_rows, "y", 0, 0)
 
     positions = jnp.arange(SEQ, dtype=jnp.int32)
     start_row = lax.cummax(jnp.where(doc_start != 0, positions, 0))[None, :]
     *mixed, numer, denom, qkv = attention_forward(order, at, qkv, start_row, ())
     mixed = exchanged(mixed, "z")
-    p0, p1, *p2, p3 = out_projection(order, at, mixed, out_weights, ())
+    p0, p1, *p2, p3 = out_projection(order, at, mixed, out_weights, (cot_rows,))
     parts = (p0, *ring_end(ring_start(p2, "y"), p1, p3, "y"))
-    mid_rows, second_normed = middle(order, at, parts, tokens, gain_second, cot_blocks)
-
-    cot_blocks = [*cot_blocks[:2], cot_blocks[2][:64], cot_blocks[2][64:], cot_blocks[3]]
+    mid_rows, second_normed = middle(order, at, parts, tokens, gain_second, ())
+
+    cot_blocks = [out_grad] + [
+        lax.dynamic_slice(cot_rows, ((y_at + d) % 4, first, 0), (1, count, D))[0]
+        for d, first, count in RING_ROWS[1:]
+    ]
     second_blocks = ring_gathered(second_normed, "y")
     feed_mine = after(feed_mine, second_blocks[1], second_blocks[4])
     feed_weights = (feed_mine, swapped(feed_mine))
@@ -862,9 +867,14 @@
     other = swapped(other)
     f0, f1, *f2, f3 = first_part(order, at, grads, head_blocks, ())
     head_part = added(exchanged(add_blocks(order, at, mine, other), "z"))
-    from_back, from_ahead = ring_end(ring_start(f2, "y"), f1, f3, "y")
+    f_arrived = ring_start(f2, "y")
+    head_part = after(head_part, *f_arrived)
+    from_back, from_ahead = ring_end(f_arrived, f1, f3, "y")
+    gu_blocks = gathered(gu_sum, "x")
+    head_part = after(head_part, *gu_blocks[1:])
     head_sum = added(exchanged([head_part[d] for d in range(4)], "x"))
-    down_part = jnp.sum(after(down_grads, head_part).astype(F32), axis=0).astype(BF16)
+    down_grads = after(down_grads, *gu_blocks[1:])
+    down_part = jnp.sum(down_grads.astype(F32), axis=0).astype(BF16)
     down_sum = added(exchanged([down_part[d] for d in range(4)], "z"))
     grad_first = f0.astype(F32) + from_back.astype(F32) + from_ahead.astype(F32)
     block_out = mid_rows + jnp.sum(b_parts.astype(F32), axis=0)
@@ -872,24 +882,24 @@
     first_inv = inverse_rms(x_rows)
     input_grad = grad_mid + norm_back(grad_first, x_rows * first_inv, first_inv, gain_first)
 
-    grad_out, grad_query, grad_key, grad_value, gains = collect(
+    grad_gate, grad_up = collect(order, at, gu_blocks, "collect_gate_up", HID, HID)
+    rest_sum = jnp.concatenate([head_sum, down_sum], axis=0)
+    rest_sum = after(rest_sum, grad_gate, from_back, from_ahead)
+    grad_out, grad_query, grad_key, grad_value, gains, grad_down = collect(
         order,
         at,
-        gathered(head_sum, "x"),
-        "collect_heads",
+        gathered(rest_sum, "x"),
+        "collect_rest",
         HEAD_V,
         FEAT,
         FEAT,
         HEAD_V,
         2,
+        HID,
         turned=3,
     )
     gains = gathered(gains, "y")
     gains = (gains[0] + gains[1]) + (gains[2] + gains[3])
-    ffn_sum = jnp.concatenate([gu_sum, down_sum], axis=0)
-    grad_gate, grad_up, grad_down = collect(
-        order, at, gathered(ffn_sum, "x"), "collect_feed", HID, HID, HID
-    )
     return (
         block_out,
         input_grad,

time: 489 us -> 462 us (0.945)
  waiting for transfers between devices: 198 us -> 171 us
    ppermute x61 -> x58, waiting for transfers between devices: 194 us -> 157 us  [shifted(): return lax.ppermute(array, axis, [(i, (i + by) % 4) for i in range(4)])]
    unnamed x3, waiting for transfers between devices: 0.05 us -> 6.2 us
    unnamed x117 -> x105, local copies, waits for them, and re-layouts: 14.2 us -> 8.5 us
    ppermute x61 -> x58, starting transfers between devices: 88.3 us -> 85.9 us  [shifted(): return lax.ppermute(array, axis, [(i, (i + by) % 4) for i in range(4)])]
  transfers between devices with their start and end apart: 72 -> 70, of which waited for: 35 -> 34; matrix products, arithmetic and copies ran while one was open for 6% -> 7% of each run, Pallas kernels for 15% -> 18%
where the time goes in v3:
time: 462 us; the launch traced here: 454 us
  waiting for transfers between devices  171 us (37%)
  Pallas kernels  124 us (27%)
  starting transfers between devices  101 us (22%)
  local copies, waits for them, and re-layouts  22.7 us (5%)
  other arithmetic  20.8 us (5%)
  between operations  15 us (3%)
    ppermute x58, waiting for transfers between devices, shifted(): return lax.ppermute(array, axis, [(i, (i + by) % 4) for i in range(4)])  157 us
    pallas_call x19, Pallas kernels, call(): pl.pallas_call(kernel, out_shape=out_shape, compiler_params=pltpu.Compile...  124 us
    ppermute x58, starting transfers between devices, shifted(): return lax.ppermute(array, axis, [(i, (i + by) % 4) for i in range(4)])  85.9 us
  transfers between devices with their start and end apart: 70, of which 34 were waited for; matrix products, arithmetic and copies ran while one was open for 7% of the time, Pallas kernels for 18%

profile of v3, /device:TPU:0, one launch (start us, length us, event | category | flops | bytes accessed | tf_op | source)
XLA Modules:
  0.0 454.1 jit_solution(3766550527738780873)
XLA Ops:
  9.6 4.2 collective-permute-start.4
  17.1 16.4 %collective-permute-done.4.refs_6_.refs_5_ = bf16[224,2048]{1,0:T(8,128)(2,1)S(1)} collective-permute-done((bf16[224,2048]{1,0:T(8,128)(2,1)S(1)}, bf16[224,2048]{1,0:T(8,128)(2,1)S(1)}, u32[]{:S(2)}, u32[]{:S(2)}) %collective-permute-start.4) | collective-permute-done | bytes 917536 | tf_op jit(solution)/shard_map/ppermute | solution.py:24
  54.4 6.8 %project.1 = (bf16[160,512]{1,0:T(8,128)(2,1)S(1)}, bf16[160,512]{1,0:T(8,128)(2,1)S(1)}, bf16[160,512]{1,0:T(8,128)(2,1)S(1)}, bf16[160,512]{1,0:T(8,128)(2,1)S(1)}, bf16[512,2048]{1,0:T(8,128)(2,1)}) custom-call(s32[4]{0:T(128)S(1)} %pad_add_fusion.at_ref.refs_0_, bf16[128,2048]{1,0:T(8,128)(2,1)} %token_ref.1, ...), custom_call_target="tpu_custom_call" | custom-call | flops 1 | bytes 1 | tf_op jit(solution)/shard_map/project/pallas_call | solution.py:246
  65.4 4.6 %all-to-all-start = ((bf16[4,128,2048]{2,1,0:T(8,128)(2,1)}), bf16[4,128,2048]{2,1,0:T(8,128)(2,1)}, u32[]{:S(2)}, u32[]{:S(2)}) async-start(bf16[4,128,2048]{2,1,0:T(8,128)(2,1)} %broadcast_in_dim.9), calls=%async_computation | async-start | bytes 4194304 | tf_op jit(solution)/shard_map/all_to_all | solution.py:796
  76.2 5.7 %attention_forward.1 = (bf16[128,512]{1,0:T(8,128)(2,1)S(1)}, bf16[128,512]{1,0:T(8,128)(2,1)S(1)}, bf16[128,512]{1,0:T(8,128)(2,1)S(1)}, bf16[128,512]{1,0:T(8,...) custom-call(s32[4]{0:T(128)S(1)} %pad_add_fusion.at_ref.refs_0_, ...), custom_call_target="tpu_custom_call" | custom-call | flops 1 | bytes 1 | tf_op jit(solution)/shard_map/attention_forward/pallas_call | solution.py:246
  89.4 4.2 all-to-all-done
  93.6 5.8 %collective-permute-done.12.m2 = bf16[128,512]{1,0:T(8,128)(2,1)S(1)} collective-permute-done((bf16[128,512]{1,0:T(8,128)(2,1)S(1)}, bf16[128,512]{1,0:T(8,128)(2,1)S(1)}, u32[]{:S(2)}, u32[]{:S(2)}) %collective-permute-start.12) | collective-permute-done | bytes 131104 | tf_op jit(solution)/shard_map/ppermute | solution.py:24
  107.6 5.6 %collective-permute-done.17 = bf16[64,2048]{1,0:T(8,128)(2,1)S(1)} collective-permute-done((bf16[64,2048]{1,0:T(8,128)(2,1)S(1)}, bf16[64,2048]{1,0:T(8,128)(2,1)S(1)}, u32[]{:S(2)}, u32[]{:S(2)}) %collective-permute-start.17) | collective-permute-done | bytes 262176 | tf_op jit(solution)/shard_map/ppermute | solution.py:24
  118.4 10.3 %collective-permute-done.18.p3 = bf16[128,2048]{1,0:T(8,128)(2,1)S(1)} collective-permute-done((bf16[128,2048]{1,0:T(8,128)(2,1)S(1)}, bf16[128,2048]{1,0:T(8,128)(2,1)S(1)}, u32[]{:S(2)}, u32[]{:S(2)}) %collective-permute-start.18) | collective-permute-done | bytes 524320 | tf_op jit(solution)/shard_map/ppermute | solution.py:24
  136.9 9.9 %collective-permute-done.19.refs_1_.refs_4_ = bf16[128,2048]{1,0:T(8,128)(2,1)S(1)} collective-permute-done((bf16[128,2048]{1,0:T(8,128)(2,1)S(1)}, bf16[128,2048]{1,0:T(8,128)(2,1)S(1)}, u32[]{:S(2)}, u32[]{:S(2)}) %collective-permute-start.19) | collective-permute-done | bytes 524320 | tf_op jit(solution)/shard_map/ppermute | solution.py:24
  162.7 23.7 %feed.1 = (bf16[4,352,512]{2,1,0:T(8,128)(2,1)}, bf16[4,352,512]{2,1,0:T(8,128)(2,1)}, bf16[4,352,512]{2,1,0:T(8,128)(2,1)}, bf16[128,2048]{1,0:T(8,128)(2,1)}, ...) custom-call(s32[4]{0:T(128)S(1)} %pad_add_fusion.at_ref.refs_0_, ...), custom_call_target="tpu_custom_call" | custom-call | flops 1 | bytes 1 | tf_op jit(solution)/shard_map/feed/pallas_call | solution.py:246
  188.6 6.3 %collective-permute-done.25 = bf16[64,2048]{1,0:T(8,128)(2,1)S(1)} collective-permute-done((bf16[64,2048]{1,0:T(8,128)(2,1)S(1)}, bf16[64,2048]{1,0:T(8,128)(2,1)S(1)}, u32[]{:S(2)}, u32[]{:S(2)}) %collective-permute-start.25) | collective-permute-done | bytes 262176 | tf_op jit(solution)/shard_map/ppermute | solution.py:24
  196.2 7.6 %feed_grads.2 = bf16[4,4,704,256]{3,2,1,0:T(8,128)(2,1)} custom-call(s32[4]{0:T(128)S(1)} %pad_add_fusion.at_ref.refs_0_, bf16[4,352,512]{2,1,0:T(8,128)(2,1)} %get-tuple-element.131.refs_1_, bf16[4,352,512]{2,1,0:T(8,128)(2,1)} %get-tuple-element.125.refs_2_, bf16[128,2048]{1,0:T(8,128)(2,1)S(1)} %copy-done.12, bf16[128,2048]{1,0:T(8,128)(2,1)S(1)} %copy-done.8, ...), custom_call_target="tpu_custom_call" | custom-call | flops 1 | bytes 1 | tf_op jit(solution)/shard_map/feed_grads/pallas_call | solution.py:246
  206.2 5.7 %feed_grads.3 = bf16[4,4,352,256]{3,2,1,0:T(8,128)(2,1)} custom-call(s32[4]{0:T(128)S(1)} %pad_add_fusion.at_ref.refs_0_, bf16[4,352,512]{2,1,0:T(8,128)(2,1)} %get-tuple-element.138.refs_1_.hidden_ref, bf16[128,2048]{1,0:T(8,128)(2,1)S(1)} %copy-done.3, bf16[128,2048]{1,0:T(8,128)(2,1)S(1)} %copy-done.6, ...), custom_call_target="tpu_custom_call" | custom-call | flops 1 | bytes 1 | tf_op jit(solution)/shard_map/feed_grads/pallas_call | solution.py:246
  211.9 6.4 %collective-permute-done.27.s3 = bf16[128,2048]{1,0:T(8,128)(2,1)S(1)} collective-permute-done((bf16[128,2048]{1,0:T(8,128)(2,1)S(1)}, bf16[128,2048]{1,0:T(8,128)(2,1)S(1)}, u32[]{:S(2)}, u32[]{:S(2)}) %collective-permute-start.27) | collective-permute-done | bytes 524320 | tf_op jit(solution)/shard_map/ppermute | solution.py:24
  225.2 10.9 %collective-permute-done.28.b1 = bf16[128,2048]{1,0:T(8,128)(2,1)S(1)} collective-permute-done((bf16[128,2048]{1,0:T(8,128)(2,1)S(1)}, bf16[128,2048]{1,0:T(8,128)(2,1)S(1)}, u32[]{:S(2)}, u32[]{:S(2)}) %collective-permute-start.28) | collective-permute-done | bytes 524320 | tf_op jit(solution)/shard_map/ppermute | solution.py:24
  241.2 9.0 %feed_grads_own.2 = bf16[4,4,704,256]{3,2,1,0:T(8,128)(2,1)} custom-call(s32[4]{0:T(128)S(1)} %pad_add_fusion.at_ref.refs_0_, bf16[4,352,512]{2,1,0:T(8,128)(2,1)} %get-tuple-element.131.refs_1_, bf16[4,352,512]{2,1,0:T(8,128)(2,1)} %get-tuple-element.125.refs_2_, bf16[128,2048]{1,0:T(8,128)(2,1)S(1)} %copy-done.12, bf16[128,2048]{1,0:T(8,128)(2,1)S(1)} %copy-done.8, ...), custom_call_target="tpu_custom_call" | custom-call | flops 1 | bytes 1 | tf_op jit(solution)/shard_map/feed_grads_own/pallas_call | solution.py:246
  255.7 9.0 %down.1 = bf16[4,128,2048]{2,1,0:T(8,128)(2,1)} custom-call(s32[4]{0:T(128)S(1)} %pad_add_fusion.at_ref.refs_0_, bf16[4,352,512]{2,1,0:T(8,128)(2,1)S(1)} %copy-done.5, bf16[4,1056,1024]{2,1,0:T(8,128)(2,1)} %bitcast.86, bf16[4,1056,1024]{2,1,0:T(8,128)(2,1)} %collective-permute-done.23.refs_11_.other_ref), custom_call_target="tpu_custom_call" | custom-call | flops 1 | bytes 1 | tf_op jit(solution)/shard_map/down/pallas_call | solution.py:246
  268.1 4.6 %all-to-all-start.1 = ((bf16[4,128,2048]{2,1,0:T(8,128)(2,1)}), bf16[4,128,2048]{2,1,0:T(8,128)(2,1)}, u32[]{:S(2)}, u32[]{:S(2)}) async-start(bf16[4,128,2048]{2,1,0:T(8,128)(2,1)} %down.1), calls=%async_computation.1 | async-start | bytes 4194304 | tf_op jit(solution)/shard_map/all_to_all | solution.py:843
  277.5 6.3 %feed_grads_own.3 = bf16[4,4,352,256]{3,2,1,0:T(8,128)(2,1)} custom-call(s32[4]{0:T(128)S(1)} %pad_add_fusion.at_ref.refs_0_, bf16[4,352,512]{2,1,0:T(8,128)(2,1)} %get-tuple-element.138.refs_1_.hidden_ref, bf16[128,2048]{1,0:T(8,128)(2,1)S(1)} %copy-done.4, bf16[128,2048]{1,0:T(8,128)(2,1)S(1)} %copy-done.6, ...), custom_call_target="tpu_custom_call" | custom-call | flops 1 | bytes 1 | tf_op jit(solution)/shard_map/feed_grads_own/pallas_call | solution.py:246
  283.8 4.4 out_grads.1.refs_11_
  288.2 8.0 %attention_backward.1 = (bf16[160,512]{1,0:T(8,128)(2,1)S(1)}, bf16[160,512]{1,0:T(8,128)(2,1)S(1)}, bf16[160,512]{1,0:T(8,128)(2,1)S(1)}, bf16[160,512]{1,0:T(8,128)(2,1)S(1)}) custom-call(s32[4]{0:T(128)S(1)} %pad_add_fusion.at_ref.refs_0_, bf16[128,512]{1,0:T(8,128)(2,1)S(1)} %get-tuple-element.140.c0, bf16[128,512]{1,0:T(8,128)(2,1)S(1)} %collective-permute-done.34.c1, ...), custom_call_target="tpu_custom_call" | custom-call | flops 1 | bytes 1 | tf_op jit(solution)/shard_map/attention_backward/pallas_call | solution.py:246
  300.7 4.5 %collective-permute-done.37.refs_1_ = bf16[160,512]{1,0:T(8,128)(2,1)S(1)} collective-permute-done((bf16[160,512]{1,0:T(8,128)(2,1)S(1)}, bf16[160,512]{1,0:T(8,128)(2,1)S(1)}, u32[]{:S(2)}, u32[]{:S(2)}) %collective-permute-start.37) | collective-permute-done | bytes 163872 | tf_op jit(solution)/shard_map/ppermute | solution.py:24
  309.1 7.1 %head_grads.1 = (bf16[4,4,304,256]{3,2,1,0:T(8,128)(2,1)}, bf16[4,4,304,256]{3,2,1,0:T(8,128)(2,1)}) custom-call(s32[4]{0:T(128)S(1)} %pad_add_fusion.at_ref.refs_0_, bf16[160,512]{1,0:T(8,128)(2,1)S(1)} %get-tuple-element.154.refs_0_, bf16[160,512]{1,0:T(8,128)(2,1)S(1)} %collective-permute-done.37.refs_1_, ...), custom_call_target="tpu_custom_call" | custom-call | flops 1 | bytes 1 | tf_op jit(solution)/shard_map/head_grads/pallas_call | solution.py:246
  316.2 5.0 %all-to-all-start.2 = ((bf16[4,4,352,256]{3,2,1,0:T(8,128)(2,1)}), bf16[4,4,352,256]{3,2,1,0:T(8,128)(2,1)}, u32[]{:S(2)}, u32[]{:S(2)}) async-start(bf16[4,4,352,256]{3,2,1,0:T(8,128)(2,1)} %feed_grads_own.3), calls=%async_computation.2 | async-start | bytes 5767168 | tf_op jit(solution)/shard_map/all_to_all | solution.py:866
  321.2 5.6 %first_part.1 = (bf16[128,2048]{1,0:T(8,128)(2,1)}, bf16[128,2048]{1,0:T(8,128)(2,1)}, bf16[64,2048]{1,0:T(8,128)(2,1)S(1)}, bf16[64,2048]{1,0:T(8,128)(2,1)S(1)}, bf16[128,2048]{1,0:T(8,128)(2,1)}) custom-call(s32[4]{0:T(128)S(1)} %pad_add_fusion.at_ref.refs_0_, bf16[160,512]{1,0:T(8,128)(2,1)S(1)} %get-tuple-element.154.refs_0_, ...), custom_call_target="tpu_custom_call" | custom-call | flops 1 | bytes 1 | tf_op jit(solution)/shard_map/first_part/pallas_call | solution.py:246
  330.1 6.2 %reduce-scatter.4.cloned.1.call-done = bf16[1,704,256]{2,1,0:T(8,128)(2,1)} async-done(((bf16[16,704,256]{2,1,0:T(8,128)(2,1)}), bf16[1,704,256]{2,1,0:T(8,128)(2,1)}) %reduce-scatter.4.cloned.1.call-update) | async-done | bytes 360464
  349.9 17.5 %collective-permute-done.48.refs_2_ = bf16[704,256]{1,0:T(8,128)(2,1)S(1)} collective-permute-done((bf16[704,256]{1,0:T(8,128)(2,1)}, bf16[704,256]{1,0:T(8,128)(2,1)S(1)}, u32[]{:S(2)}, u32[]{:S(2)}) %collective-permute-start.48) | collective-permute-done | bytes 360480 | tf_op jit(solution)/shard_map/ppermute | solution.py:24
  369.5 8.8 %collective-permute-done.50.refs_4_ = bf16[704,256]{1,0:T(8,128)(2,1)S(1)} collective-permute-done((bf16[704,256]{1,0:T(8,128)(2,1)S(1)}, bf16[704,256]{1,0:T(8,128)(2,1)S(1)}, u32[]{:S(2)}, u32[]{:S(2)}) %collective-permute-start.50) | collective-permute-done | bytes 360480 | tf_op jit(solution)/shard_map/ppermute | solution.py:24
  406.6 4.3 collect_gate_up.1
  413.0 8.8 %collective-permute-done.58.refs_2_ = bf16[656,256]{1,0:T(8,128)(2,1)S(1)} collective-permute-done((bf16[656,256]{1,0:T(8,128)(2,1)S(1)}, bf16[656,256]{1,0:T(8,128)(2,1)S(1)}, u32[]{:S(2)}, u32[]{:S(2)}) %collective-permute-start.58) | collective-permute-done | bytes 335904 | tf_op jit(solution)/shard_map/ppermute | solution.py:24
  423.7 4.8 %collective-permute-done.60.refs_4_ = bf16[656,256]{1,0:T(8,128)(2,1)S(1)} collective-permute-done((bf16[656,256]{1,0:T(8,128)(2,1)S(1)}, bf16[656,256]{1,0:T(8,128)(2,1)S(1)}, u32[]{:S(2)}, u32[]{:S(2)}) %collective-permute-start.60) | collective-permute-done | bytes 335904 | tf_op jit(solution)/shard_map/ppermute | solution.py:24
  (290 shorter events, 190.9 us)
Async XLA Ops:
  7.2 141.6 %all-gather.3.cloned.1.call-start = ((), (), s32[]{:S(2)}) async-start(), calls=%async_computation.4 | async-start | bytes 10813440 | tf_op jit(solution)/shard_map/all_gather | solution.py:790
  9.6 23.8 %collective-permute-start.4 = (bf16[224,2048]{1,0:T(8,128)(2,1)S(1)}, bf16[224,2048]{1,0:T(8,128)(2,1)S(1)}, u32[]{:S(2)}, u32[]{:S(2)}) collective-permute-start(bf16[224,2048]{1,0:T(8,128)(2,1)S(1)} %pad_maximum_fusion.3.refs_5_.refs_4_), channel_id=1, source_target_pairs={{0,12},{4,0},{8,4},{12,8},{1,13},{5,1},{9,5},{13,9},{2,14},{6,2},{... | collective-permute-start | bytes 2752520 | tf_op jit(solution)/shard_map/ppermute | solution.py:24
  13.8 24.1 %collective-permute-start.5 = (bf16[224,2048]{1,0:T(8,128)(2,1)S(1)}, bf16[224,2048]{1,0:T(8,128)(2,1)S(1)}, u32[]{:S(2)}, u32[]{:S(2)}) collective-permute-start(bf16[224,2048]{1,0:T(8,128)(2,1)S(1)} %pad_maximum_fusion.3.refs_5_.refs_4_), channel_id=1, source_target_pairs={{0,4},{4,8},{8,12},{12,0},{1,5},{5,9},{9,13},{13,1},{2,6},{6,10},{... | collective-permute-start | bytes 2752520 | tf_op jit(solution)/shard_map/ppermute | solution.py:24
  13.8 25.9 %collective-permute-start.1 = (bf16[128,2048]{1,0:T(8,128)(2,1)S(1)}, bf16[128,2048]{1,0:T(8,128)(2,1)}, u32[]{:S(2)}, u32[]{:S(2)}) collective-permute-start(bf16[128,2048]{1,0:T(8,128)(2,1)S(1)} %copy-done.32), channel_id=1, source_target_pairs={{0,1},{1,2},{2,3},{3,0},{4,5},{5,6},{6,7},{7,4},{8,9},{9,10},{10,1... | collective-permute-start | bytes 1572872 | tf_op jit(solution)/shard_map/ppermute | solution.py:24
  15.4 26.9 %collective-permute-start = (bf16[128,2048]{1,0:T(8,128)(2,1)S(1)}, bf16[128,2048]{1,0:T(8,128)(2,1)}, u32[]{:S(2)}, u32[]{:S(2)}) collective-permute-start(bf16[128,2048]{1,0:T(8,128)(2,1)S(1)} %copy-done.32), channel_id=1, source_target_pairs={{0,3},{1,0},{2,1},{3,2},{4,7},{5,4},{6,5},{7,6},{8,11},{9,8},{10,9... | collective-permute-start | bytes 1572872 | tf_op jit(solution)/shard_map/ppermute | solution.py:24
  34.3 15.7 %collective-permute-start.7 = (bf16[112,2048]{1,0:T(8,128)(2,1)}, bf16[112,2048]{1,0:T(8,128)(2,1)S(1)}, u32[]{:S(2)}, u32[]{:S(2)}) collective-permute-start(bf16[112,2048]{1,0:T(8,128)(2,1)} %slice.144), channel_id=1, source_target_pairs={{0,12},{4,0},{8,4},{12,8},{1,13},{5,1},{9,5},{13,9},{2,14},{6,2},{... | collective-permute-start | bytes 1376264 | tf_op jit(solution)/shard_map/ppermute | solution.py:24
  65.4 28.2 %all-to-all-start = ((bf16[4,128,2048]{2,1,0:T(8,128)(2,1)}), bf16[4,128,2048]{2,1,0:T(8,128)(2,1)}, u32[]{:S(2)}, u32[]{:S(2)}) async-start(bf16[4,128,2048]{2,1,0:T(8,128)(2,1)} %broadcast_in_dim.9), calls=%async_computation | async-start | bytes 4194304 | tf_op jit(solution)/shard_map/all_to_all | solution.py:796
  70.0 266.3 %reduce-scatter.4.cloned.1.call-start = ((), (), s32[]{:S(2)}) async-start(), calls=%async_computation.5 | async-start | bytes 6127616
  75.3 24.1 %collective-permute-start.14 = (bf16[4,64,2048]{2,1,0:T(8,128)(2,1)}, bf16[4,64,2048]{2,1,0:T(8,128)(2,1)S(1)}, u32[]{:S(2)}, u32[]{:S(2)}) collective-permute-start(bf16[4,64,2048]{2,1,0:T(8,128)(2,1)} %pad_maximum_fusion.2.own_ref), channel_id=1, source_target_pairs={{0,16},{16,0},{1,17},{17,1},{2,18},{18,2},{3,19},{19,3},{4,20},{20... | collective-permute-start | bytes 3145736 | tf_op jit(solution)/shard_map/ppermute | solution.py:28
  82.8 16.6 %collective-permute-start.12 = (bf16[128,512]{1,0:T(8,128)(2,1)S(1)}, bf16[128,512]{1,0:T(8,128)(2,1)S(1)}, u32[]{:S(2)}, u32[]{:S(2)}) collective-permute-start(bf16[128,512]{1,0:T(8,128)(2,1)S(1)} %get-tuple-element.106), channel_id=1, source_target_pairs={{0,8},{4,12},{8,0},{12,4},{1,9},{5,13},{9,1},{13,5},{2,10},{6,14},... | collective-permute-start | bytes 393224 | tf_op jit(solution)/shard_map/ppermute | solution.py:24
  114.5 14.3 %collective-permute-start.18 = (bf16[128,2048]{1,0:T(8,128)(2,1)S(1)}, bf16[128,2048]{1,0:T(8,128)(2,1)S(1)}, u32[]{:S(2)}, u32[]{:S(2)}) collective-permute-start(bf16[128,2048]{1,0:T(8,128)(2,1)S(1)} %pad_maximum_fusion.5), channel_id=1, source_target_pairs={{0,3},{1,0},{2,1},{3,2},{4,7},{5,4},{6,5},{7,6},{8,11},{9,8},{10,9... | collective-permute-start | bytes 1572872 | tf_op jit(solution)/shard_map/ppermute | solution.py:24
  118.4 14.0 %collective-permute-start.16 = (bf16[128,2048]{1,0:T(8,128)(2,1)S(1)}, bf16[128,2048]{1,0:T(8,128)(2,1)S(1)}, u32[]{:S(2)}, u32[]{:S(2)}) collective-permute-start(bf16[128,2048]{1,0:T(8,128)(2,1)S(1)} %pad_maximum_fusion.4), channel_id=1, source_target_pairs={{0,1},{1,2},{2,3},{3,0},{4,5},{5,6},{6,7},{7,4},{8,9},{9,10},{10,1... | collective-permute-start | bytes 1572872 | tf_op jit(solution)/shard_map/ppermute | solution.py:24
  203.8 34.8 %collective-permute-start.30 = (bf16[4,4,704,256]{3,2,1,0:T(8,128)(2,1)}, bf16[4,4,704,256]{3,2,1,0:T(8,128)(2,1)S(1)}, u32[]{:S(2)}, u32[]{:S(2)}) collective-permute-start(bf16[4,4,704,256]{3,2,1,0:T(8,128)(2,1)} %feed_grads.2), channel_id=1, source_target_pairs={{0,16},{16,0},{1,17},{17,1},{2,18},{18,2},{3,19},{19,3},{4,20},{20... | collective-permute-start | bytes 17301512 | tf_op jit(solution)/shard_map/ppermute | solution.py:28
  203.9 14.4 %collective-permute-start.27 = (bf16[128,2048]{1,0:T(8,128)(2,1)S(1)}, bf16[128,2048]{1,0:T(8,128)(2,1)S(1)}, u32[]{:S(2)}, u32[]{:S(2)}) collective-permute-start(bf16[128,2048]{1,0:T(8,128)(2,1)S(1)} %pad_maximum_fusion.7), channel_id=1, source_target_pairs={{0,3},{1,0},{2,1},{3,2},{4,7},{5,4},{6,5},{7,6},{8,11},{9,8},{10,9... | collective-permute-start | bytes 1572872 | tf_op jit(solution)/shard_map/ppermute | solution.py:24
  204.9 14.8 %collective-permute-start.26 = (bf16[128,2048]{1,0:T(8,128)(2,1)S(1)}, bf16[128,2048]{1,0:T(8,128)(2,1)S(1)}, u32[]{:S(2)}, u32[]{:S(2)}) collective-permute-start(bf16[128,2048]{1,0:T(8,128)(2,1)S(1)} %pad_maximum_fusion.6), channel_id=1, source_target_pairs={{0,1},{1,2},{2,3},{3,0},{4,5},{5,6},{6,7},{7,4},{8,9},{9,10},{10,1... | collective-permute-start | bytes 1572872 | tf_op jit(solution)/shard_map/ppermute | solution.py:24
  224.1 14.5 %collective-permute-start.29 = (bf16[128,2048]{1,0:T(8,128)(2,1)S(1)}, bf16[128,2048]{1,0:T(8,128)(2,1)S(1)}, u32[]{:S(2)}, u32[]{:S(2)}) collective-permute-start(bf16[128,2048]{1,0:T(8,128)(2,1)S(1)} %get-tuple-element.133.b0), channel_id=1, source_target_pairs={{0,1},{1,2},{2,3},{3,0},{4,5},{5,6},{6,7},{7,4},{8,9},{9,10},{10,1... | collective-permute-start | bytes 1572872 | tf_op jit(solution)/shard_map/ppermute | solution.py:24
  250.2 27.2 %collective-permute-start.33 = (bf16[4,4,352,256]{3,2,1,0:T(8,128)(2,1)}, bf16[4,4,352,256]{3,2,1,0:T(8,128)(2,1)}, u32[]{:S(2)}, u32[]{:S(2)}) collective-permute-start(bf16[4,4,352,256]{3,2,1,0:T(8,128)(2,1)} %feed_grads.3), channel_id=1, source_target_pairs={{0,16},{16,0},{1,17},{17,1},{2,18},{18,2},{3,19},{19,3},{4,20},{20... | collective-permute-start | bytes 8650760 | tf_op jit(solution)/shard_map/ppermute | solution.py:28
  268.1 32.6 %all-to-all-start.1 = ((bf16[4,128,2048]{2,1,0:T(8,128)(2,1)}), bf16[4,128,2048]{2,1,0:T(8,128)(2,1)}, u32[]{:S(2)}, u32[]{:S(2)}) async-start(bf16[4,128,2048]{2,1,0:T(8,128)(2,1)} %down.1), calls=%async_computation.1 | async-start | bytes 4194304 | tf_op jit(solution)/shard_map/all_to_all | solution.py:843
  272.8 15.4 %collective-permute-start.34 = (bf16[128,512]{1,0:T(8,128)(2,1)S(1)}, bf16[128,512]{1,0:T(8,128)(2,1)S(1)}, u32[]{:S(2)}, u32[]{:S(2)}) collective-permute-start(bf16[128,512]{1,0:T(8,128)(2,1)S(1)} %get-tuple-element.141), channel_id=1, source_target_pairs={{0,4},{4,8},{8,12},{12,0},{1,5},{5,9},{9,13},{13,1},{2,6},{6,10},{... | collective-permute-start | bytes 393224 | tf_op jit(solution)/shard_map/ppermute | solution.py:24
  272.9 15.3 %collective-permute-start.35 = (bf16[128,512]{1,0:T(8,128)(2,1)S(1)}, bf16[128,512]{1,0:T(8,128)(2,1)S(1)}, u32[]{:S(2)}, u32[]{:S(2)}) collective-permute-start(bf16[128,512]{1,0:T(8,128)(2,1)S(1)} %get-tuple-element.142), channel_id=1, source_target_pairs={{0,8},{4,12},{8,0},{12,4},{1,9},{5,13},{9,1},{13,5},{2,10},{6,14},... | collective-permute-start | bytes 393224 | tf_op jit(solution)/shard_map/ppermute | solution.py:24
  316.2 24.3 %collective-permute-start.44 = (bf16[4,4,304,256]{3,2,1,0:T(8,128)(2,1)}, bf16[4,4,304,256]{3,2,1,0:T(8,128)(2,1)}, u32[]{:S(2)}, u32[]{:S(2)}) collective-permute-start(bf16[4,4,304,256]{3,2,1,0:T(8,128)(2,1)} %get-tuple-element.161), channel_id=1, source_target_pairs={{0,16},{16,0},{1,17},{17,1},{2,18},{18,2},{3,19},{19,3},{4,20},{20... | collective-permute-start | bytes 7471112 | tf_op jit(solution)/shard_map/ppermute | solution.py:28
  316.2 68.6 %all-to-all-start.2 = ((bf16[4,4,352,256]{3,2,1,0:T(8,128)(2,1)}), bf16[4,4,352,256]{3,2,1,0:T(8,128)(2,1)}, u32[]{:S(2)}, u32[]{:S(2)}) async-start(bf16[4,4,352,256]{3,2,1,0:T(8,128)(2,1)} %feed_grads_own.3), calls=%async_computation.2 | async-start | bytes 5767168 | tf_op jit(solution)/shard_map/all_to_all | solution.py:866
  328.5 19.8 %collective-permute-start.42 = (bf16[64,2048]{1,0:T(8,128)(2,1)S(1)}, bf16[64,2048]{1,0:T(8,128)(2,1)S(1)}, u32[]{:S(2)}, u32[]{:S(2)}) collective-permute-start(bf16[64,2048]{1,0:T(8,128)(2,1)S(1)} %get-tuple-element.159), channel_id=1, source_target_pairs={{0,3},{1,0},{2,1},{3,2},{4,7},{5,4},{6,5},{7,6},{8,11},{9,8},{10,9... | collective-permute-start | bytes 786440 | tf_op jit(solution)/shard_map/ppermute | solution.py:24
  336.2 31.2 %collective-permute-start.48 = (bf16[704,256]{1,0:T(8,128)(2,1)}, bf16[704,256]{1,0:T(8,128)(2,1)S(1)}, u32[]{:S(2)}, u32[]{:S(2)}) collective-permute-start(bf16[704,256]{1,0:T(8,128)(2,1)} %bitcast.68), channel_id=1, source_target_pairs={{0,96},{32,0},{64,32},{96,64},{1,97},{33,1},{65,33},{97,65},{2,98}... | collective-permute-start | bytes 1081352 | tf_op jit(solution)/shard_map/ppermute | solution.py:24
  344.0 35.7 %collective-permute-start.45 = (bf16[4,304,256]{2,1,0:T(8,128)(2,1)S(1)}, bf16[4,304,256]{2,1,0:T(8,128)(2,1)S(1)}, u32[]{:S(2)}, u32[]{:S(2)}) collective-permute-start(bf16[4,304,256]{2,1,0:T(8,128)(2,1)S(1)} %get-tuple-element.163), channel_id=1, source_target_pairs={{0,4},{4,8},{8,12},{12,0},{1,5},{5,9},{9,13},{13,1},{2,6},{6,10},{... | collective-permute-start | bytes 1867784 | tf_op jit(solution)/shard_map/ppermute | solution.py:24
  344.4 35.2 %collective-permute-start.46 = (bf16[4,304,256]{2,1,0:T(8,128)(2,1)S(1)}, bf16[4,304,256]{2,1,0:T(8,128)(2,1)S(1)}, u32[]{:S(2)}, u32[]{:S(2)}) collective-permute-start(bf16[4,304,256]{2,1,0:T(8,128)(2,1)S(1)} %get-tuple-element.164), channel_id=1, source_target_pairs={{0,8},{4,12},{8,0},{12,4},{1,9},{5,13},{9,1},{13,5},{2,10},{6,14},... | collective-permute-start | bytes 1867784 | tf_op jit(solution)/shard_map/ppermute | solution.py:24
  346.5 33.1 %collective-permute-start.47 = (bf16[4,304,256]{2,1,0:T(8,128)(2,1)}, bf16[4,304,256]{2,1,0:T(8,128)(2,1)S(1)}, u32[]{:S(2)}, u32[]{:S(2)}) collective-permute-start(bf16[4,304,256]{2,1,0:T(8,128)(2,1)} %get-tuple-element.165), channel_id=1, source_target_pairs={{0,12},{4,0},{8,4},{12,8},{1,13},{5,1},{9,5},{13,9},{2,14},{6,2},{... | collective-permute-start | bytes 1867784 | tf_op jit(solution)/shard_map/ppermute | solution.py:24
  348.3 21.2 %collective-permute-start.49 = (bf16[704,256]{1,0:T(8,128)(2,1)S(1)}, bf16[704,256]{1,0:T(8,128)(2,1)S(1)}, u32[]{:S(2)}, u32[]{:S(2)}) collective-permute-start(bf16[704,256]{1,0:T(8,128)(2,1)S(1)} %bitcast.69), channel_id=1, source_target_pairs={{0,64},{32,96},{64,0},{96,32},{1,65},{33,97},{65,1},{97,33},{2,66}... | collective-permute-start | bytes 1081352 | tf_op jit(solution)/shard_map/ppermute | solution.py:24
  379.6 26.9 %collective-permute-start.57 = (bf16[4,704,256]{2,1,0:T(8,128)(2,1)}, bf16[4,704,256]{2,1,0:T(8,128)(2,1)}, u32[]{:S(2)}, u32[]{:S(2)}) collective-permute-start(bf16[4,704,256]{2,1,0:T(8,128)(2,1)} %pad_maximum_fusion), channel_id=1, source_target_pairs={{0,16},{16,0},{1,17},{17,1},{2,18},{18,2},{3,19},{19,3},{4,20},{20... | collective-permute-start | bytes 4325384 | tf_op jit(solution)/shard_map/ppermute | solution.py:28
  392.1 18.8 %collective-permute-start.41 = (bf16[128,2048]{1,0:T(8,128)(2,1)S(1)}, bf16[128,2048]{1,0:T(8,128)(2,1)S(1)}, u32[]{:S(2)}, u32[]{:S(2)}) collective-permute-start(bf16[128,2048]{1,0:T(8,128)(2,1)S(1)} %copy-done.44), channel_id=1, source_target_pairs={{0,1},{1,2},{2,3},{3,0},{4,5},{5,6},{6,7},{7,4},{8,9},{9,10},{10,1... | collective-permute-start | bytes 1572872 | tf_op jit(solution)/shard_map/ppermute | solution.py:24
  393.7 17.2 %collective-permute-start.43 = (bf16[128,2048]{1,0:T(8,128)(2,1)S(1)}, bf16[128,2048]{1,0:T(8,128)(2,1)S(1)}, u32[]{:S(2)}, u32[]{:S(2)}) collective-permute-start(bf16[128,2048]{1,0:T(8,128)(2,1)S(1)} %pad_maximum_fusion.9), channel_id=1, source_target_pairs={{0,3},{1,0},{2,1},{3,2},{4,7},{5,4},{6,5},{7,6},{8,11},{9,8},{10,9... | collective-permute-start | bytes 1572872 | tf_op jit(solution)/shard_map/ppermute | solution.py:24
  411.8 16.8 %collective-permute-start.60 = (bf16[656,256]{1,0:T(8,128)(2,1)S(1)}, bf16[656,256]{1,0:T(8,128)(2,1)S(1)}, u32[]{:S(2)}, u32[]{:S(2)}) collective-permute-start(bf16[656,256]{1,0:T(8,128)(2,1)S(1)} %pad_maximum_fusion.10.refs_1_), channel_id=1, source_target_pairs={{0,32},{32,64},{64,96},{96,0},{1,33},{33,65},{65,97},{97,1},{2,34}... | collective-permute-start | bytes 1007624 | tf_op jit(solution)/shard_map/ppermute | solution.py:24
  (90 other events, 905.2 us)
Sparse Core Ops, SparseCore 0:
  52.4 93.8 all-gather.2
  250.3 85.8 reduce-scatter.3

commit v4 on v3

--- a/solution.py
+++ b/solution.py
@@ -884,11 +884,13 @@
 
     grad_gate, grad_up = collect(order, at, gu_blocks, "collect_gate_up", HID, HID)
     rest_sum = jnp.concatenate([head_sum, down_sum], axis=0)
-    rest_sum = after(rest_sum, grad_gate, from_back, from_ahead)
+    rest_sum = after(rest_sum, from_back, from_ahead)
+    rest_blocks = gathered(rest_sum, "x")
+    rest_blocks = lax.optimization_barrier((*rest_blocks, grad_gate))[:4]
     grad_out, grad_query, grad_key, grad_value, gains, grad_down = collect(
         order,
         at,
-        gathered(rest_sum, "x"),
+        list(rest_blocks),
         "collect_rest",
         HEAD_V,
         FEAT,

time: 462 us -> 455 us (0.985)
  waiting for transfers between devices: 171 us -> 163 us
    unnamed x3, waiting for transfers between devices: 6.2 us -> 0.05 us
  transfers between devices with their start and end apart: 70 -> 70, of which waited for: 34 -> 38; matrix products, arithmetic and copies ran while one was open for 7% -> 8% of each run, Pallas kernels for 18% -> 18%
where the time goes in v4:
time: 455 us; the launch traced here: 447 us
  waiting for transfers between devices  163 us (36%)
  Pallas kernels  124 us (27%)
  starting transfers between devices  101 us (22%)
  local copies, waits for them, and re-layouts  22.7 us (5%)
  other arithmetic  22 us (5%)
  between operations  15 us (3%)
    ppermute x58, waiting for transfers between devices, shifted(): return lax.ppermute(array, axis, [(i, (i + by) % 4) for i in range(4)])  155 us
    pallas_call x19, Pallas kernels, call(): pl.pallas_call(kernel, out_shape=out_shape, compiler_params=pltpu.Compile...  124 us
    ppermute x58, starting transfers between devices, shifted(): return lax.ppermute(array, axis, [(i, (i + by) % 4) for i in range(4)])  85.7 us
  transfers between devices with their start and end apart: 70, of which 38 were waited for; matrix products, arithmetic and copies ran while one was open for 8% of the time, Pallas kernels for 18%

profile of v4, /device:TPU:0, one launch (start us, length us, event | category | flops | bytes accessed | tf_op | source)
XLA Modules:
  0.0 447.0 jit_solution(12694686876540683974)
XLA Ops:
  17.1 16.4 %collective-permute-done.4.refs_6_.refs_5_ = bf16[224,2048]{1,0:T(8,128)(2,1)S(1)} collective-permute-done((bf16[224,2048]{1,0:T(8,128)(2,1)S(1)}, bf16[224,2048]{1,0:T(8,128)(2,1)S(1)}, u32[]{:S(2)}, u32[]{:S(2)}) %collective-permute-start.4) | collective-permute-done | bytes 917536 | tf_op jit(solution)/shard_map/ppermute | solution.py:24
  54.4 6.8 %project.1 = (bf16[160,512]{1,0:T(8,128)(2,1)S(1)}, bf16[160,512]{1,0:T(8,128)(2,1)S(1)}, bf16[160,512]{1,0:T(8,128)(2,1)S(1)}, bf16[160,512]{1,0:T(8,128)(2,1)S(1)}, bf16[512,2048]{1,0:T(8,128)(2,1)}) custom-call(s32[4]{0:T(128)S(1)} %pad_add_fusion.at_ref.refs_0_, bf16[128,2048]{1,0:T(8,128)(2,1)} %token_ref.1, ...), custom_call_target="tpu_custom_call" | custom-call | flops 1 | bytes 1 | tf_op jit(solution)/shard_map/project/pallas_call | solution.py:246
  65.4 4.6 %all-to-all-start = ((bf16[4,128,2048]{2,1,0:T(8,128)(2,1)}), bf16[4,128,2048]{2,1,0:T(8,128)(2,1)}, u32[]{:S(2)}, u32[]{:S(2)}) async-start(bf16[4,128,2048]{2,1,0:T(8,128)(2,1)} %broadcast_in_dim.9), calls=%async_computation | async-start | bytes 4194304 | tf_op jit(solution)/shard_map/all_to_all | solution.py:796
  76.2 5.7 %attention_forward.1 = (bf16[128,512]{1,0:T(8,128)(2,1)S(1)}, bf16[128,512]{1,0:T(8,128)(2,1)S(1)}, bf16[128,512]{1,0:T(8,128)(2,1)S(1)}, bf16[128,512]{1,0:T(8,...) custom-call(s32[4]{0:T(128)S(1)} %pad_add_fusion.at_ref.refs_0_, ...), custom_call_target="tpu_custom_call" | custom-call | flops 1 | bytes 1 | tf_op jit(solution)/shard_map/attention_forward/pallas_call | solution.py:246
  89.4 4.2 all-to-all-done
  93.6 5.8 %collective-permute-done.12.m2 = bf16[128,512]{1,0:T(8,128)(2,1)S(1)} collective-permute-done((bf16[128,512]{1,0:T(8,128)(2,1)S(1)}, bf16[128,512]{1,0:T(8,128)(2,1)S(1)}, u32[]{:S(2)}, u32[]{:S(2)}) %collective-permute-start.12) | collective-permute-done | bytes 131104 | tf_op jit(solution)/shard_map/ppermute | solution.py:24
  107.6 5.6 %collective-permute-done.17 = bf16[64,2048]{1,0:T(8,128)(2,1)S(1)} collective-permute-done((bf16[64,2048]{1,0:T(8,128)(2,1)S(1)}, bf16[64,2048]{1,0:T(8,128)(2,1)S(1)}, u32[]{:S(2)}, u32[]{:S(2)}) %collective-permute-start.17) | collective-permute-done | bytes 262176 | tf_op jit(solution)/shard_map/ppermute | solution.py:24
  118.4 10.3 %collective-permute-done.18.p3 = bf16[128,2048]{1,0:T(8,128)(2,1)S(1)} collective-permute-done((bf16[128,2048]{1,0:T(8,128)(2,1)S(1)}, bf16[128,2048]{1,0:T(8,128)(2,1)S(1)}, u32[]{:S(2)}, u32[]{:S(2)}) %collective-permute-start.18) | collective-permute-done | bytes 524320 | tf_op jit(solution)/shard_map/ppermute | solution.py:24
  136.9 9.9 %collective-permute-done.19.refs_1_.refs_4_ = bf16[128,2048]{1,0:T(8,128)(2,1)S(1)} collective-permute-done((bf16[128,2048]{1,0:T(8,128)(2,1)S(1)}, bf16[128,2048]{1,0:T(8,128)(2,1)S(1)}, u32[]{:S(2)}, u32[]{:S(2)}) %collective-permute-start.19) | collective-permute-done | bytes 524320 | tf_op jit(solution)/shard_map/ppermute | solution.py:24
  162.7 23.7 %feed.1 = (bf16[4,352,512]{2,1,0:T(8,128)(2,1)}, bf16[4,352,512]{2,1,0:T(8,128)(2,1)}, bf16[4,352,512]{2,1,0:T(8,128)(2,1)}, bf16[128,2048]{1,0:T(8,128)(2,1)}, ...) custom-call(s32[4]{0:T(128)S(1)} %pad_add_fusion.at_ref.refs_0_, ...), custom_call_target="tpu_custom_call" | custom-call | flops 1 | bytes 1 | tf_op jit(solution)/shard_map/feed/pallas_call | solution.py:246
  188.6 6.3 %collective-permute-done.25 = bf16[64,2048]{1,0:T(8,128)(2,1)S(1)} collective-permute-done((bf16[64,2048]{1,0:T(8,128)(2,1)S(1)}, bf16[64,2048]{1,0:T(8,128)(2,1)S(1)}, u32[]{:S(2)}, u32[]{:S(2)}) %collective-permute-start.25) | collective-permute-done | bytes 262176 | tf_op jit(solution)/shard_map/ppermute | solution.py:24
  196.2 7.6 %feed_grads.2 = bf16[4,4,704,256]{3,2,1,0:T(8,128)(2,1)} custom-call(s32[4]{0:T(128)S(1)} %pad_add_fusion.at_ref.refs_0_, bf16[4,352,512]{2,1,0:T(8,128)(2,1)} %get-tuple-element.135.refs_1_, bf16[4,352,512]{2,1,0:T(8,128)(2,1)} %get-tuple-element.129.refs_2_, bf16[128,2048]{1,0:T(8,128)(2,1)S(1)} %copy-done.12, bf16[128,2048]{1,0:T(8,128)(2,1)S(1)} %copy-done.8, ...), custom_call_target="tpu_custom_call" | custom-call | flops 1 | bytes 1 | tf_op jit(solution)/shard_map/feed_grads/pallas_call | solution.py:246
  206.2 5.7 %feed_grads.3 = bf16[4,4,352,256]{3,2,1,0:T(8,128)(2,1)} custom-call(s32[4]{0:T(128)S(1)} %pad_add_fusion.at_ref.refs_0_, bf16[4,352,512]{2,1,0:T(8,128)(2,1)} %get-tuple-element.142.refs_1_.hidden_ref, bf16[128,2048]{1,0:T(8,128)(2,1)S(1)} %copy-done.3, bf16[128,2048]{1,0:T(8,128)(2,1)S(1)} %copy-done.6, ...), custom_call_target="tpu_custom_call" | custom-call | flops 1 | bytes 1 | tf_op jit(solution)/shard_map/feed_grads/pallas_call | solution.py:246
  211.9 6.4 %collective-permute-done.27.s3 = bf16[128,2048]{1,0:T(8,128)(2,1)S(1)} collective-permute-done((bf16[128,2048]{1,0:T(8,128)(2,1)S(1)}, bf16[128,2048]{1,0:T(8,128)(2,1)S(1)}, u32[]{:S(2)}, u32[]{:S(2)}) %collective-permute-start.27) | collective-permute-done | bytes 524320 | tf_op jit(solution)/shard_map/ppermute | solution.py:24
  225.2 10.9 %collective-permute-done.28.b1 = bf16[128,2048]{1,0:T(8,128)(2,1)S(1)} collective-permute-done((bf16[128,2048]{1,0:T(8,128)(2,1)S(1)}, bf16[128,2048]{1,0:T(8,128)(2,1)S(1)}, u32[]{:S(2)}, u32[]{:S(2)}) %collective-permute-start.28) | collective-permute-done | bytes 524320 | tf_op jit(solution)/shard_map/ppermute | solution.py:24
  241.2 9.0 %feed_grads_own.2 = bf16[4,4,704,256]{3,2,1,0:T(8,128)(2,1)} custom-call(s32[4]{0:T(128)S(1)} %pad_add_fusion.at_ref.refs_0_, bf16[4,352,512]{2,1,0:T(8,128)(2,1)} %get-tuple-element.135.refs_1_, bf16[4,352,512]{2,1,0:T(8,128)(2,1)} %get-tuple-element.129.refs_2_, bf16[128,2048]{1,0:T(8,128)(2,1)S(1)} %copy-done.12, bf16[128,2048]{1,0:T(8,128)(2,1)S(1)} %copy-done.8, ...), custom_call_target="tpu_custom_call" | custom-call | flops 1 | bytes 1 | tf_op jit(solution)/shard_map/feed_grads_own/pallas_call | solution.py:246
  255.7 9.0 %down.1 = bf16[4,128,2048]{2,1,0:T(8,128)(2,1)} custom-call(s32[4]{0:T(128)S(1)} %pad_add_fusion.at_ref.refs_0_, bf16[4,352,512]{2,1,0:T(8,128)(2,1)S(1)} %copy-done.5, bf16[4,1056,1024]{2,1,0:T(8,128)(2,1)} %bitcast.86, bf16[4,1056,1024]{2,1,0:T(8,128)(2,1)} %collective-permute-done.23.refs_11_.other_ref), custom_call_target="tpu_custom_call" | custom-call | flops 1 | bytes 1 | tf_op jit(solution)/shard_map/down/pallas_call | solution.py:246
  268.1 4.6 %all-to-all-start.1 = ((bf16[4,128,2048]{2,1,0:T(8,128)(2,1)}), bf16[4,128,2048]{2,1,0:T(8,128)(2,1)}, u32[]{:S(2)}, u32[]{:S(2)}) async-start(bf16[4,128,2048]{2,1,0:T(8,128)(2,1)} %down.1), calls=%async_computation.1 | async-start | bytes 4194304 | tf_op jit(solution)/shard_map/all_to_all | solution.py:843
  277.5 6.3 %feed_grads_own.3 = bf16[4,4,352,256]{3,2,1,0:T(8,128)(2,1)} custom-call(s32[4]{0:T(128)S(1)} %pad_add_fusion.at_ref.refs_0_, bf16[4,352,512]{2,1,0:T(8,128)(2,1)} %get-tuple-element.142.refs_1_.hidden_ref, bf16[128,2048]{1,0:T(8,128)(2,1)S(1)} %copy-done.4, bf16[128,2048]{1,0:T(8,128)(2,1)S(1)} %copy-done.6, ...), custom_call_target="tpu_custom_call" | custom-call | flops 1 | bytes 1 | tf_op jit(solution)/shard_map/feed_grads_own/pallas_call | solution.py:246
  283.8 4.4 out_grads.1.refs_11_
  288.2 8.0 %attention_backward.1 = (bf16[160,512]{1,0:T(8,128)(2,1)S(1)}, bf16[160,512]{1,0:T(8,128)(2,1)S(1)}, bf16[160,512]{1,0:T(8,128)(2,1)S(1)}, bf16[160,512]{1,0:T(8,128)(2,1)S(1)}) custom-call(s32[4]{0:T(128)S(1)} %pad_add_fusion.at_ref.refs_0_, bf16[128,512]{1,0:T(8,128)(2,1)S(1)} %get-tuple-element.144.c0, bf16[128,512]{1,0:T(8,128)(2,1)S(1)} %collective-permute-done.34.c1, ...), custom_call_target="tpu_custom_call" | custom-call | flops 1 | bytes 1 | tf_op jit(solution)/shard_map/attention_backward/pallas_call | solution.py:246
  300.7 4.5 %collective-permute-done.37.refs_1_ = bf16[160,512]{1,0:T(8,128)(2,1)S(1)} collective-permute-done((bf16[160,512]{1,0:T(8,128)(2,1)S(1)}, bf16[160,512]{1,0:T(8,128)(2,1)S(1)}, u32[]{:S(2)}, u32[]{:S(2)}) %collective-permute-start.37) | collective-permute-done | bytes 163872 | tf_op jit(solution)/shard_map/ppermute | solution.py:24
  309.1 7.1 %head_grads.1 = (bf16[4,4,304,256]{3,2,1,0:T(8,128)(2,1)}, bf16[4,4,304,256]{3,2,1,0:T(8,128)(2,1)}) custom-call(s32[4]{0:T(128)S(1)} %pad_add_fusion.at_ref.refs_0_, bf16[160,512]{1,0:T(8,128)(2,1)S(1)} %get-tuple-element.158.refs_0_, bf16[160,512]{1,0:T(8,128)(2,1)S(1)} %collective-permute-done.37.refs_1_, ...), custom_call_target="tpu_custom_call" | custom-call | flops 1 | bytes 1 | tf_op jit(solution)/shard_map/head_grads/pallas_call | solution.py:246
  316.2 5.0 %all-to-all-start.2 = ((bf16[4,4,352,256]{3,2,1,0:T(8,128)(2,1)}), bf16[4,4,352,256]{3,2,1,0:T(8,128)(2,1)}, u32[]{:S(2)}, u32[]{:S(2)}) async-start(bf16[4,4,352,256]{3,2,1,0:T(8,128)(2,1)} %feed_grads_own.3), calls=%async_computation.2 | async-start | bytes 5767168 | tf_op jit(solution)/shard_map/all_to_all | solution.py:866
  321.2 5.6 %first_part.1 = (bf16[128,2048]{1,0:T(8,128)(2,1)}, bf16[128,2048]{1,0:T(8,128)(2,1)}, bf16[64,2048]{1,0:T(8,128)(2,1)S(1)}, bf16[64,2048]{1,0:T(8,128)(2,1)S(1)}, bf16[128,2048]{1,0:T(8,128)(2,1)}) custom-call(s32[4]{0:T(128)S(1)} %pad_add_fusion.at_ref.refs_0_, bf16[160,512]{1,0:T(8,128)(2,1)S(1)} %get-tuple-element.158.refs_0_, ...), custom_call_target="tpu_custom_call" | custom-call | flops 1 | bytes 1 | tf_op jit(solution)/shard_map/first_part/pallas_call | solution.py:246
  345.3 5.5 %collective-permute-done.45 = bf16[4,304,256]{2,1,0:T(8,128)(2,1)} collective-permute-done((bf16[4,304,256]{2,1,0:T(8,128)(2,1)S(1)}, bf16[4,304,256]{2,1,0:T(8,128)(2,1)}, u32[]{:S(2)}, u32[]{:S(2)}) %collective-permute-start.45) | collective-permute-done | bytes 622624 | tf_op jit(solution)/shard_map/ppermute | solution.py:24
  354.6 10.6 %collective-permute-done.46 = bf16[4,304,256]{2,1,0:T(8,128)(2,1)} collective-permute-done((bf16[4,304,256]{2,1,0:T(8,128)(2,1)S(1)}, bf16[4,304,256]{2,1,0:T(8,128)(2,1)}, u32[]{:S(2)}, u32[]{:S(2)}) %collective-permute-start.46) | collective-permute-done | bytes 622624 | tf_op jit(solution)/shard_map/ppermute | solution.py:24
  370.4 5.8 %collective-permute-done.50.refs_4_ = bf16[704,256]{1,0:T(8,128)(2,1)S(1)} collective-permute-done((bf16[704,256]{1,0:T(8,128)(2,1)}, bf16[704,256]{1,0:T(8,128)(2,1)S(1)}, u32[]{:S(2)}, u32[]{:S(2)}) %collective-permute-start.50) | collective-permute-done | bytes 360480 | tf_op jit(solution)/shard_map/ppermute | solution.py:24
  385.1 4.5 collective-permute-done.51
  406.5 4.3 collect_gate_up.1
  410.8 4.5 %collective-permute-done.57.refs_2_ = bf16[656,256]{1,0:T(8,128)(2,1)S(1)} collective-permute-done((bf16[656,256]{1,0:T(8,128)(2,1)S(1)}, bf16[656,256]{1,0:T(8,128)(2,1)S(1)}, u32[]{:S(2)}, u32[]{:S(2)}) %collective-permute-start.57) | collective-permute-done | bytes 335904 | tf_op jit(solution)/shard_map/ppermute | solution.py:24
  416.8 4.8 %collective-permute-done.59.refs_4_ = bf16[656,256]{1,0:T(8,128)(2,1)S(1)} collective-permute-done((bf16[656,256]{1,0:T(8,128)(2,1)S(1)}, bf16[656,256]{1,0:T(8,128)(2,1)S(1)}, u32[]{:S(2)}, u32[]{:S(2)}) %collective-permute-start.59) | collective-permute-done | bytes 335904 | tf_op jit(solution)/shard_map/ppermute | solution.py:24
  (290 shorter events, 198.4 us)
Async XLA Ops:
  7.2 141.6 %all-gather.3.cloned.1.call-start = ((), (), s32[]{:S(2)}) async-start(), calls=%async_computation.4 | async-start | bytes 10813440 | tf_op jit(solution)/shard_map/all_gather | solution.py:790
  9.6 23.8 %collective-permute-start.4 = (bf16[224,2048]{1,0:T(8,128)(2,1)S(1)}, bf16[224,2048]{1,0:T(8,128)(2,1)S(1)}, u32[]{:S(2)}, u32[]{:S(2)}) collective-permute-start(bf16[224,2048]{1,0:T(8,128)(2,1)S(1)} %pad_maximum_fusion.3.refs_5_.refs_4_), channel_id=1, source_target_pairs={{0,12},{4,0},{8,4},{12,8},{1,13},{5,1},{9,5},{13,9},{2,14},{6,2},{... | collective-permute-start | bytes 2752520 | tf_op jit(solution)/shard_map/ppermute | solution.py:24
  13.8 24.1 %collective-permute-start.5 = (bf16[224,2048]{1,0:T(8,128)(2,1)S(1)}, bf16[224,2048]{1,0:T(8,128)(2,1)S(1)}, u32[]{:S(2)}, u32[]{:S(2)}) collective-permute-start(bf16[224,2048]{1,0:T(8,128)(2,1)S(1)} %pad_maximum_fusion.3.refs_5_.refs_4_), channel_id=1, source_target_pairs={{0,4},{4,8},{8,12},{12,0},{1,5},{5,9},{9,13},{13,1},{2,6},{6,10},{... | collective-permute-start | bytes 2752520 | tf_op jit(solution)/shard_map/ppermute | solution.py:24
  13.8 25.9 %collective-permute-start.1 = (bf16[128,2048]{1,0:T(8,128)(2,1)S(1)}, bf16[128,2048]{1,0:T(8,128)(2,1)}, u32[]{:S(2)}, u32[]{:S(2)}) collective-permute-start(bf16[128,2048]{1,0:T(8,128)(2,1)S(1)} %copy-done.32), channel_id=1, source_target_pairs={{0,1},{1,2},{2,3},{3,0},{4,5},{5,6},{6,7},{7,4},{8,9},{9,10},{10,1... | collective-permute-start | bytes 1572872 | tf_op jit(solution)/shard_map/ppermute | solution.py:24
  15.4 26.9 %collective-permute-start = (bf16[128,2048]{1,0:T(8,128)(2,1)S(1)}, bf16[128,2048]{1,0:T(8,128)(2,1)}, u32[]{:S(2)}, u32[]{:S(2)}) collective-permute-start(bf16[128,2048]{1,0:T(8,128)(2,1)S(1)} %copy-done.32), channel_id=1, source_target_pairs={{0,3},{1,0},{2,1},{3,2},{4,7},{5,4},{6,5},{7,6},{8,11},{9,8},{10,9... | collective-permute-start | bytes 1572872 | tf_op jit(solution)/shard_map/ppermute | solution.py:24
  34.3 15.7 %collective-permute-start.7 = (bf16[112,2048]{1,0:T(8,128)(2,1)}, bf16[112,2048]{1,0:T(8,128)(2,1)S(1)}, u32[]{:S(2)}, u32[]{:S(2)}) collective-permute-start(bf16[112,2048]{1,0:T(8,128)(2,1)} %slice.144), channel_id=1, source_target_pairs={{0,12},{4,0},{8,4},{12,8},{1,13},{5,1},{9,5},{13,9},{2,14},{6,2},{... | collective-permute-start | bytes 1376264 | tf_op jit(solution)/shard_map/ppermute | solution.py:24
  65.4 28.2 %all-to-all-start = ((bf16[4,128,2048]{2,1,0:T(8,128)(2,1)}), bf16[4,128,2048]{2,1,0:T(8,128)(2,1)}, u32[]{:S(2)}, u32[]{:S(2)}) async-start(bf16[4,128,2048]{2,1,0:T(8,128)(2,1)} %broadcast_in_dim.9), calls=%async_computation | async-start | bytes 4194304 | tf_op jit(solution)/shard_map/all_to_all | solution.py:796
  70.0 271.4 %reduce-scatter.4.cloned.1.call-start = ((), (), s32[]{:S(2)}) async-start(), calls=%async_computation.5 | async-start | bytes 6127616
  75.3 24.1 %collective-permute-start.14 = (bf16[4,64,2048]{2,1,0:T(8,128)(2,1)}, bf16[4,64,2048]{2,1,0:T(8,128)(2,1)S(1)}, u32[]{:S(2)}, u32[]{:S(2)}) collective-permute-start(bf16[4,64,2048]{2,1,0:T(8,128)(2,1)} %pad_maximum_fusion.2.own_ref), channel_id=1, source_target_pairs={{0,16},{16,0},{1,17},{17,1},{2,18},{18,2},{3,19},{19,3},{4,20},{20... | collective-permute-start | bytes 3145736 | tf_op jit(solution)/shard_map/ppermute | solution.py:28
  82.8 16.6 %collective-permute-start.12 = (bf16[128,512]{1,0:T(8,128)(2,1)S(1)}, bf16[128,512]{1,0:T(8,128)(2,1)S(1)}, u32[]{:S(2)}, u32[]{:S(2)}) collective-permute-start(bf16[128,512]{1,0:T(8,128)(2,1)S(1)} %get-tuple-element.110), channel_id=1, source_target_pairs={{0,8},{4,12},{8,0},{12,4},{1,9},{5,13},{9,1},{13,5},{2,10},{6,14},... | collective-permute-start | bytes 393224 | tf_op jit(solution)/shard_map/ppermute | solution.py:24
  114.5 14.3 %collective-permute-start.18 = (bf16[128,2048]{1,0:T(8,128)(2,1)S(1)}, bf16[128,2048]{1,0:T(8,128)(2,1)S(1)}, u32[]{:S(2)}, u32[]{:S(2)}) collective-permute-start(bf16[128,2048]{1,0:T(8,128)(2,1)S(1)} %pad_maximum_fusion.5), channel_id=1, source_target_pairs={{0,3},{1,0},{2,1},{3,2},{4,7},{5,4},{6,5},{7,6},{8,11},{9,8},{10,9... | collective-permute-start | bytes 1572872 | tf_op jit(solution)/shard_map/ppermute | solution.py:24
  118.4 14.0 %collective-permute-start.16 = (bf16[128,2048]{1,0:T(8,128)(2,1)S(1)}, bf16[128,2048]{1,0:T(8,128)(2,1)S(1)}, u32[]{:S(2)}, u32[]{:S(2)}) collective-permute-start(bf16[128,2048]{1,0:T(8,128)(2,1)S(1)} %pad_maximum_fusion.4), channel_id=1, source_target_pairs={{0,1},{1,2},{2,3},{3,0},{4,5},{5,6},{6,7},{7,4},{8,9},{9,10},{10,1... | collective-permute-start | bytes 1572872 | tf_op jit(solution)/shard_map/ppermute | solution.py:24
  148.9 13.9 %collective-permute-start.23 = (bf16[4,1056,1024]{2,1,0:T(8,128)(2,1)}, bf16[4,1056,1024]{2,1,0:T(8,128)(2,1)}, u32[]{:S(2)}, u32[]{:S(2)}) collective-permute-start(bf16[4,1056,1024]{2,1,0:T(8,128)(2,1)} %bitcast.84), channel_id=1, source_target_pairs={{0,16},{16,0},{1,17},{17,1},{2,18},{18,2},{3,19},{19,3},{4,20},{20... | collective-permute-start | bytes 25952264 | tf_op jit(solution)/shard_map/ppermute | solution.py:28
  203.8 34.8 %collective-permute-start.30 = (bf16[4,4,704,256]{3,2,1,0:T(8,128)(2,1)}, bf16[4,4,704,256]{3,2,1,0:T(8,128)(2,1)S(1)}, u32[]{:S(2)}, u32[]{:S(2)}) collective-permute-start(bf16[4,4,704,256]{3,2,1,0:T(8,128)(2,1)} %feed_grads.2), channel_id=1, source_target_pairs={{0,16},{16,0},{1,17},{17,1},{2,18},{18,2},{3,19},{19,3},{4,20},{20... | collective-permute-start | bytes 17301512 | tf_op jit(solution)/shard_map/ppermute | solution.py:28
  203.9 14.4 %collective-permute-start.27 = (bf16[128,2048]{1,0:T(8,128)(2,1)S(1)}, bf16[128,2048]{1,0:T(8,128)(2,1)S(1)}, u32[]{:S(2)}, u32[]{:S(2)}) collective-permute-start(bf16[128,2048]{1,0:T(8,128)(2,1)S(1)} %pad_maximum_fusion.7), channel_id=1, source_target_pairs={{0,3},{1,0},{2,1},{3,2},{4,7},{5,4},{6,5},{7,6},{8,11},{9,8},{10,9... | collective-permute-start | bytes 1572872 | tf_op jit(solution)/shard_map/ppermute | solution.py:24
  204.9 14.8 %collective-permute-start.26 = (bf16[128,2048]{1,0:T(8,128)(2,1)S(1)}, bf16[128,2048]{1,0:T(8,128)(2,1)S(1)}, u32[]{:S(2)}, u32[]{:S(2)}) collective-permute-start(bf16[128,2048]{1,0:T(8,128)(2,1)S(1)} %pad_maximum_fusion.6), channel_id=1, source_target_pairs={{0,1},{1,2},{2,3},{3,0},{4,5},{5,6},{6,7},{7,4},{8,9},{9,10},{10,1... | collective-permute-start | bytes 1572872 | tf_op jit(solution)/shard_map/ppermute | solution.py:24
  224.1 14.5 %collective-permute-start.29 = (bf16[128,2048]{1,0:T(8,128)(2,1)S(1)}, bf16[128,2048]{1,0:T(8,128)(2,1)S(1)}, u32[]{:S(2)}, u32[]{:S(2)}) collective-permute-start(bf16[128,2048]{1,0:T(8,128)(2,1)S(1)} %get-tuple-element.137.b0), channel_id=1, source_target_pairs={{0,1},{1,2},{2,3},{3,0},{4,5},{5,6},{6,7},{7,4},{8,9},{9,10},{10,1... | collective-permute-start | bytes 1572872 | tf_op jit(solution)/shard_map/ppermute | solution.py:24
  250.2 27.2 %collective-permute-start.33 = (bf16[4,4,352,256]{3,2,1,0:T(8,128)(2,1)}, bf16[4,4,352,256]{3,2,1,0:T(8,128)(2,1)}, u32[]{:S(2)}, u32[]{:S(2)}) collective-permute-start(bf16[4,4,352,256]{3,2,1,0:T(8,128)(2,1)} %feed_grads.3), channel_id=1, source_target_pairs={{0,16},{16,0},{1,17},{17,1},{2,18},{18,2},{3,19},{19,3},{4,20},{20... | collective-permute-start | bytes 8650760 | tf_op jit(solution)/shard_map/ppermute | solution.py:28
  268.1 32.6 %all-to-all-start.1 = ((bf16[4,128,2048]{2,1,0:T(8,128)(2,1)}), bf16[4,128,2048]{2,1,0:T(8,128)(2,1)}, u32[]{:S(2)}, u32[]{:S(2)}) async-start(bf16[4,128,2048]{2,1,0:T(8,128)(2,1)} %down.1), calls=%async_computation.1 | async-start | bytes 4194304 | tf_op jit(solution)/shard_map/all_to_all | solution.py:843
  272.8 15.4 %collective-permute-start.34 = (bf16[128,512]{1,0:T(8,128)(2,1)S(1)}, bf16[128,512]{1,0:T(8,128)(2,1)S(1)}, u32[]{:S(2)}, u32[]{:S(2)}) collective-permute-start(bf16[128,512]{1,0:T(8,128)(2,1)S(1)} %get-tuple-element.145), channel_id=1, source_target_pairs={{0,4},{4,8},{8,12},{12,0},{1,5},{5,9},{9,13},{13,1},{2,6},{6,10},{... | collective-permute-start | bytes 393224 | tf_op jit(solution)/shard_map/ppermute | solution.py:24
  272.9 15.3 %collective-permute-start.35 = (bf16[128,512]{1,0:T(8,128)(2,1)S(1)}, bf16[128,512]{1,0:T(8,128)(2,1)S(1)}, u32[]{:S(2)}, u32[]{:S(2)}) collective-permute-start(bf16[128,512]{1,0:T(8,128)(2,1)S(1)} %get-tuple-element.146), channel_id=1, source_target_pairs={{0,8},{4,12},{8,0},{12,4},{1,9},{5,13},{9,1},{13,5},{2,10},{6,14},... | collective-permute-start | bytes 393224 | tf_op jit(solution)/shard_map/ppermute | solution.py:24
  316.2 13.9 %collective-permute-start.44 = (bf16[4,4,304,256]{3,2,1,0:T(8,128)(2,1)}, bf16[4,4,304,256]{3,2,1,0:T(8,128)(2,1)}, u32[]{:S(2)}, u32[]{:S(2)}) collective-permute-start(bf16[4,4,304,256]{3,2,1,0:T(8,128)(2,1)} %get-tuple-element.165), channel_id=1, source_target_pairs={{0,16},{16,0},{1,17},{17,1},{2,18},{18,2},{3,19},{19,3},{4,20},{20... | collective-permute-start | bytes 7471112 | tf_op jit(solution)/shard_map/ppermute | solution.py:28
  316.2 65.4 %all-to-all-start.2 = ((bf16[4,4,352,256]{3,2,1,0:T(8,128)(2,1)}), bf16[4,4,352,256]{3,2,1,0:T(8,128)(2,1)}, u32[]{:S(2)}, u32[]{:S(2)}) async-start(bf16[4,4,352,256]{3,2,1,0:T(8,128)(2,1)} %feed_grads_own.3), calls=%async_computation.2 | async-start | bytes 5767168 | tf_op jit(solution)/shard_map/all_to_all | solution.py:866
  333.6 17.2 %collective-permute-start.45 = (bf16[4,304,256]{2,1,0:T(8,128)(2,1)S(1)}, bf16[4,304,256]{2,1,0:T(8,128)(2,1)}, u32[]{:S(2)}, u32[]{:S(2)}) collective-permute-start(bf16[4,304,256]{2,1,0:T(8,128)(2,1)S(1)} %get-tuple-element.167), channel_id=1, source_target_pairs={{0,4},{4,8},{8,12},{12,0},{1,5},{5,9},{9,13},{13,1},{2,6},{6,10},{... | collective-permute-start | bytes 1867784 | tf_op jit(solution)/shard_map/ppermute | solution.py:24
  337.6 27.5 %collective-permute-start.46 = (bf16[4,304,256]{2,1,0:T(8,128)(2,1)S(1)}, bf16[4,304,256]{2,1,0:T(8,128)(2,1)}, u32[]{:S(2)}, u32[]{:S(2)}) collective-permute-start(bf16[4,304,256]{2,1,0:T(8,128)(2,1)S(1)} %get-tuple-element.168), channel_id=1, source_target_pairs={{0,8},{4,12},{8,0},{12,4},{1,9},{5,13},{9,1},{13,5},{2,10},{6,14},... | collective-permute-start | bytes 1867784 | tf_op jit(solution)/shard_map/ppermute | solution.py:24
  339.1 29.4 %collective-permute-start.47 = (bf16[4,304,256]{2,1,0:T(8,128)(2,1)}, bf16[4,304,256]{2,1,0:T(8,128)(2,1)}, u32[]{:S(2)}, u32[]{:S(2)}) collective-permute-start(bf16[4,304,256]{2,1,0:T(8,128)(2,1)} %get-tuple-element.169), channel_id=1, source_target_pairs={{0,12},{4,0},{8,4},{12,8},{1,13},{5,1},{9,5},{13,9},{2,14},{6,2},{... | collective-permute-start | bytes 1867784 | tf_op jit(solution)/shard_map/ppermute | solution.py:24
  341.4 29.0 %collective-permute-start.48 = (bf16[704,256]{1,0:T(8,128)(2,1)}, bf16[704,256]{1,0:T(8,128)(2,1)S(1)}, u32[]{:S(2)}, u32[]{:S(2)}) collective-permute-start(bf16[704,256]{1,0:T(8,128)(2,1)} %bitcast.68), channel_id=1, source_target_pairs={{0,96},{32,0},{64,32},{96,64},{1,97},{33,1},{65,33},{97,65},{2,98}... | collective-permute-start | bytes 1081352 | tf_op jit(solution)/shard_map/ppermute | solution.py:24
  344.4 26.0 %collective-permute-start.49 = (bf16[704,256]{1,0:T(8,128)(2,1)}, bf16[704,256]{1,0:T(8,128)(2,1)S(1)}, u32[]{:S(2)}, u32[]{:S(2)}) collective-permute-start(bf16[704,256]{1,0:T(8,128)(2,1)} %bitcast.69), channel_id=1, source_target_pairs={{0,64},{32,96},{64,0},{96,32},{1,65},{33,97},{65,1},{97,33},{2,66}... | collective-permute-start | bytes 1081352 | tf_op jit(solution)/shard_map/ppermute | solution.py:24
  350.8 25.4 %collective-permute-start.50 = (bf16[704,256]{1,0:T(8,128)(2,1)}, bf16[704,256]{1,0:T(8,128)(2,1)S(1)}, u32[]{:S(2)}, u32[]{:S(2)}) collective-permute-start(bf16[704,256]{1,0:T(8,128)(2,1)} %bitcast.70), channel_id=1, source_target_pairs={{0,32},{32,64},{64,96},{96,0},{1,33},{33,65},{65,97},{97,1},{2,34}... | collective-permute-start | bytes 1081352 | tf_op jit(solution)/shard_map/ppermute | solution.py:24
  377.5 29.0 %collective-permute-start.60 = (bf16[4,704,256]{2,1,0:T(8,128)(2,1)}, bf16[4,704,256]{2,1,0:T(8,128)(2,1)}, u32[]{:S(2)}, u32[]{:S(2)}) collective-permute-start(bf16[4,704,256]{2,1,0:T(8,128)(2,1)} %pad_maximum_fusion), channel_id=1, source_target_pairs={{0,16},{16,0},{1,17},{17,1},{2,18},{18,2},{3,19},{19,3},{4,20},{20... | collective-permute-start | bytes 4325384 | tf_op jit(solution)/shard_map/ppermute | solution.py:28
  389.6 14.8 %collective-permute-start.41 = (bf16[128,2048]{1,0:T(8,128)(2,1)S(1)}, bf16[128,2048]{1,0:T(8,128)(2,1)S(1)}, u32[]{:S(2)}, u32[]{:S(2)}) collective-permute-start(bf16[128,2048]{1,0:T(8,128)(2,1)S(1)} %copy-done.44), channel_id=1, source_target_pairs={{0,1},{1,2},{2,3},{3,0},{4,5},{5,6},{6,7},{7,4},{8,9},{9,10},{10,1... | collective-permute-start | bytes 1572872 | tf_op jit(solution)/shard_map/ppermute | solution.py:24
  404.5 17.1 %collective-permute-start.59 = (bf16[656,256]{1,0:T(8,128)(2,1)S(1)}, bf16[656,256]{1,0:T(8,128)(2,1)S(1)}, u32[]{:S(2)}, u32[]{:S(2)}) collective-permute-start(bf16[656,256]{1,0:T(8,128)(2,1)S(1)} %pad_maximum_fusion.10.refs_1_), channel_id=1, source_target_pairs={{0,32},{32,64},{64,96},{96,0},{1,33},{33,65},{65,97},{97,1},{2,34}... | collective-permute-start | bytes 1007624 | tf_op jit(solution)/shard_map/ppermute | solution.py:24
  (90 other events, 903.8 us)
Sparse Core Ops, SparseCore 0:
  52.4 93.8 all-gather.2
  250.3 85.8 reduce-scatter.3
